TPU v7x, 32 devices: a whole 2x2x4 slice. The times are simulated.
32 devices in a mesh: row: 8 (over y, x, core), col: 4 (over z).
Axes of the slice: x: 2, y: 2, z: 4, core: 2. Of those that a mesh axis runs over, the one named last changes fastest.
Arguments:
- matrix: float32 [24576, 2048], P('row', 'col'), may hold values from -6 to 6
Outputs:
- top_rows: float32 [2048, 256], P(('col', 'row'))
- remainder: float32 [24576, 2048], P('row', 'col')
All inputs are finite; a program needn't handle non-finite values.
Results may differ from a plain program's by a relative error of at most 0.00013.
Values sent between devices are 32-bit elements; how exact they have to be, the bound alone decides.
No kernel may reach another device: no remote copies, remote signals or barrier semaphores. Data moves between devices by JAX's collectives and lax.ppermute only.
A program may use at most 64 MiB of HBM per device.

v0:
```python
import jax
import jax.numpy as jnp
from jax import lax
from jax.sharding import PartitionSpec as P

PANEL = 256


def broadcast(block, axis, owner):
    block = jnp.where(lax.axis_index(axis) == owner, block, jnp.zeros_like(block))
    return lax.psum(block, axis)


def gram_total(panel_cols):
    local_gram = lax.dot_general(
        panel_cols,
        panel_cols,
        (((0,), (0,)), ((), ())),
        precision=lax.Precision.HIGHEST,
        preferred_element_type=jnp.float32,
    )
    return lax.psum(local_gram, "row")


def shards(matrix):
    highest = lax.Precision.HIGHEST
    own_panel = matrix[:, :PANEL]
    panel_cols = broadcast(own_panel, "col", 0)
    lower_factor = jnp.linalg.cholesky(gram_total(panel_cols))
    column_block = matrix
    products = lax.psum_scatter(
        lax.dot_general(
            column_block,
            panel_cols,
            (((0,), (0,)), ((), ())),
            precision=highest,
            preferred_element_type=jnp.float32,
        ),
        "row",
        scatter_dimension=0,
        tiled=True,
    )
    top_rows = lax.linalg.triangular_solve(
        lower_factor, products, left_side=False, lower=True, transpose_a=True
    )
    coeffs = lax.linalg.triangular_solve(lower_factor, top_rows, left_side=False, lower=True)
    column_block = matrix
    remainder = column_block - lax.dot_general(
        panel_cols,
        lax.all_gather(coeffs, "row", axis=0, tiled=True),
        (((1,), (1,)), ((), ())),
        precision=highest,
        preferred_element_type=jnp.float32,
    )
    return (top_rows, remainder)


def solution(mesh):
    return jax.shard_map(
        shards,
        mesh=mesh,
        in_specs=(P("row", "col"),),
        out_specs=(P(("col", "row"), None), P("row", "col")),
        check_vma=False,
    )
```

profile of v0, /device:TPU:17, one launch (start us, length us, event | category | flops | bytes accessed | tf_op | source)
XLA Modules:
  0.0 293.3 jit_solution(14773742906455125220)
XLA Ops:
  7.2 3.8 %slice_select_fusion = f32[3072,256]{1,0:T(8,128)} fusion(f32[3072,512]{1,0:T(8,128)} %param.1, pred[]{:T(512)S(6)} %eq.3), kind=kLoop, calls=%fused_computation.3 | loop fusion | flops 786432 | bytes 6291457 | tf_op jit(solution)/shard_map/jit(_where)/select_n | solution.py:10
  11.1 121.3 %all-reduce.4.cloned.1.call-done = f32[3072,256]{1,0:T(8,128)} async-done(((f32[3072,256]{1,0:T(8,128)}), f32[3072,256]{1,0:T(8,128)}) %all-reduce.4.cloned.1.call-update) | async-done | bytes 3145744 | tf_op jit(solution)/shard_map/psum | solution.py:11
  132.3 8.8 %fusion.12 = f32[256,256]{0,1:T(8,128)} fusion(f32[3072,256]{1,0:T(8,128)} %all-reduce.4.cloned.1.call-done), kind=kOutput, calls=%fused_computation.37 | convolution fusion | flops 2415919104 | bytes 3407872 | tf_op jit(solution)/shard_map/dot_general | solution.py:15
  141.2 8.3 %convolution_bitcast_fusion = f32[512,256]{0,1:T(8,128)} fusion(f32[3072,256]{1,0:T(8,128)S(1)} %copy-done, f32[3072,512]{1,0:T(8,128)} %param.1), kind=kOutput, calls=%fused_computation.4 | convolution fusion | flops 4831838208 | bytes 9961472 | tf_op jit(solution)/shard_map/dot_general | solution.py:32
  149.5 2.0 copy.8
  151.5 42.4 %all-reduce.6.cloned.1.call-done = f32[256,256]{0,1:T(8,128)} async-done(((f32[256,256]{0,1:T(8,128)}), f32[256,256]{0,1:T(8,128)}) %all-reduce.6.cloned.1.call-update) | async-done | bytes 262160 | tf_op jit(solution)/shard_map/psum | solution.py:22
  194.0 1.1 copy.6
  195.1 1.0 fusion
  196.8 11.7 %cholesky.50 = f32[128,128]{1,0:T(8,128)S(1)} custom-call(f32[128,128]{1,0:T(8,128)S(1)} %cholesky.118), custom_call_target="Cholesky" | custom-call | tf_op jit(solution)/shard_map/jit(cholesky)/cholesky | solution.py:29
  208.5 9.8 %custom-call.16 = f32[1,128,128]{1,2,0:T(8,128)S(1)} custom-call(f32[1,128,128]{2,1,0:T(8,128)S(1)} %get-tuple-element.23), custom_call_target="InvertDiagBlocksLowerTriangular" | custom-call | tf_op jit(solution)/shard_map/jit(cholesky)/cholesky | solution.py:29
  218.4 1.0 constant_dynamic-update-slice_fusion.1
  219.4 1.1 convolution_subtract_fusion.2
  220.5 11.7 %cholesky.105 = f32[128,128]{1,0:T(8,128)S(1)} custom-call(f32[128,128]{1,0:T(8,128)S(1)} %convolution_subtract_fusion.2), custom_call_target="Cholesky" | custom-call | tf_op jit(solution)/shard_map/jit(cholesky)/cholesky | solution.py:29
  234.2 1.0 select_select_fusion
  235.3 5.0 %while.1 = (s32[]{:T(128)}, f32[256,256]{1,0:T(8,128)S(1)}, s32[2,2]{1,0:T(2,128)S(1)}, f32[2,128,128]{2,1,0:T(8,128)}, s32[]{:T(128)}) while((s32[]{:T(128)}, f32[256,256]{1,0:T(8,128)S(1)}, s32[2,2]{1,0:T(2,128)S(1)}, f32[2,128,128]{2,1,0:T(8,128)}, s32[]{:T(128)}) %tuple.27), condition=%wide.while_cond, body=%wide.while_body.sunk | while | flops 2 | bytes 132205 | solution.py:43
  235.9 1.9 bitcast_dynamic-update-slice_fusion.2
  238.4 1.9 bitcast_dynamic-update-slice_fusion.2
  240.3 20.5 %custom-call.17 = f32[2,128,128]{1,2,0:T(8,128)S(1)} custom-call(f32[2,128,128]{2,1,0:T(8,128)} %get-tuple-element.9), custom_call_target="InvertDiagBlocksLowerTriangular" | custom-call | tf_op jit(solution)/shard_map/triangular_solve | solution.py:43
  260.8 1.4 triangular_solve.89
  262.2 1.5 copy.11
  263.7 0.9 fusion.5
  264.6 1.0 convolution_subtract_fusion.1
  267.3 10.5 %all_gather.3 = f32[512,256]{1,0:T(8,128)S(1)} all-gather(f32[64,256]{1,0:T(8,128)S(1)} %pad_maximum_fusion.1), channel_id=1, replica_groups=mesh['row'=8,'col'=4] {'row'}, dimensions={0}, use_global_device_ids=true | all-gather | bytes 589824 | tf_op jit(solution)/shard_map/all_gather | solution.py:50
  277.8 8.9 %convolution_subtract_fusion = f32[3072,512]{1,0:T(8,128)} fusion(f32[3072,512]{1,0:T(8,128)} %param.1, f32[3072,256]{1,0:T(8,128)S(1)} %copy-done, f32[512,256]{1,0:T(8,128)S(1)} %all_gather.3), kind=kOutput, calls=%fused_computation.2 | convolution fusion | flops 4833411072 | bytes 16252928 | tf_op jit(solution)/shard_map/dot_general | solution.py:48
  (31 shorter events, 4.5 us)
Async XLA Ops:
  7.2 125.2 %all-reduce.4.cloned.1.call-start = ((), (), s32[]{:S(2)}) async-start(), calls=%async_computation.1 | async-start | bytes 6291456 | tf_op jit(solution)/shard_map/psum | solution.py:11
  11.0 183.0 %all-reduce.6.cloned.1.call-start = ((), (), s32[]{:S(2)}) async-start(), calls=%async_computation.2 | async-start | bytes 524288 | tf_op jit(solution)/shard_map/psum | solution.py:22
  132.3 8.9 %copy-start = (f32[3072,256]{1,0:T(8,128)S(1)}, f32[3072,256]{1,0:T(8,128)}, u32[]{:S(2)}) copy-start(f32[3072,256]{1,0:T(8,128)} %all-reduce.4.cloned.1.call-done) | copy-start | bytes 9437188
  141.1 119.7 %reduce-scatter.4.cloned.1.call-start = ((), (), s32[]{:S(2)}) async-start(), calls=%async_computation.3 | async-start | bytes 589824
  196.1 0.7 copy-start.2
  232.3 1.9 copy-start.1
Sparse Core Ops, SparseCore 0:
  11.1 121.1 all-reduce.3
  141.3 52.6 all-reduce.5
  197.4 34.1 reduce-scatter.3
where the time goes:
time: 295 us; the launch traced here: 293 us
  waiting for transfers between devices  164 us (56%)
  other arithmetic  60.9 us (21%)
  matrix products  31.1 us (11%)
  between operations  15.1 us (5%)
  local copies, waits for them, and re-layouts  11.8 us (4%)
  blocking collectives  10.5 us (4%)
    psum x1, waiting for transfers between devices, broadcast(): return lax.psum(block, axis)  121 us
    psum x1, waiting for transfers between devices, gram_total(): return lax.psum(local_gram, 'row')  42.4 us
    another operation x6, other arithmetic, shards(): lower_factor = jnp.linalg.cholesky(gram_total(panel_cols))  34 us
    another operation x4, other arithmetic, shards(): lax.linalg.triangular_solve(lower_factor, products, left_side=False, lowe...  22.1 us
    all_gather x1, blocking collectives, shards(): lax.all_gather(coeffs, 'row', axis=0, tiled=True)  10.5 us
    dot_general x1, matrix products, shards(): lax.dot_general(panel_cols, lax.all_gather(coeffs, 'row', axis=0, tiled=T...  8.95 us
    dot_general x1, matrix products, gram_total(): lax.dot_general(panel_cols, panel_cols, (((0,), (0,)), ((), ())), precisi...  8.78 us
    dot_general x1, matrix products, shards(): lax.dot_general(column_block, panel_cols, (((0,), (0,)), ((), ())), preci...  8.29 us
  transfers between devices with their start and end apart: 3, of which 2 were waited for; matrix products, arithmetic and copies ran while one was open for 26% of the time, Pallas kernels for 0%

commit v1 on v0

v1 whole, which is shorter than its diff:
```python
import jax
import jax.numpy as jnp
from jax import lax
from jax.experimental import pallas as pl
from jax.experimental.pallas import tpu as pltpu
from jax.sharding import PartitionSpec as P

PANEL = 256
CHUNKS = 8
AHEAD = 2
BLOCK = 32
VMEM = 48 * 1024 * 1024
HIGHEST = lax.Precision.HIGHEST
F32, BF16 = jnp.float32, jnp.bfloat16
ANY = pl.BlockSpec(memory_space=pl.ANY)
SMEM = pl.BlockSpec(memory_space=pltpu.SMEM)


def whole(shape):
    return pl.BlockSpec(shape, lambda *i: (0,) * len(shape))


def params():
    return pltpu.CompilerParams(vmem_limit_bytes=VMEM)


def cost(flops, nbytes):
    return pl.CostEstimate(flops=flops, bytes_accessed=nbytes, transcendentals=0)


def split(x):
    hi = x.astype(BF16)
    return hi, (x - hi.astype(F32)).astype(BF16)


def dot(a, b, dims, precision=None):
    return lax.dot_general(
        a, b, (dims, ((), ())), precision=precision, preferred_element_type=F32
    )


def pack(matrix, chunk, rows, after):
    steps = 2

    def body(*refs):
        refs[-1][...] = refs[0][...]

    return pl.pallas_call(
        body,
        grid=(steps,),
        in_specs=[pl.BlockSpec((rows // steps, PANEL), lambda i: (chunk * steps + i, 0))]
        + [ANY] * len(after),
        out_specs=pl.BlockSpec((rows // steps, PANEL), lambda i: (i, 0)),
        out_shape=jax.ShapeDtypeStruct((rows, PANEL), F32),
        cost_estimate=cost(0, 8 * rows * PANEL),
        name=f"pack{chunk}",
    )(matrix, *after)


def gram_part(col, matrix):
    rows = matrix.shape[0]
    tile = rows // 4

    def body(col_ref, panel, out):
        @pl.when(col_ref[0] == 0)
        def _():
            @pl.when(pl.program_id(0) == 0)
            def _():
                out[...] = jnp.zeros_like(out)

            x = panel[...]
            out[...] += dot(x, x, ((0,), (0,)), HIGHEST)

    return pl.pallas_call(
        body,
        grid=(4,),
        in_specs=[SMEM, pl.BlockSpec((tile, PANEL), lambda i: (i, 0))],
        out_specs=whole((PANEL, PANEL)),
        out_shape=jax.ShapeDtypeStruct((PANEL, PANEL), F32),
        compiler_params=params(),
        cost_estimate=cost(12 * rows * PANEL * PANEL, 4 * rows * PANEL),
        name="gram",
    )(col, matrix)


def eliminate(col, state, block, after):
    first, last = block * BLOCK, (block + 1) * BLOCK
    width = 2 * PANEL

    def body(col_ref, src, *rest):
        out = rest[-1]

        @pl.when(col_ref[0] == 0)
        def _():
            if block == 0:
                row = lax.broadcasted_iota(jnp.int32, (PANEL, PANEL), 0)
                lane = lax.broadcasted_iota(jnp.int32, (PANEL, PANEL), 1)
                out[:, :PANEL] = src[...]
                out[:, PANEL:] = (row == lane).astype(F32)
            else:
                out[...] = src[...]
            row = lax.broadcasted_iota(jnp.int32, (BLOCK, BLOCK), 0)
            lane = lax.broadcasted_iota(jnp.int32, (BLOCK, BLOCK), 1)
            work = jnp.concatenate(
                [out[first:last, first:last], (row == lane).astype(F32)], axis=1
            )
            below = lax.broadcasted_iota(jnp.int32, (BLOCK, 2 * BLOCK), 0)
            scale = jnp.zeros((BLOCK, 2 * BLOCK), F32)
            for i in range(BLOCK):
                column = jnp.broadcast_to(work[:, i : i + 1], work.shape)
                pivot = column[i : i + 1, :]
                scale = jnp.where(below == i, pivot, scale)
                factor = jnp.where(below > i, column / pivot, 0.0)
                work = work - factor * work[i : i + 1, :]
            root = lax.rsqrt(scale)
            root = root * (1.5 - 0.5 * scale * root * root)
            inverse = (work * root)[:, BLOCK:]
            rows = dot(inverse, out[first:last, :], ((1,), (0,)), HIGHEST)
            out[first:last, :] = rows
            if last < PANEL:
                out[last:, :] -= dot(rows[:, last:PANEL], rows, ((0,), (0,)), HIGHEST)

    return pl.pallas_call(
        body,
        in_specs=[SMEM, whole(state.shape)] + [ANY] * len(after),
        out_specs=whole((PANEL, width)),
        out_shape=jax.ShapeDtypeStruct((PANEL, width), F32),
        grid=(1,),
        input_output_aliases={1: 0} if block else {},
        compiler_params=params(),
        cost_estimate=cost(12 * BLOCK * PANEL * width, 8 * PANEL * width),
        name=f"eliminate{block}",
    )(col, state, *after)


def consume(col, matrix, hops, chunk, before):
    rows, width = hops[0].shape[0], matrix.shape[1]
    last = chunk == CHUNKS - 1

    def body(col_ref, block, *refs):
        sources, rest = refs[: len(hops)], refs[len(hops) :]
        if chunk:
            total, _, out, halves, held, sem = rest
        else:
            out, halves, held, sem = rest
        for h, source in enumerate(sources):

            @pl.when(col_ref[0] == h)
            def _():
                copy = pltpu.make_async_copy(source, held, sem)
                copy.start()
                copy.wait()

        high, low = split(held[...])
        halves[:, :PANEL] = high
        halves[:, PANEL:] = low
        a_high, a_low = split(block[...])
        dims = ((0,), (0,))
        value = dot(high, a_high, dims) + dot(low, a_high, dims) + dot(high, a_low, dims)
        if chunk:
            value += total[...]
        out[...] = value.T if last else value

    total_shape = (width, PANEL) if last else (PANEL, width)
    out_shape = (
        jax.ShapeDtypeStruct(total_shape, F32),
        jax.ShapeDtypeStruct((matrix.shape[0], 2 * PANEL), BF16),
    )
    n = 2 + len(hops)
    return pl.pallas_call(
        body,
        grid=(1,),
        in_specs=[SMEM, pl.BlockSpec((rows, width), lambda i: (chunk, 0))]
        + [ANY] * len(hops)
        + ([whole((PANEL, width)), ANY] if chunk else []),
        out_specs=(
            whole(total_shape),
            pl.BlockSpec((rows, 2 * PANEL), lambda i: (chunk, 0)),
        ),
        out_shape=out_shape,
        input_output_aliases={n + 1: 1} if chunk else {},
        scratch_shapes=[pltpu.VMEM((rows, PANEL), F32), pltpu.SemaphoreType.DMA(())],
        compiler_params=params(),
        cost_estimate=cost(
            6 * rows * PANEL * width, 4 * rows * (2 * PANEL + width) + 8 * PANEL * width
        ),
        name=f"consume{chunk}",
    )(col, matrix, *hops, *before)


def solve(col, parts, hops):
    n, rows, _ = parts.shape

    def body(col_ref, parts_ref, *refs):
        sources, (top, coeffs, held, sem) = refs[: len(hops)], refs[len(hops) :]
        for h, source in enumerate(sources):

            @pl.when(col_ref[0] == h)
            def _():
                copy = pltpu.make_async_copy(source, held, sem)
                copy.start()
                copy.wait()

        total = parts_ref[0]
        for p in range(1, n):
            total += parts_ref[p]
        inverse = held[...]
        value = dot(total, inverse, ((1,), (1,)), HIGHEST)
        top[...] = value
        coeffs[...] = dot(value, inverse, ((1,), (0,)), HIGHEST)

    return pl.pallas_call(
        body,
        grid=(1,),
        in_specs=[SMEM, whole(parts.shape)] + [ANY] * len(hops),
        out_specs=(whole((rows, PANEL)),) * 2,
        out_shape=(jax.ShapeDtypeStruct((rows, PANEL), F32),) * 2,
        scratch_shapes=[pltpu.VMEM((PANEL, PANEL), F32), pltpu.SemaphoreType.DMA(())],
        compiler_params=params(),
        cost_estimate=cost(24 * rows * PANEL * PANEL, 4 * PANEL * PANEL),
        name="solve",
    )(col, parts, *hops)


def subtract(matrix, halves, coeffs):
    rows, width = matrix.shape
    tile = rows // 12

    def body(a, p, c, out, c_high, c_low):
        @pl.when(pl.program_id(0) == 0)
        def _():
            c_high[...], c_low[...] = split(c[...])

        high, low = p[:, :PANEL], p[:, PANEL:]
        dims = ((1,), (1,))
        out[...] = a[...] - (
            dot(high, c_high[...], dims) + dot(low, c_high[...], dims) + dot(high, c_low[...], dims)
        )

    return pl.pallas_call(
        body,
        grid=(12,),
        in_specs=[
            pl.BlockSpec((tile, width), lambda i: (i, 0)),
            pl.BlockSpec((tile, 2 * PANEL), lambda i: (i, 0)),
            whole((width, PANEL)),
        ],
        out_specs=pl.BlockSpec((tile, width), lambda i: (i, 0)),
        out_shape=jax.ShapeDtypeStruct((rows, width), F32),
        scratch_shapes=[pltpu.VMEM((width, PANEL), BF16)] * 2,
        compiler_params=params(),
        cost_estimate=cost(6 * rows * PANEL * width, 8 * rows * (width + PANEL)),
        name="subtract",
    )(matrix, halves, coeffs)


def program(n_row, n_col):
    def down(x):
        hops = [x]
        for h in range(1, n_col):
            hops.append(lax.ppermute(hops[-1], "col", [(h - 1, h)]))
        return hops

    def shards(matrix):
        rows, width = matrix.shape
        col = lax.axis_index("col").astype(jnp.int32).reshape(1)
        size = rows // CHUNKS
        blocks = PANEL // BLOCK
        chain = []
        state = None
        done = 0
        gram = None
        for k in range(CHUNKS):
            after = [chain[k - AHEAD][1 % n_col]] if k >= AHEAD else []
            if k >= AHEAD + 1 and done < blocks:
                for _ in range(2 if k >= CHUNKS - 2 else 1):
                    state = eliminate(col, gram if state is None else state, done, after[:1])
                    done += 1
                after.append(state)
            chain.append(down(pack(matrix, k, size, after)))
            if k == AHEAD - 1:
                parts = gram_part(col, matrix).reshape(n_row, PANEL // n_row, PANEL)
                mine = lax.all_to_all(parts, "row", 0, 0).sum(0)
                gram = lax.all_gather(mine, "row", axis=0, tiled=True)
        while done < blocks:
            state = eliminate(col, state, done, [chain[-1][1 % n_col]] if done == blocks - 1 else [])
            done += 1
        inverse = down(state[:, PANEL:])
        before = ()
        for k in range(CHUNKS):
            before = consume(col, matrix, chain[k], k, before)
        products, halves = before
        parts = lax.all_to_all(products.reshape(n_row, width // n_row, PANEL), "row", 0, 0)
        top_rows, coeffs = solve(col, parts, inverse)
        coeffs = lax.all_gather(coeffs, "row", axis=0, tiled=True)
        return top_rows, subtract(matrix, halves, coeffs)

    return shards


def solution(mesh):
    return jax.shard_map(
        program(mesh.shape["row"], mesh.shape["col"]),
        mesh=mesh,
        in_specs=(P("row", "col"),),
        out_specs=(P(("col", "row"), None), P("row", "col")),
        check_vma=False,
    )
```

time: 295 us -> 189 us (0.64)
  the two profiles are of different devices: /device:TPU:17 before, /device:TPU:9 now
where the time goes in v1:
time: 189 us; the launch traced here: 187 us
  waiting for transfers between devices  49.7 us (26%)
  Pallas kernels  47.4 us (25%)
  starting transfers between devices  40.8 us (22%)
  blocking collectives  31.1 us (16%)
  local copies, waits for them, and re-layouts  16.7 us (9%)
    ppermute x27, waiting for transfers between devices, down(): hops.append(lax.ppermute(hops[-1], 'col', [(h - 1, h)]))  44.2 us
    ppermute x27, starting transfers between devices, down(): hops.append(lax.ppermute(hops[-1], 'col', [(h - 1, h)]))  35.3 us
    unnamed x96, local copies, waits for them, and re-layouts  16.7 us
    pallas_call x8, Pallas kernels, consume(): pl.pallas_call(body, grid=(1,), in_specs=[SMEM, pl.BlockSpec((rows, width...  16.5 us
    pallas_call x8, Pallas kernels, pack(): pl.pallas_call(body, grid=(steps,), in_specs=[pl.BlockSpec((rows // steps...  13.9 us
    all_gather x1, blocking collectives, shards(): coeffs = lax.all_gather(coeffs, 'row', axis=0, tiled=True)  11.8 us
    pallas_call x1, Pallas kernels, subtract(): pl.pallas_call(body, grid=(12,), in_specs=[pl.BlockSpec((tile, width), la...  11.3 us
    all_to_all x1, blocking collectives, shards(): mine = lax.all_to_all(parts, 'row', 0, 0).sum(0)  9.79 us
  transfers between devices with their start and end apart: 28, of which 7 were waited for; matrix products, arithmetic and copies ran while one was open for 0% of the time, Pallas kernels for 17%

profile of v1, /device:TPU:9, one launch (start us, length us, event | category | flops | bytes accessed | tf_op | source)
XLA Modules:
  0.0 187.2 jit_solution(11878699820275963011)
XLA Ops:
  6.7 2.6 %gram.1 = f32[256,256]{1,0:T(8,128)S(1)} custom-call(s32[1]{0:T(128)} %bitcast.col_ref, f32[3072,512]{1,0:T(8,128)} %a.1), custom_call_target="tpu_custom_call" | custom-call | flops 2415919104 | bytes 3145728 | tf_op jit(solution)/shard_map/gram/pallas_call | solution.py:74
  9.3 9.8 %all_to_all.10 = f32[8,32,256]{2,1,0:T(8,128)S(1)} all-to-all(f32[8,32,256]{2,1,0:T(8,128)S(1)} %bitcast.4), channel_id=1, replica_groups=mesh['row'=8,'col'=4] {'row'}, dimensions={0} | all-to-all | bytes 524288 | tf_op jit(solution)/shard_map/all_to_all | solution.py:283
  22.8 9.5 %all_gather.6.src = f32[256,256]{1,0:T(8,128)S(1)} all-gather(f32[32,256]{1,0:T(8,128)S(1)} %reduce_sum.9), channel_id=1, replica_groups=mesh['row'=8,'col'=4] {'row'}, dimensions={0}, use_global_device_ids=true | all-gather | bytes 294912 | tf_op jit(solution)/shard_map/all_gather | solution.py:284
  45.2 10.4 %collective-permute-done.1.rest_0_.refs_1_ = f32[384,256]{1,0:T(8,128)S(1)} collective-permute-done((f32[384,256]{1,0:T(8,128)}, f32[384,256]{1,0:T(8,128)S(1)}, u32[]{:S(2)}, u32[]{:S(2)}) %collective-permute-start.1) | collective-permute-done | bytes 393248 | tf_op jit(solution)/shard_map/ppermute | solution.py:261
  58.2 1.8 pack5.1.refs_0_
  71.7 5.0 %collective-permute-done.4.rest_0_.refs_1_ = f32[384,256]{1,0:T(8,128)S(1)} collective-permute-done((f32[384,256]{1,0:T(8,128)}, f32[384,256]{1,0:T(8,128)S(1)}, u32[]{:S(2)}, u32[]{:S(2)}) %collective-permute-start.4) | collective-permute-done | bytes 393248 | tf_op jit(solution)/shard_map/ppermute | solution.py:261
  79.9 1.8 pack7.1.refs_0_
  86.3 9.1 %collective-permute-done.9.refs_1_ = f32[384,256]{1,0:T(8,128)S(1)} collective-permute-done((f32[384,256]{1,0:T(8,128)}, f32[384,256]{1,0:T(8,128)S(1)}, u32[]{:S(2)}, u32[]{:S(2)}) %collective-permute-start.9) | collective-permute-done | bytes 393248 | tf_op jit(solution)/shard_map/ppermute | solution.py:261
  96.8 13.1 %collective-permute-done.6.refs_1_.rest_0_ = f32[384,256]{1,0:T(8,128)S(1)} collective-permute-done((f32[384,256]{1,0:T(8,128)}, f32[384,256]{1,0:T(8,128)S(1)}, u32[]{:S(2)}, u32[]{:S(2)}) %collective-permute-start.6) | collective-permute-done | bytes 393248 | tf_op jit(solution)/shard_map/ppermute | solution.py:261
  114.0 5.2 %collective-permute-done.7.refs_2_ = f32[384,256]{1,0:T(8,128)S(1)} collective-permute-done((f32[384,256]{1,0:T(8,128)S(1)}, f32[384,256]{1,0:T(8,128)S(1)}, u32[]{:S(2)}, u32[]{:S(2)}) %collective-permute-start.7) | collective-permute-done | bytes 393248 | tf_op jit(solution)/shard_map/ppermute | solution.py:261
  124.4 2.0 %consume0.1 = (f32[256,512]{1,0:T(8,128)S(1)}, bf16[3072,512]{1,0:T(8,128)(2,1)S(1)}) custom-call(s32[1]{0:T(128)} %bitcast.col_ref, f32[3072,512]{1,0:T(8,128)} %a.1, f32[384,256]{1,0:T(8,128)S(1)} %copy-done.23, f32[384,256]{1,0:T(8,128)S(1)} %copy-done.26, f32[384,256]{1,0:T(8,128)S(1)} %copy-done.41, f32[384,256]{1,0:T(8,128)} %collective-permute-done.23.refs_3_), custom_call_target="tpu_custom_call" | custom-call | flops 301989888 | bytes 2621440 | tf_op jit(solution)/shard_map/consume0/pallas_call | solution.py:170
  126.5 2.1 %consume1.1 = (f32[256,512]{1,0:T(8,128)S(1)}, bf16[3072,512]{1,0:T(8,128)(2,1)S(1)}) custom-call(s32[1]{0:T(128)} %bitcast.col_ref, f32[3072,512]{1,0:T(8,128)} %a.1, f32[384,256]{1,0:T(8,128)S(1)} %copy-done.22, f32[384,256]{1,0:T(8,128)S(1)} %copy-done.16, f32[384,256]{1,0:T(8,128)S(1)} %copy-done.39, ...), custom_call_target="tpu_custom_call", output_to_operand_aliasing={{1}: (7, {})} | custom-call | flops 301989888 | bytes 2621440 | tf_op jit(solution)/shard_map/consume1/pallas_call | solution.py:170
  128.6 2.2 %consume2.1 = (f32[256,512]{1,0:T(8,128)S(1)}, bf16[3072,512]{1,0:T(8,128)(2,1)S(1)}) custom-call(s32[1]{0:T(128)} %bitcast.col_ref, f32[3072,512]{1,0:T(8,128)} %a.1, f32[384,256]{1,0:T(8,128)S(1)} %copy-done.27, f32[384,256]{1,0:T(8,128)S(1)} %copy-done.19, f32[384,256]{1,0:T(8,128)S(1)} %copy-done.43, ...), custom_call_target="tpu_custom_call", output_to_operand_aliasing={{1}: (7, {})} | custom-call | flops 301989888 | bytes 2621440 | tf_op jit(solution)/shard_map/consume2/pallas_call | solution.py:170
  130.9 2.0 %consume3.1 = (f32[256,512]{1,0:T(8,128)S(1)}, bf16[3072,512]{1,0:T(8,128)(2,1)S(1)}) custom-call(s32[1]{0:T(128)} %bitcast.col_ref, f32[3072,512]{1,0:T(8,128)} %a.1, f32[384,256]{1,0:T(8,128)S(1)} %copy-done.30, f32[384,256]{1,0:T(8,128)S(1)} %copy-done.21, f32[384,256]{1,0:T(8,128)S(1)} %copy-done.45, ...), custom_call_target="tpu_custom_call", output_to_operand_aliasing={{1}: (7, {})} | custom-call | flops 301989888 | bytes 2621440 | tf_op jit(solution)/shard_map/consume3/pallas_call | solution.py:170
  132.9 5.5 %collective-permute-start.25 = (f32[256,256]{1,0:T(8,128)}, f32[256,256]{1,0:T(8,128)}, u32[]{:S(2)}, u32[]{:S(2)}) collective-permute-start(f32[256,256]{1,0:T(8,128)} %collective-permute-done.24.refs_1_), channel_id=1, source_target_pairs={{1,2},{5,6},{9,10},{13,14},{17,18},{21,22},{25,26},{29,30}} | collective-permute-start | bytes 786440 | tf_op jit(solution)/shard_map/ppermute | solution.py:261
  138.5 2.0 %consume4.1 = (f32[256,512]{1,0:T(8,128)S(1)}, bf16[3072,512]{1,0:T(8,128)(2,1)S(1)}) custom-call(s32[1]{0:T(128)} %bitcast.col_ref, f32[3072,512]{1,0:T(8,128)} %a.1, f32[384,256]{1,0:T(8,128)S(1)} %copy-done.29, f32[384,256]{1,0:T(8,128)S(1)} %copy-done.14, f32[384,256]{1,0:T(8,128)S(1)} %collective-permute-done.14.refs_2_, ...), custom_call_target="tpu_custom_call", output_to_operand_aliasing={{1}: (7, {})} | custom-call | flops 301989888 | bytes 2621440 | tf_op jit(solution)/shard_map/consume4/pallas_call | solution.py:170
  140.5 2.0 %consume5.1 = (f32[256,512]{1,0:T(8,128)S(1)}, bf16[3072,512]{1,0:T(8,128)(2,1)S(1)}) custom-call(s32[1]{0:T(128)} %bitcast.col_ref, f32[3072,512]{1,0:T(8,128)} %a.1, f32[384,256]{1,0:T(8,128)S(1)} %copy-done.28, f32[384,256]{1,0:T(8,128)S(1)} %copy-done.11, f32[384,256]{1,0:T(8,128)S(1)} %collective-permute-done.12.refs_2_, ...), custom_call_target="tpu_custom_call", output_to_operand_aliasing={{1}: (7, {})} | custom-call | flops 301989888 | bytes 2621440 | tf_op jit(solution)/shard_map/consume5/pallas_call | solution.py:170
  142.6 2.0 %consume6.1 = (f32[256,512]{1,0:T(8,128)S(1)}, bf16[3072,512]{1,0:T(8,128)(2,1)S(1)}) custom-call(s32[1]{0:T(128)} %bitcast.col_ref, f32[3072,512]{1,0:T(8,128)} %a.1, f32[384,256]{1,0:T(8,128)S(1)} %copy-done.32, f32[384,256]{1,0:T(8,128)S(1)} %copy-done.37, f32[384,256]{1,0:T(8,128)S(1)} %collective-permute-done.10.refs_2_, ...), custom_call_target="tpu_custom_call", output_to_operand_aliasing={{1}: (7, {})} | custom-call | flops 301989888 | bytes 2621440 | tf_op jit(solution)/shard_map/consume6/pallas_call | solution.py:170
  144.7 2.1 %consume7.1 = (f32[512,256]{1,0:T(8,128)S(1)}, bf16[3072,512]{1,0:T(8,128)(2,1)S(1)}) custom-call(s32[1]{0:T(128)} %bitcast.col_ref, f32[3072,512]{1,0:T(8,128)} %a.1, f32[384,256]{1,0:T(8,128)S(1)} %copy-done.31, f32[384,256]{1,0:T(8,128)S(1)} %collective-permute-done.6.refs_1_.rest_0_, ...), custom_call_target="tpu_custom_call", output_to_operand_aliasing={{1}: (7, {})} | custom-call | flops 301989888 | bytes 2621440 | tf_op jit(solution)/shard_map/consume7/pallas_call | solution.py:170
  147.6 5.6 %all-to-all-start.1 = ((f32[8,64,256]{2,1,0:T(8,128)}), f32[8,64,256]{2,1,0:T(8,128)}, u32[]{:S(2)}, u32[]{:S(2)}) async-start(f32[8,64,256]{2,1,0:T(8,128)} %bitcast.3), calls=%async_computation.1 | async-start | bytes 1048576 | tf_op jit(solution)/shard_map/all_to_all | solution.py:293
  154.6 5.5 %all-to-all-done.1.parts_ref = f32[8,64,256]{2,1,0:T(8,128)} async-done(((f32[8,64,256]{2,1,0:T(8,128)}), f32[8,64,256]{2,1,0:T(8,128)}, u32[]{:S(2)}, u32[]{:S(2)}) %all-to-all-start.1) | async-done | bytes 524320 | tf_op jit(solution)/shard_map/all_to_all | solution.py:293
  161.0 3.1 %solve.1 = (f32[64,256]{1,0:T(8,128)}, f32[64,256]{1,0:T(8,128)S(1)}) custom-call(s32[1]{0:T(128)} %bitcast.col_ref, f32[8,64,256]{2,1,0:T(8,128)} %all-to-all-done.1.parts_ref, f32[256,256]{1,0:T(8,128)S(1)} %copy-done.34, f32[256,256]{1,0:T(8,128)} %collective-permute-done.24.refs_1_, f32[256,256]{1,0:T(8,128)} %collective-permute-done.25.refs_2_, ...), custom_call_target="tpu_custom_call" | custom-call | flops 100663296 | bytes 262144 | tf_op jit(solution)/shard_map/solve/pallas_call | solution.py:212
  164.1 11.8 %all_gather.7.c = f32[512,256]{1,0:T(8,128)S(1)} all-gather(f32[64,256]{1,0:T(8,128)S(1)} %get-tuple-element.37), channel_id=1, replica_groups=mesh['row'=8,'col'=4] {'row'}, dimensions={0}, use_global_device_ids=true | all-gather | bytes 589824 | tf_op jit(solution)/shard_map/all_gather | solution.py:295
  175.9 11.3 %subtract.1 = f32[3072,512]{1,0:T(8,128)} custom-call(f32[3072,512]{1,0:T(8,128)} %a.1, bf16[3072,512]{1,0:T(8,128)(2,1)S(1)} %get-tuple-element.36.p, f32[512,256]{1,0:T(8,128)S(1)} %all_gather.7.c), custom_call_target="tpu_custom_call" | custom-call | flops 2415919104 | bytes 18874368 | tf_op jit(solution)/shard_map/subtract/pallas_call | solution.py:240
  (160 shorter events, 58.3 us)
Async XLA Ops:
  2.4 16.7 %collective-permute-start.2 = (f32[384,256]{1,0:T(8,128)}, f32[384,256]{1,0:T(8,128)S(1)}, u32[]{:S(2)}, u32[]{:S(2)}) collective-permute-start(f32[384,256]{1,0:T(8,128)} %pack0.1.refs_0_), channel_id=1, source_target_pairs={{0,1},{4,5},{8,9},{12,13},{16,17},{20,21},{24,25},{28,29}} | collective-permute-start | bytes 1179656 | tf_op jit(solution)/shard_map/ppermute | solution.py:261
  5.4 27.0 %collective-permute-start = (f32[384,256]{1,0:T(8,128)}, f32[384,256]{1,0:T(8,128)S(1)}, u32[]{:S(2)}, u32[]{:S(2)}) collective-permute-start(f32[384,256]{1,0:T(8,128)} %pack1.1.refs_0_), channel_id=1, source_target_pairs={{0,1},{4,5},{8,9},{12,13},{16,17},{20,21},{24,25},{28,29}} | collective-permute-start | bytes 1179656 | tf_op jit(solution)/shard_map/ppermute | solution.py:261
  21.6 18.1 %collective-permute-start.3 = (f32[384,256]{1,0:T(8,128)}, f32[384,256]{1,0:T(8,128)S(1)}, u32[]{:S(2)}, u32[]{:S(2)}) collective-permute-start(f32[384,256]{1,0:T(8,128)} %pack2.1.refs_0_), channel_id=1, source_target_pairs={{0,1},{4,5},{8,9},{12,13},{16,17},{20,21},{24,25},{28,29}} | collective-permute-start | bytes 1179656 | tf_op jit(solution)/shard_map/ppermute | solution.py:261
  35.7 20.0 %collective-permute-start.1 = (f32[384,256]{1,0:T(8,128)}, f32[384,256]{1,0:T(8,128)S(1)}, u32[]{:S(2)}, u32[]{:S(2)}) collective-permute-start(f32[384,256]{1,0:T(8,128)} %pack3.1.refs_0_), channel_id=1, source_target_pairs={{0,1},{4,5},{8,9},{12,13},{16,17},{20,21},{24,25},{28,29}} | collective-permute-start | bytes 1179656 | tf_op jit(solution)/shard_map/ppermute | solution.py:261
  37.0 24.3 %collective-permute-start.22 = (f32[384,256]{1,0:T(8,128)S(1)}, f32[384,256]{1,0:T(8,128)S(1)}, u32[]{:S(2)}, u32[]{:S(2)}) collective-permute-start(f32[384,256]{1,0:T(8,128)S(1)} %copy-done.25), channel_id=1, source_target_pairs={{1,2},{5,6},{9,10},{13,14},{17,18},{21,22},{25,26},{29,30}} | collective-permute-start | bytes 1179656 | tf_op jit(solution)/shard_map/ppermute | solution.py:261
  38.3 25.8 %collective-permute-start.20 = (f32[384,256]{1,0:T(8,128)}, f32[384,256]{1,0:T(8,128)S(1)}, u32[]{:S(2)}, u32[]{:S(2)}) collective-permute-start(f32[384,256]{1,0:T(8,128)} %copy-done.15), channel_id=1, source_target_pairs={{1,2},{5,6},{9,10},{13,14},{17,18},{21,22},{25,26},{29,30}} | collective-permute-start | bytes 1179656 | tf_op jit(solution)/shard_map/ppermute | solution.py:261
  43.9 22.9 %collective-permute-start.5 = (f32[384,256]{1,0:T(8,128)}, f32[384,256]{1,0:T(8,128)S(1)}, u32[]{:S(2)}, u32[]{:S(2)}) collective-permute-start(f32[384,256]{1,0:T(8,128)} %pack4.1.refs_0_), channel_id=1, source_target_pairs={{0,1},{4,5},{8,9},{12,13},{16,17},{20,21},{24,25},{28,29}} | collective-permute-start | bytes 1179656 | tf_op jit(solution)/shard_map/ppermute | solution.py:261
  60.0 16.8 %collective-permute-start.4 = (f32[384,256]{1,0:T(8,128)}, f32[384,256]{1,0:T(8,128)S(1)}, u32[]{:S(2)}, u32[]{:S(2)}) collective-permute-start(f32[384,256]{1,0:T(8,128)} %pack5.1.refs_0_), channel_id=1, source_target_pairs={{0,1},{4,5},{8,9},{12,13},{16,17},{20,21},{24,25},{28,29}} | collective-permute-start | bytes 1179656 | tf_op jit(solution)/shard_map/ppermute | solution.py:261
  61.3 20.4 %collective-permute-start.23 = (f32[384,256]{1,0:T(8,128)S(1)}, f32[384,256]{1,0:T(8,128)}, u32[]{:S(2)}, u32[]{:S(2)}) collective-permute-start(f32[384,256]{1,0:T(8,128)S(1)} %collective-permute-done.22.refs_2_), channel_id=1, source_target_pairs={{2,3},{6,7},{10,11},{14,15},{18,19},{22,23},{26,27},{30,31}} | collective-permute-start | bytes 1179656 | tf_op jit(solution)/shard_map/ppermute | solution.py:261
  62.7 20.2 %collective-permute-start.18 = (f32[384,256]{1,0:T(8,128)S(1)}, f32[384,256]{1,0:T(8,128)S(1)}, u32[]{:S(2)}, u32[]{:S(2)}) collective-permute-start(f32[384,256]{1,0:T(8,128)S(1)} %copy-done.18), channel_id=1, source_target_pairs={{1,2},{5,6},{9,10},{13,14},{17,18},{21,22},{25,26},{29,30}} | collective-permute-start | bytes 1179656 | tf_op jit(solution)/shard_map/ppermute | solution.py:261
  64.1 19.6 %collective-permute-start.21 = (f32[384,256]{1,0:T(8,128)S(1)}, f32[384,256]{1,0:T(8,128)}, u32[]{:S(2)}, u32[]{:S(2)}) collective-permute-start(f32[384,256]{1,0:T(8,128)S(1)} %collective-permute-done.20.refs_2_), channel_id=1, source_target_pairs={{2,3},{6,7},{10,11},{14,15},{18,19},{22,23},{26,27},{30,31}} | collective-permute-start | bytes 1179656 | tf_op jit(solution)/shard_map/ppermute | solution.py:261
  66.9 18.1 %collective-permute-start.16 = (f32[384,256]{1,0:T(8,128)}, f32[384,256]{1,0:T(8,128)S(1)}, u32[]{:S(2)}, u32[]{:S(2)}) collective-permute-start(f32[384,256]{1,0:T(8,128)} %copy-done.20), channel_id=1, source_target_pairs={{1,2},{5,6},{9,10},{13,14},{17,18},{21,22},{25,26},{29,30}} | collective-permute-start | bytes 1179656 | tf_op jit(solution)/shard_map/ppermute | solution.py:261
  76.7 18.7 %collective-permute-start.9 = (f32[384,256]{1,0:T(8,128)}, f32[384,256]{1,0:T(8,128)S(1)}, u32[]{:S(2)}, u32[]{:S(2)}) collective-permute-start(f32[384,256]{1,0:T(8,128)} %pack6.1.refs_0_), channel_id=1, source_target_pairs={{0,1},{4,5},{8,9},{12,13},{16,17},{20,21},{24,25},{28,29}} | collective-permute-start | bytes 1179656 | tf_op jit(solution)/shard_map/ppermute | solution.py:261
  81.7 28.2 %collective-permute-start.6 = (f32[384,256]{1,0:T(8,128)}, f32[384,256]{1,0:T(8,128)S(1)}, u32[]{:S(2)}, u32[]{:S(2)}) collective-permute-start(f32[384,256]{1,0:T(8,128)} %pack7.1.refs_0_), channel_id=1, source_target_pairs={{0,1},{4,5},{8,9},{12,13},{16,17},{20,21},{24,25},{28,29}} | collective-permute-start | bytes 1179656 | tf_op jit(solution)/shard_map/ppermute | solution.py:261
  83.0 28.2 %collective-permute-start.19 = (f32[384,256]{1,0:T(8,128)S(1)}, f32[384,256]{1,0:T(8,128)S(1)}, u32[]{:S(2)}, u32[]{:S(2)}) collective-permute-start(f32[384,256]{1,0:T(8,128)S(1)} %collective-permute-done.18.refs_2_), channel_id=1, source_target_pairs={{2,3},{6,7},{10,11},{14,15},{18,19},{22,23},{26,27},{30,31}} | collective-permute-start | bytes 1179656 | tf_op jit(solution)/shard_map/ppermute | solution.py:261
  83.7 28.2 %collective-permute-start.14 = (f32[384,256]{1,0:T(8,128)S(1)}, f32[384,256]{1,0:T(8,128)S(1)}, u32[]{:S(2)}, u32[]{:S(2)}) collective-permute-start(f32[384,256]{1,0:T(8,128)S(1)} %copy-done.13), channel_id=1, source_target_pairs={{1,2},{5,6},{9,10},{13,14},{17,18},{21,22},{25,26},{29,30}} | collective-permute-start | bytes 1179656 | tf_op jit(solution)/shard_map/ppermute | solution.py:261
  85.0 27.6 %collective-permute-start.12 = (f32[384,256]{1,0:T(8,128)}, f32[384,256]{1,0:T(8,128)S(1)}, u32[]{:S(2)}, u32[]{:S(2)}) collective-permute-start(f32[384,256]{1,0:T(8,128)} %copy-done.10), channel_id=1, source_target_pairs={{1,2},{5,6},{9,10},{13,14},{17,18},{21,22},{25,26},{29,30}} | collective-permute-start | bytes 1179656 | tf_op jit(solution)/shard_map/ppermute | solution.py:261
  95.5 17.8 %collective-permute-start.10 = (f32[384,256]{1,0:T(8,128)S(1)}, f32[384,256]{1,0:T(8,128)S(1)}, u32[]{:S(2)}, u32[]{:S(2)}) collective-permute-start(f32[384,256]{1,0:T(8,128)S(1)} %collective-permute-done.9.refs_1_), channel_id=1, source_target_pairs={{1,2},{5,6},{9,10},{13,14},{17,18},{21,22},{25,26},{29,30}} | collective-permute-start | bytes 1179656 | tf_op jit(solution)/shard_map/ppermute | solution.py:261
  111.9 26.5 %collective-permute-start.15 = (f32[384,256]{1,0:T(8,128)S(1)}, f32[384,256]{1,0:T(8,128)S(1)}, u32[]{:S(2)}, u32[]{:S(2)}) collective-permute-start(f32[384,256]{1,0:T(8,128)S(1)} %collective-permute-done.14.refs_2_), channel_id=1, source_target_pairs={{2,3},{6,7},{10,11},{14,15},{18,19},{22,23},{26,27},{30,31}} | collective-permute-start | bytes 1179656 | tf_op jit(solution)/shard_map/ppermute | solution.py:261
  112.6 27.9 %collective-permute-start.13 = (f32[384,256]{1,0:T(8,128)S(1)}, f32[384,256]{1,0:T(8,128)S(1)}, u32[]{:S(2)}, u32[]{:S(2)}) collective-permute-start(f32[384,256]{1,0:T(8,128)S(1)} %collective-permute-done.12.refs_2_), channel_id=1, source_target_pairs={{2,3},{6,7},{10,11},{14,15},{18,19},{22,23},{26,27},{30,31}} | collective-permute-start | bytes 1179656 | tf_op jit(solution)/shard_map/ppermute | solution.py:261
  113.3 29.3 %collective-permute-start.11 = (f32[384,256]{1,0:T(8,128)S(1)}, f32[384,256]{1,0:T(8,128)S(1)}, u32[]{:S(2)}, u32[]{:S(2)}) collective-permute-start(f32[384,256]{1,0:T(8,128)S(1)} %collective-permute-done.10.refs_2_), channel_id=1, source_target_pairs={{2,3},{6,7},{10,11},{14,15},{18,19},{22,23},{26,27},{30,31}} | collective-permute-start | bytes 1179656 | tf_op jit(solution)/shard_map/ppermute | solution.py:261
  119.2 25.5 %collective-permute-start.8 = (f32[384,256]{1,0:T(8,128)S(1)}, f32[384,256]{1,0:T(8,128)S(1)}, u32[]{:S(2)}, u32[]{:S(2)}) collective-permute-start(f32[384,256]{1,0:T(8,128)S(1)} %collective-permute-done.7.refs_2_), channel_id=1, source_target_pairs={{2,3},{6,7},{10,11},{14,15},{18,19},{22,23},{26,27},{30,31}} | collective-permute-start | bytes 1179656 | tf_op jit(solution)/shard_map/ppermute | solution.py:261
  132.9 20.3 %collective-permute-start.25 = (f32[256,256]{1,0:T(8,128)}, f32[256,256]{1,0:T(8,128)}, u32[]{:S(2)}, u32[]{:S(2)}) collective-permute-start(f32[256,256]{1,0:T(8,128)} %collective-permute-done.24.refs_1_), channel_id=1, source_target_pairs={{1,2},{5,6},{9,10},{13,14},{17,18},{21,22},{25,26},{29,30}} | collective-permute-start | bytes 786440 | tf_op jit(solution)/shard_map/ppermute | solution.py:261
  147.6 12.4 %all-to-all-start.1 = ((f32[8,64,256]{2,1,0:T(8,128)}), f32[8,64,256]{2,1,0:T(8,128)}, u32[]{:S(2)}, u32[]{:S(2)}) async-start(f32[8,64,256]{2,1,0:T(8,128)} %bitcast.3), calls=%async_computation.1 | async-start | bytes 1048576 | tf_op jit(solution)/shard_map/all_to_all | solution.py:293
  (52 other events, 300.6 us)

commit v2 on v0

v2 whole, which is shorter than its diff:
```python
import jax
import jax.numpy as jnp
from jax import lax
from jax.experimental import pallas as pl
from jax.experimental.pallas import tpu as pltpu
from jax.sharding import PartitionSpec as P

PANEL = 256
CHUNKS = 12
LAG = 2
BLOCK = 32
HIGHEST = lax.Precision.HIGHEST
F32, BF16 = jnp.float32, jnp.bfloat16
ANY = pl.BlockSpec(memory_space=pl.ANY)
SMEM = pl.BlockSpec(memory_space=pltpu.SMEM)
VMEM = pl.BlockSpec(memory_space=pltpu.VMEM)


def params(mib):
    return pltpu.CompilerParams(vmem_limit_bytes=mib * 1024 * 1024)


def small():
    return pl.CostEstimate(flops=1, bytes_accessed=1, transcendentals=0)


def shape(*dims, dtype=F32):
    return jax.ShapeDtypeStruct(dims, dtype)


def split(x):
    hi = x.astype(BF16)
    return hi, (x - hi.astype(F32)).astype(BF16)


def dot(a, b, dims, precision=None):
    return lax.dot_general(
        a, b, (dims, ((), ())), precision=precision, preferred_element_type=F32
    )


def pack(matrix):
    rows = matrix.shape[0] // CHUNKS

    def body(source, *refs):
        outs, sems = refs[:CHUNKS], refs[CHUNKS]
        copies = [
            pltpu.make_async_copy(
                source.at[pl.ds(k * rows, rows), pl.ds(0, PANEL)], out, sems.at[k]
            )
            for k, out in enumerate(outs)
        ]
        for copy in copies:
            copy.start()
        for copy in copies:
            copy.wait()

    return pl.pallas_call(
        body,
        in_specs=[ANY],
        out_specs=(VMEM,) * CHUNKS,
        out_shape=(shape(rows, PANEL),) * CHUNKS,
        scratch_shapes=[pltpu.SemaphoreType.DMA((CHUNKS,))],
        compiler_params=params(5),
        cost_estimate=small(),
        name="pack",
    )(matrix)


def gate(x, *after):
    def body(*refs):
        pass

    return pl.pallas_call(
        body,
        in_specs=[ANY] * (1 + len(after)),
        out_specs=ANY,
        out_shape=shape(*x.shape, dtype=x.dtype),
        input_output_aliases={0: 0},
        compiler_params=params(1),
        cost_estimate=small(),
        name="gate",
    )(x, *after)


def fill(place, received, own, *after):
    def body(place_ref, _, own_ref, *refs):
        @pl.when(place_ref[0] == 0)
        def _():
            source = own_ref.at[:, pl.ds(own.shape[1] - PANEL, PANEL)]
            copy = pltpu.make_async_copy(source, refs[-2], refs[-1])
            copy.start()
            copy.wait()

    return pl.pallas_call(
        body,
        in_specs=[SMEM] + [ANY] * (2 + len(after)),
        out_specs=ANY,
        out_shape=shape(*received.shape),
        input_output_aliases={1: 0},
        scratch_shapes=[pltpu.SemaphoreType.DMA(())],
        compiler_params=params(1),
        cost_estimate=small(),
        name="fill",
    )(place, received, own, *after)


def halve(total, place_ref, keep, give, pairs):
    size = total.shape[0] // (2 * pairs)
    core = place_ref[1] % 2
    for k in range(pairs):
        here = slice(k * size, (k + 1) * size)
        mine = pl.multiple_of((2 * k + core) * size, size)
        other = pl.multiple_of((2 * k + 1 - core) * size, size)
        keep[here, :] = total[pl.ds(mine, size), :]
        give[here, :] = total[pl.ds(other, size), :]


def spread(place, keep, got, pairs):
    size = keep.shape[0] // pairs

    def body(place_ref, keep_ref, got_ref, *outs):
        chip = place_ref[1] // 2
        for j, out in enumerate(outs):
            here = pl.ds(pl.multiple_of((chip ^ j) * size, size), size)
            out[...] = keep_ref[here, :] + got_ref[here, :]

    return pl.pallas_call(
        body,
        in_specs=[SMEM, VMEM, VMEM],
        out_specs=(VMEM,) * pairs,
        out_shape=(shape(size, PANEL),) * pairs,
        compiler_params=params(4),
        cost_estimate=small(),
        name="spread",
    )(place, keep, got)


def add(parts):
    def body(*refs):
        total = refs[0][...]
        for ref in refs[1:-1]:
            total += ref[...]
        refs[-1][...] = total

    return pl.pallas_call(
        body,
        in_specs=[VMEM] * len(parts),
        out_specs=VMEM,
        out_shape=shape(*parts[0].shape),
        compiler_params=params(2),
        cost_estimate=small(),
        name="add",
    )(*parts)


def gram_part(place, chunks, pairs):
    def body(place_ref, *refs):
        sources, (keep, give, held) = refs[:-3], refs[-3:]

        @pl.when(place_ref[0] == 0)
        def _():
            total = jnp.zeros((PANEL, PANEL), F32)
            for ref in sources:
                x = ref[...]
                total += dot(x, x, ((0,), (0,)), HIGHEST)
            held[...] = total
            halve(held, place_ref, keep, give, pairs)

    return pl.pallas_call(
        body,
        in_specs=[SMEM] + [VMEM] * len(chunks),
        out_specs=(VMEM, VMEM),
        out_shape=(shape(PANEL // 2, PANEL),) * 2,
        scratch_shapes=[pltpu.VMEM((PANEL, PANEL), F32)],
        compiler_params=params(8),
        cost_estimate=small(),
        name="gram",
    )(place, *chunks)


def eliminate(col, state, block):
    first, last = block * BLOCK, (block + 1) * BLOCK
    width = 2 * PANEL

    def body(col_ref, src, out):
        @pl.when(col_ref[0] == 0)
        def _():
            if block == 0:
                row = lax.broadcasted_iota(jnp.int32, (PANEL, PANEL), 0)
                lane = lax.broadcasted_iota(jnp.int32, (PANEL, PANEL), 1)
                out[:, :PANEL] = src[...]
                out[:, PANEL:] = (row == lane).astype(F32)
            else:
                out[...] = src[...]
            row = lax.broadcasted_iota(jnp.int32, (BLOCK, BLOCK), 0)
            lane = lax.broadcasted_iota(jnp.int32, (BLOCK, BLOCK), 1)
            work = jnp.concatenate(
                [out[first:last, first:last], (row == lane).astype(F32)], axis=1
            )
            below = lax.broadcasted_iota(jnp.int32, (BLOCK, 2 * BLOCK), 0)
            scale = jnp.zeros((BLOCK, 2 * BLOCK), F32)
            for i in range(0, BLOCK, 2):
                column = jnp.broadcast_to(work[:, i : i + 1], work.shape)
                follow = jnp.broadcast_to(work[:, i + 1 : i + 2], work.shape)
                upper, lower = work[i : i + 1, :], work[i + 1 : i + 2, :]
                pivot, cross = column[i : i + 1, :], column[i + 1 : i + 2, :]
                inverse = 1.0 / pivot
                ratio = cross * inverse
                second = follow[i + 1 : i + 2, :] - ratio * follow[i : i + 1, :]
                factor = jnp.where(below > i, column * inverse, 0.0)
                follow = follow - factor * follow[i : i + 1, :]
                after = jnp.where(below > i + 1, follow * (1.0 / second), 0.0)
                lower = lower - ratio * upper
                work = work - factor * upper - after * lower
                scale = jnp.where(below == i, pivot, jnp.where(below == i + 1, second, scale))
            root = lax.rsqrt(scale)
            root = root * (1.5 - 0.5 * scale * root * root)
            rows = dot((work * root)[:, BLOCK:], out[first:last, :], ((1,), (0,)), HIGHEST)
            out[first:last, :] = rows
            if last < PANEL:
                left, right = last // 128 * 128, PANEL + -(-last // 128) * 128
                out[last:, left:right] -= dot(
                    rows[:, last:PANEL], rows[:, left:right], ((0,), (0,)), HIGHEST
                )

    return pl.pallas_call(
        body,
        in_specs=[SMEM, VMEM],
        out_specs=VMEM,
        out_shape=shape(PANEL, width),
        input_output_aliases={1: 0} if block else {},
        compiler_params=params(8),
        cost_estimate=small(),
        name=f"eliminate{block}",
    )(col, state)


def consume(place, matrix, sent, step, before, pairs):
    rows, width = sent.shape[0], matrix.shape[1]

    def body(place_ref, block, source, *refs):
        if pairs:
            total, _, keep, give, halves, held, sem, turned = refs
        elif step:
            total, _, out, halves, held, sem = refs
        else:
            out, halves, held, sem = refs
        chunk = step - LAG * place_ref[0]
        valid = (chunk >= 0) & (chunk < CHUNKS)

        def part():
            here = pl.ds(pl.multiple_of(chunk * rows, rows), rows)
            high, low = split(source[...])
            held[:, :PANEL] = high
            held[:, PANEL:] = low
            copy = pltpu.make_async_copy(held, halves.at[here, :], sem)
            copy.start()
            a_high, a_low = split(block[here, :])
            dims = ((0,), (0,))
            value = dot(high, a_high, dims) + dot(low, a_high, dims) + dot(high, a_low, dims)
            copy.wait()
            return value

        if pairs:
            turned[...] = total[...].T

            @pl.when(valid)
            def _():
                turned[...] += part().T

            halve(turned, place_ref, keep, give, pairs)
        else:
            out[...] = total[...] if step else jnp.zeros_like(out)

            @pl.when(valid)
            def _():
                out[...] += part()

    halves = shape(matrix.shape[0], 2 * PANEL, dtype=BF16)
    if pairs:
        outs = (shape(width // 2, PANEL),) * 2 + (halves,)
    else:
        outs = (shape(PANEL, width), halves)
    return pl.pallas_call(
        body,
        in_specs=[SMEM, VMEM, VMEM] + ([VMEM, ANY] if step else []),
        out_specs=(VMEM,) * (len(outs) - 1) + (ANY,),
        out_shape=outs,
        input_output_aliases={4: len(outs) - 1} if step else {},
        scratch_shapes=[pltpu.VMEM((rows, 2 * PANEL), BF16), pltpu.SemaphoreType.DMA(())]
        + ([pltpu.VMEM((width, PANEL), F32)] if pairs else []),
        compiler_params=params(16),
        cost_estimate=small(),
        name="consume",
    )(place, matrix, sent, *before)


def solve(place, parts, hops):
    n, rows = len(parts), parts[0].shape[0]

    def body(col_ref, *refs):
        sources, (top, coeffs, inverse) = refs[n : n + len(hops)], refs[n + len(hops) :]
        for h, source in enumerate(sources):

            @pl.when(col_ref[0] == h)
            def _():
                inverse[...] = source[...]

        total = refs[0][...]
        for ref in refs[1:n]:
            total += ref[...]
        value = dot(total, inverse[...], ((1,), (1,)), HIGHEST)
        top[...] = value
        coeffs[...] = dot(value, inverse[...], ((1,), (0,)), HIGHEST)

    return pl.pallas_call(
        body,
        in_specs=[SMEM] + [VMEM] * (n + len(hops)),
        out_specs=(VMEM, VMEM),
        out_shape=(shape(rows, PANEL),) * 2,
        scratch_shapes=[pltpu.VMEM((PANEL, PANEL), F32)],
        compiler_params=params(4),
        cost_estimate=small(),
        name="solve",
    )(place, *parts, *hops)


def subtract(matrix, halves, coeffs):
    rows, width = matrix.shape
    tiles = 12
    size = rows // tiles
    slots = 3

    def body(a, p, c, out, ct, held, sems):
        ct_high, ct_low = split(c[...].T)
        ct[:PANEL, :] = ct_high
        ct[PANEL : 2 * PANEL, :] = ct_high
        ct[2 * PANEL :, :] = ct_low
        copies = [
            pltpu.make_async_copy(
                held.at[t % slots], out.at[pl.ds(t * size, size), :], sems.at[t % slots]
            )
            for t in range(tiles)
        ]
        for t in range(tiles):
            here = slice(t * size, (t + 1) * size)
            both = p[here, :]
            thrice = jnp.concatenate([both, both[:, :PANEL]], axis=1)
            value = a[here, :] - dot(thrice, ct[...], ((1,), (0,)))
            if t >= slots:
                copies[t - slots].wait()
            held[t % slots] = value
            copies[t].start()
        for t in range(tiles - slots, tiles):
            copies[t].wait()

    return pl.pallas_call(
        body,
        in_specs=[VMEM] * 3,
        out_specs=ANY,
        out_shape=shape(rows, width),
        scratch_shapes=[
            pltpu.VMEM((3 * PANEL, width), BF16),
            pltpu.VMEM((slots, size, width), F32),
            pltpu.SemaphoreType.DMA((slots,)),
        ],
        compiler_params=params(20),
        cost_estimate=small(),
        name="subtract",
    )(matrix, halves, coeffs)


def program(n_row, n_col):
    shift = [(h, h + 1) for h in range(n_col - 1)]
    pairs = n_row // 2

    def scatter(place, keep, give):
        got = lax.ppermute(give, "row", [(r, r ^ 1) for r in range(n_row)])
        parts = spread(place, keep, got, pairs)
        return [parts[0]] + [
            lax.ppermute(parts[j], "row", [(r, r ^ (2 * j)) for r in range(n_row)])
            for j in range(1, pairs)
        ]

    def shards(matrix):
        place = jnp.stack([lax.axis_index("col"), lax.axis_index("row")]).astype(jnp.int32)
        blocks = PANEL // BLOCK
        shifts = CHUNKS + 1 + LAG * (n_col - 2)
        last = CHUNKS - 1 + LAG * (n_col - 1)
        own = pack(matrix)
        sent, received, sums = [], [], []
        state = None
        done = 0
        for s in range(max(shifts, last + 1) + 1):
            if s < LAG:
                sent.append(own[s])
            elif s < shifts:
                after = [sums[s - LAG][0]] if s - LAG < len(sums) else []
                if state is not None:
                    after.append(state)
                source = own[s] if s < CHUNKS else state if s == CHUNKS else None
                x = received[s - LAG]
                sent.append(gate(x, *after) if source is None else fill(place, x, source, *after))
            elif s - LAG < shifts:
                sent.append(received[s - LAG])
            if s < shifts:
                received.append(lax.ppermute(sent[s], "col", shift))
            if s <= last:
                sums.append(
                    consume(
                        place,
                        matrix,
                        sent[s],
                        s,
                        sums[-1] if s else (),
                        pairs if s == last else 0,
                    )
                )
            if s == LAG - 1:
                state = add(scatter(place, *gram_part(place, own, pairs)))
            elif s == 2 * LAG - 1:
                state = lax.all_gather(gate(state, received[s - LAG]), "row", axis=0, tiled=True)
            elif s >= 2 * LAG and done < blocks:
                state = eliminate(place, gate(state, received[s - LAG]), done)
                done += 1
        keep, give, halves = sums[-1]
        parts = scatter(place, keep, give)
        top_rows, coeffs = solve(place, parts, [sent[CHUNKS + LAG * h] for h in range(n_col)])
        coeffs = lax.all_gather(coeffs, "row", axis=0, tiled=True)
        return top_rows, subtract(matrix, halves, coeffs)

    return shards


def solution(mesh):
    return jax.shard_map(
        program(mesh.shape["row"], mesh.shape["col"]),
        mesh=mesh,
        in_specs=(P("row", "col"),),
        out_specs=(P(("col", "row"), None), P("row", "col")),
        check_vma=False,
    )
```

time: 295 us -> 150 us (0.51)
  the two profiles are of different devices: /device:TPU:17 before, /device:TPU:0 now
where the time goes in v2:
time: 150 us; the launch traced here: 149 us
  Pallas kernels  62.7 us (42%)
  starting transfers between devices  48.3 us (32%)
  blocking collectives  19.4 us (13%)
  waiting for transfers between devices  11.1 us (7%)
  local copies, waits for them, and re-layouts  5.79 us (4%)
  between operations  1.57 us (1%)
    ppermute x17, starting transfers between devices, shards(): received.append(lax.ppermute(sent[s], 'col', shift))  41.1 us
    pallas_call x8, Pallas kernels, eliminate(): pl.pallas_call(body, in_specs=[SMEM, VMEM], out_specs=VMEM, out_shape=sha...  25 us
    pallas_call x18, Pallas kernels, consume(): pl.pallas_call(body, in_specs=[SMEM, VMEM, VMEM] + ([VMEM, ANY] if step e...  17.9 us
    all_gather x1, blocking collectives, shards(): coeffs = lax.all_gather(coeffs, 'row', axis=0, tiled=True)  10 us
    all_gather x1, blocking collectives, shards(): lax.all_gather(gate(state, received[s - LAG]), 'row', axis=0, tiled=True)  9.32 us
    ppermute x17, waiting for transfers between devices, shards(): received.append(lax.ppermute(sent[s], 'col', shift))  7.78 us
    ppermute x6, starting transfers between devices, scatter(): lax.ppermute(parts[j], 'row', [(r, r ^ 2 * j) for r in range(n_row)])  7.11 us
    pallas_call x11, Pallas kernels, fill(): pl.pallas_call(body, in_specs=[SMEM] + [ANY] * (2 + len(after)), out_spec...  6.35 us
  transfers between devices with their start and end apart: 25, of which 7 were waited for; matrix products, arithmetic and copies ran while one was open for 0% of the time, Pallas kernels for 36%

profile of v2, /device:TPU:0, one launch (start us, length us, event | category | flops | bytes accessed | tf_op | source)
XLA Modules:
  0.0 148.9 jit_solution(1961572321002472662)
XLA Ops:
  0.6 2.8 %copy-done = f32[3072,512]{1,0:T(8,128)S(1)} copy-done((f32[3072,512]{1,0:T(8,128)S(1)}, f32[3072,512]{1,0:T(8,128)}, u32[]{:S(2)}) %copy-start) | copy-done | bytes 6291480
  4.5 4.9 %collective-permute-start = (f32[256,256]{1,0:T(8,128)S(1)}, f32[256,256]{1,0:T(8,128)S(1)}, u32[]{:S(2)}, u32[]{:S(2)}) collective-permute-start(f32[256,256]{1,0:T(8,128)S(1)} %get-tuple-element.63.source.refs_1_), channel_id=1, source_target_pairs={{0,1},{1,2},{2,3},{4,5},{5,6},{6,7},{8,9},{9,10},{10,11},{12,13},{... | collective-permute-start | bytes 786440 | tf_op jit(solution)/shard_map/ppermute | solution.py:408
  9.4 3.5 %collective-permute-start.6 = (f32[256,256]{1,0:T(8,128)}, f32[256,256]{1,0:T(8,128)S(1)}, u32[]{:S(2)}, u32[]{:S(2)}) collective-permute-start(f32[256,256]{1,0:T(8,128)} %get-tuple-element.65.source.refs_0_), channel_id=1, source_target_pairs={{0,1},{1,2},{2,3},{4,5},{5,6},{6,7},{8,9},{9,10},{10,11},{12,13},{... | collective-permute-start | bytes 786440 | tf_op jit(solution)/shard_map/ppermute | solution.py:408
  13.0 4.0 %gram.1 = (f32[128,256]{1,0:T(8,128)S(1)}, f32[128,256]{1,0:T(8,128)S(1)}) custom-call(s32[2]{0:T(128)S(1)} %pad_add_fusion.place_ref.col_ref, f32[256,256]{1,0:T(8,128)} %get-tuple-element.65.source.refs_0_, f32[256,256]{1,0:T(8,128)S(1)} %get-tuple-element.63.source.refs_1_, f32[256,256]{1,0:T(8,128)S(1)} %get-tuple-element.69.refs_2_.own_ref, ...), custom_call_target="tpu_custom_call" | custom-call | flops 1 | bytes 1 | tf_op jit(solution)/shard_map/gram/pallas_call | solution.py:170
  22.6 2.8 %copy-done.1 = f32[3072,512]{1,0:T(8,128)S(1)} copy-done((f32[3072,512]{1,0:T(8,128)S(1)}, f32[3072,512]{1,0:T(8,128)}, u32[]{:S(2)}) %copy-start.1) | copy-done | bytes 6291480
  33.1 9.3 %all_gather.6.refs_0_.refs_1_ = f32[256,256]{1,0:T(8,128)S(1)} all-gather(f32[32,256]{1,0:T(8,128)S(1)} %gate.13), channel_id=1, replica_groups=mesh['row'=8,'col'=4] {'row'}, dimensions={0}, use_global_device_ids=true | all-gather | bytes 294912 | tf_op jit(solution)/shard_map/all_gather | solution.py:423
  43.0 1.8 %collective-permute-start.9 = (f32[256,256]{1,0:T(8,128)S(1)}, f32[256,256]{1,0:T(8,128)S(1)}, u32[]{:S(2)}, u32[]{:S(2)}) collective-permute-start(f32[256,256]{1,0:T(8,128)S(1)} %fill.14.source), channel_id=1, source_target_pairs={{0,1},{1,2},{2,3},{4,5},{5,6},{6,7},{8,9},{9,10},{10,11},{12,13},{... | collective-permute-start | bytes 786440 | tf_op jit(solution)/shard_map/ppermute | solution.py:408
  45.9 3.3 %eliminate0.1.refs_1_ = f32[256,512]{1,0:T(8,128)S(1)} custom-call(s32[2]{0:T(128)S(1)} %pad_add_fusion.place_ref.col_ref, f32[256,256]{1,0:T(8,128)S(1)} %gate.14.src), custom_call_target="tpu_custom_call" | custom-call | flops 1 | bytes 1 | tf_op jit(solution)/shard_map/eliminate0/pallas_call | solution.py:227
  51.2 3.3 %eliminate1.1.refs_0_.refs_1_ = f32[256,512]{1,0:T(8,128)S(1)} custom-call(s32[2]{0:T(128)S(1)} %pad_add_fusion.place_ref.col_ref, f32[256,512]{1,0:T(8,128)S(1)} %gate.15.src), custom_call_target="tpu_custom_call", output_to_operand_aliasing={{}: (1, {})} | custom-call | flops 1 | bytes 1 | tf_op jit(solution)/shard_map/eliminate1/pallas_call | solution.py:227
  58.7 3.3 %eliminate2.1.refs_1_ = f32[256,512]{1,0:T(8,128)S(1)} custom-call(s32[2]{0:T(128)S(1)} %pad_add_fusion.place_ref.col_ref, f32[256,512]{1,0:T(8,128)S(1)} %gate.16.src), custom_call_target="tpu_custom_call", output_to_operand_aliasing={{}: (1, {})} | custom-call | flops 1 | bytes 1 | tf_op jit(solution)/shard_map/eliminate2/pallas_call | solution.py:227
  64.0 3.1 %eliminate3.1.refs_0_.refs_1_ = f32[256,512]{1,0:T(8,128)S(1)} custom-call(s32[2]{0:T(128)S(1)} %pad_add_fusion.place_ref.col_ref, f32[256,512]{1,0:T(8,128)S(1)} %gate.17.src), custom_call_target="tpu_custom_call", output_to_operand_aliasing={{}: (1, {})} | custom-call | flops 1 | bytes 1 | tf_op jit(solution)/shard_map/eliminate3/pallas_call | solution.py:227
  71.5 3.1 %eliminate4.1.refs_1_ = f32[256,512]{1,0:T(8,128)S(1)} custom-call(s32[2]{0:T(128)S(1)} %pad_add_fusion.place_ref.col_ref, f32[256,512]{1,0:T(8,128)S(1)} %gate.18.src), custom_call_target="tpu_custom_call", output_to_operand_aliasing={{}: (1, {})} | custom-call | flops 1 | bytes 1 | tf_op jit(solution)/shard_map/eliminate4/pallas_call | solution.py:227
  76.6 3.1 %eliminate5.1.refs_0_.refs_1_ = f32[256,512]{1,0:T(8,128)S(1)} custom-call(s32[2]{0:T(128)S(1)} %pad_add_fusion.place_ref.col_ref, f32[256,512]{1,0:T(8,128)S(1)} %gate.19.src), custom_call_target="tpu_custom_call", output_to_operand_aliasing={{}: (1, {})} | custom-call | flops 1 | bytes 1 | tf_op jit(solution)/shard_map/eliminate5/pallas_call | solution.py:227
  83.9 3.1 %eliminate6.1.refs_1_ = f32[256,512]{1,0:T(8,128)S(1)} custom-call(s32[2]{0:T(128)S(1)} %pad_add_fusion.place_ref.col_ref, f32[256,512]{1,0:T(8,128)S(1)} %gate.20.src), custom_call_target="tpu_custom_call", output_to_operand_aliasing={{}: (1, {})} | custom-call | flops 1 | bytes 1 | tf_op jit(solution)/shard_map/eliminate6/pallas_call | solution.py:227
  88.9 2.8 %eliminate7.1.refs_2_.own_ref.refs_1_ = f32[256,512]{1,0:T(8,128)S(1)} custom-call(s32[2]{0:T(128)S(1)} %pad_add_fusion.place_ref.col_ref, f32[256,512]{1,0:T(8,128)S(1)} %gate.21.src), custom_call_target="tpu_custom_call", output_to_operand_aliasing={{}: (1, {})} | custom-call | flops 1 | bytes 1 | tf_op jit(solution)/shard_map/eliminate7/pallas_call | solution.py:227
  93.4 2.0 %collective-permute-start.18 = (f32[256,256]{1,0:T(8,128)S(1)}, f32[256,256]{1,0:T(8,128)S(1)}, u32[]{:S(2)}, u32[]{:S(2)}) collective-permute-start(f32[256,256]{1,0:T(8,128)S(1)} %fill.21.source.refs_4_), channel_id=1, source_target_pairs={{0,1},{1,2},{2,3},{4,5},{5,6},{6,7},{8,9},{9,10},{10,11},{12,13},{... | collective-permute-start | bytes 786440 | tf_op jit(solution)/shard_map/ppermute | solution.py:408
  96.7 3.6 %collective-permute-start.15 = (f32[256,256]{1,0:T(8,128)S(1)}, f32[256,256]{1,0:T(8,128)S(1)}, u32[]{:S(2)}, u32[]{:S(2)}) collective-permute-start(f32[256,256]{1,0:T(8,128)S(1)} %gate.22.source), channel_id=1, source_target_pairs={{0,1},{1,2},{2,3},{4,5},{5,6},{6,7},{8,9},{9,10},{10,11},{12,13},{... | collective-permute-start | bytes 786440 | tf_op jit(solution)/shard_map/ppermute | solution.py:408
  102.2 4.4 %collective-permute-start.19 = (f32[256,256]{1,0:T(8,128)S(1)}, f32[256,256]{1,0:T(8,128)S(1)}, u32[]{:S(2)}, u32[]{:S(2)}) collective-permute-start(f32[256,256]{1,0:T(8,128)S(1)} %gate.24.source.refs_5_), channel_id=1, source_target_pairs={{0,1},{1,2},{2,3},{4,5},{5,6},{6,7},{8,9},{9,10},{10,11},{12,13},{... | collective-permute-start | bytes 786440 | tf_op jit(solution)/shard_map/ppermute | solution.py:408
  107.8 4.4 %collective-permute-start.17 = (f32[256,256]{1,0:T(8,128)S(1)}, f32[256,256]{1,0:T(8,128)S(1)}, u32[]{:S(2)}, u32[]{:S(2)}) collective-permute-start(f32[256,256]{1,0:T(8,128)S(1)} %gate.23.source), channel_id=1, source_target_pairs={{0,1},{1,2},{2,3},{4,5},{5,6},{6,7},{8,9},{9,10},{10,11},{12,13},{... | collective-permute-start | bytes 786440 | tf_op jit(solution)/shard_map/ppermute | solution.py:408
  114.0 4.0 %collective-permute-done.17.source = f32[256,256]{1,0:T(8,128)S(1)} collective-permute-done((f32[256,256]{1,0:T(8,128)S(1)}, f32[256,256]{1,0:T(8,128)S(1)}, u32[]{:S(2)}, u32[]{:S(2)}) %collective-permute-start.17) | collective-permute-done | bytes 262176 | tf_op jit(solution)/shard_map/ppermute | solution.py:408
  118.9 4.7 %collective-permute-start.24 = (f32[256,256]{1,0:T(8,128)S(1)}, f32[256,256]{1,0:T(8,128)S(1)}, u32[]{:S(2)}, u32[]{:S(2)}) collective-permute-start(f32[256,256]{1,0:T(8,128)S(1)} %gate.25.source.refs_6_), channel_id=1, source_target_pairs={{0,1},{1,2},{2,3},{4,5},{5,6},{6,7},{8,9},{9,10},{10,11},{12,13},{... | collective-permute-start | bytes 786440 | tf_op jit(solution)/shard_map/ppermute | solution.py:408
  127.7 1.8 %collective-permute-done.24.refs_7_ = f32[256,256]{1,0:T(8,128)S(1)} collective-permute-done((f32[256,256]{1,0:T(8,128)S(1)}, f32[256,256]{1,0:T(8,128)S(1)}, u32[]{:S(2)}, u32[]{:S(2)}) %collective-permute-start.24) | collective-permute-done | bytes 262176 | tf_op jit(solution)/shard_map/ppermute | solution.py:408
  133.2 10.0 %all_gather.7.c = f32[512,256]{1,0:T(8,128)S(1)} all-gather(f32[64,256]{1,0:T(8,128)S(1)} %get-tuple-element.123), channel_id=1, replica_groups=mesh['row'=8,'col'=4] {'row'}, dimensions={0}, use_global_device_ids=true | all-gather | bytes 589824 | tf_op jit(solution)/shard_map/all_gather | solution.py:430
  143.2 5.5 %subtract.1 = f32[3072,512]{1,0:T(8,128)} custom-call(f32[3072,512]{1,0:T(8,128)S(1)} %bitcast.3, bf16[3072,512]{1,0:T(8,128)(2,1)S(1)} %get-tuple-element.122.p, f32[512,256]{1,0:T(8,128)S(1)} %all_gather.7.c), custom_call_target="tpu_custom_call" | custom-call | flops 1 | bytes 1 | tf_op jit(solution)/shard_map/subtract/pallas_call | solution.py:358
  (104 shorter events, 52.8 us)
Async XLA Ops:
  4.5 25.5 %collective-permute-start = (f32[256,256]{1,0:T(8,128)S(1)}, f32[256,256]{1,0:T(8,128)S(1)}, u32[]{:S(2)}, u32[]{:S(2)}) collective-permute-start(f32[256,256]{1,0:T(8,128)S(1)} %get-tuple-element.63.source.refs_1_), channel_id=1, source_target_pairs={{0,1},{1,2},{2,3},{4,5},{5,6},{6,7},{8,9},{9,10},{10,11},{12,13},{... | collective-permute-start | bytes 786440 | tf_op jit(solution)/shard_map/ppermute | solution.py:408
  9.4 17.5 %collective-permute-start.6 = (f32[256,256]{1,0:T(8,128)}, f32[256,256]{1,0:T(8,128)S(1)}, u32[]{:S(2)}, u32[]{:S(2)}) collective-permute-start(f32[256,256]{1,0:T(8,128)} %get-tuple-element.65.source.refs_0_), channel_id=1, source_target_pairs={{0,1},{1,2},{2,3},{4,5},{5,6},{6,7},{8,9},{9,10},{10,11},{12,13},{... | collective-permute-start | bytes 786440 | tf_op jit(solution)/shard_map/ppermute | solution.py:408
  19.0 7.9 %collective-permute-start.2 = (f32[32,256]{1,0:T(8,128)S(1)}, f32[32,256]{1,0:T(8,128)S(1)}, u32[]{:S(2)}, u32[]{:S(2)}) collective-permute-start(f32[32,256]{1,0:T(8,128)S(1)} %get-tuple-element.81), channel_id=1, source_target_pairs={{0,8},{4,12},{8,0},{12,4},{16,24},{20,28},{24,16},{28,20},{1,9},{5... | collective-permute-start | bytes 98312 | tf_op jit(solution)/shard_map/ppermute | solution.py:382
  20.6 6.3 %collective-permute-start.3 = (f32[32,256]{1,0:T(8,128)S(1)}, f32[32,256]{1,0:T(8,128)S(1)}, u32[]{:S(2)}, u32[]{:S(2)}) collective-permute-start(f32[32,256]{1,0:T(8,128)S(1)} %get-tuple-element.82), channel_id=1, source_target_pairs={{0,16},{4,20},{8,24},{12,28},{16,0},{20,4},{24,8},{28,12},{1,17},{... | collective-permute-start | bytes 98312 | tf_op jit(solution)/shard_map/ppermute | solution.py:382
  22.1 4.8 %collective-permute-start.4 = (f32[32,256]{1,0:T(8,128)S(1)}, f32[32,256]{1,0:T(8,128)S(1)}, u32[]{:S(2)}, u32[]{:S(2)}) collective-permute-start(f32[32,256]{1,0:T(8,128)S(1)} %get-tuple-element.83), channel_id=1, source_target_pairs={{0,24},{4,28},{8,16},{12,20},{16,8},{20,12},{24,0},{28,4},{1,25},{... | collective-permute-start | bytes 98312 | tf_op jit(solution)/shard_map/ppermute | solution.py:382
  27.5 14.9 %collective-permute-start.7 = (f32[256,256]{1,0:T(8,128)S(1)}, f32[256,256]{1,0:T(8,128)S(1)}, u32[]{:S(2)}, u32[]{:S(2)}) collective-permute-start(f32[256,256]{1,0:T(8,128)S(1)} %fill.12.source), channel_id=1, source_target_pairs={{0,1},{1,2},{2,3},{4,5},{5,6},{6,7},{8,9},{9,10},{10,11},{12,13},{... | collective-permute-start | bytes 786440 | tf_op jit(solution)/shard_map/ppermute | solution.py:408
  30.6 18.6 %collective-permute-start.5 = (f32[256,256]{1,0:T(8,128)S(1)}, f32[256,256]{1,0:T(8,128)S(1)}, u32[]{:S(2)}, u32[]{:S(2)}) collective-permute-start(f32[256,256]{1,0:T(8,128)S(1)} %fill.11.source), channel_id=1, source_target_pairs={{0,1},{1,2},{2,3},{4,5},{5,6},{6,7},{8,9},{9,10},{10,11},{12,13},{... | collective-permute-start | bytes 786440 | tf_op jit(solution)/shard_map/ppermute | solution.py:408
  43.0 12.6 %collective-permute-start.9 = (f32[256,256]{1,0:T(8,128)S(1)}, f32[256,256]{1,0:T(8,128)S(1)}, u32[]{:S(2)}, u32[]{:S(2)}) collective-permute-start(f32[256,256]{1,0:T(8,128)S(1)} %fill.14.source), channel_id=1, source_target_pairs={{0,1},{1,2},{2,3},{4,5},{5,6},{6,7},{8,9},{9,10},{10,11},{12,13},{... | collective-permute-start | bytes 786440 | tf_op jit(solution)/shard_map/ppermute | solution.py:408
  49.9 12.2 %collective-permute-start.8 = (f32[256,256]{1,0:T(8,128)S(1)}, f32[256,256]{1,0:T(8,128)S(1)}, u32[]{:S(2)}, u32[]{:S(2)}) collective-permute-start(f32[256,256]{1,0:T(8,128)S(1)} %fill.13.source), channel_id=1, source_target_pairs={{0,1},{1,2},{2,3},{4,5},{5,6},{6,7},{8,9},{9,10},{10,11},{12,13},{... | collective-permute-start | bytes 786440 | tf_op jit(solution)/shard_map/ppermute | solution.py:408
  56.3 11.9 %collective-permute-start.11 = (f32[256,256]{1,0:T(8,128)S(1)}, f32[256,256]{1,0:T(8,128)S(1)}, u32[]{:S(2)}, u32[]{:S(2)}) collective-permute-start(f32[256,256]{1,0:T(8,128)S(1)} %fill.16.source), channel_id=1, source_target_pairs={{0,1},{1,2},{2,3},{4,5},{5,6},{6,7},{8,9},{9,10},{10,11},{12,13},{... | collective-permute-start | bytes 786440 | tf_op jit(solution)/shard_map/ppermute | solution.py:408
  62.6 12.0 %collective-permute-start.10 = (f32[256,256]{1,0:T(8,128)S(1)}, f32[256,256]{1,0:T(8,128)S(1)}, u32[]{:S(2)}, u32[]{:S(2)}) collective-permute-start(f32[256,256]{1,0:T(8,128)S(1)} %fill.15.source), channel_id=1, source_target_pairs={{0,1},{1,2},{2,3},{4,5},{5,6},{6,7},{8,9},{9,10},{10,11},{12,13},{... | collective-permute-start | bytes 786440 | tf_op jit(solution)/shard_map/ppermute | solution.py:408
  68.8 12.0 %collective-permute-start.13 = (f32[256,256]{1,0:T(8,128)S(1)}, f32[256,256]{1,0:T(8,128)S(1)}, u32[]{:S(2)}, u32[]{:S(2)}) collective-permute-start(f32[256,256]{1,0:T(8,128)S(1)} %fill.18.source), channel_id=1, source_target_pairs={{0,1},{1,2},{2,3},{4,5},{5,6},{6,7},{8,9},{9,10},{10,11},{12,13},{... | collective-permute-start | bytes 786440 | tf_op jit(solution)/shard_map/ppermute | solution.py:408
  75.3 11.8 %collective-permute-start.12 = (f32[256,256]{1,0:T(8,128)S(1)}, f32[256,256]{1,0:T(8,128)S(1)}, u32[]{:S(2)}, u32[]{:S(2)}) collective-permute-start(f32[256,256]{1,0:T(8,128)S(1)} %fill.17.source), channel_id=1, source_target_pairs={{0,1},{1,2},{2,3},{4,5},{5,6},{6,7},{8,9},{9,10},{10,11},{12,13},{... | collective-permute-start | bytes 786440 | tf_op jit(solution)/shard_map/ppermute | solution.py:408
  82.6 10.2 %collective-permute-start.16 = (f32[256,256]{1,0:T(8,128)S(1)}, f32[256,256]{1,0:T(8,128)S(1)}, u32[]{:S(2)}, u32[]{:S(2)}) collective-permute-start(f32[256,256]{1,0:T(8,128)S(1)} %fill.20.source), channel_id=1, source_target_pairs={{0,1},{1,2},{2,3},{4,5},{5,6},{6,7},{8,9},{9,10},{10,11},{12,13},{... | collective-permute-start | bytes 786440 | tf_op jit(solution)/shard_map/ppermute | solution.py:408
  87.6 9.0 %collective-permute-start.14 = (f32[256,256]{1,0:T(8,128)S(1)}, f32[256,256]{1,0:T(8,128)S(1)}, u32[]{:S(2)}, u32[]{:S(2)}) collective-permute-start(f32[256,256]{1,0:T(8,128)S(1)} %fill.19.source), channel_id=1, source_target_pairs={{0,1},{1,2},{2,3},{4,5},{5,6},{6,7},{8,9},{9,10},{10,11},{12,13},{... | collective-permute-start | bytes 786440 | tf_op jit(solution)/shard_map/ppermute | solution.py:408
  93.4 8.8 %collective-permute-start.18 = (f32[256,256]{1,0:T(8,128)S(1)}, f32[256,256]{1,0:T(8,128)S(1)}, u32[]{:S(2)}, u32[]{:S(2)}) collective-permute-start(f32[256,256]{1,0:T(8,128)S(1)} %fill.21.source.refs_4_), channel_id=1, source_target_pairs={{0,1},{1,2},{2,3},{4,5},{5,6},{6,7},{8,9},{9,10},{10,11},{12,13},{... | collective-permute-start | bytes 786440 | tf_op jit(solution)/shard_map/ppermute | solution.py:408
  96.7 11.2 %collective-permute-start.15 = (f32[256,256]{1,0:T(8,128)S(1)}, f32[256,256]{1,0:T(8,128)S(1)}, u32[]{:S(2)}, u32[]{:S(2)}) collective-permute-start(f32[256,256]{1,0:T(8,128)S(1)} %gate.22.source), channel_id=1, source_target_pairs={{0,1},{1,2},{2,3},{4,5},{5,6},{6,7},{8,9},{9,10},{10,11},{12,13},{... | collective-permute-start | bytes 786440 | tf_op jit(solution)/shard_map/ppermute | solution.py:408
  102.2 11.2 %collective-permute-start.19 = (f32[256,256]{1,0:T(8,128)S(1)}, f32[256,256]{1,0:T(8,128)S(1)}, u32[]{:S(2)}, u32[]{:S(2)}) collective-permute-start(f32[256,256]{1,0:T(8,128)S(1)} %gate.24.source.refs_5_), channel_id=1, source_target_pairs={{0,1},{1,2},{2,3},{4,5},{5,6},{6,7},{8,9},{9,10},{10,11},{12,13},{... | collective-permute-start | bytes 786440 | tf_op jit(solution)/shard_map/ppermute | solution.py:408
  107.8 10.2 %collective-permute-start.17 = (f32[256,256]{1,0:T(8,128)S(1)}, f32[256,256]{1,0:T(8,128)S(1)}, u32[]{:S(2)}, u32[]{:S(2)}) collective-permute-start(f32[256,256]{1,0:T(8,128)S(1)} %gate.23.source), channel_id=1, source_target_pairs={{0,1},{1,2},{2,3},{4,5},{5,6},{6,7},{8,9},{9,10},{10,11},{12,13},{... | collective-permute-start | bytes 786440 | tf_op jit(solution)/shard_map/ppermute | solution.py:408
  118.8 4.8 %collective-permute-start.20 = (f32[256,256]{1,0:T(8,128)S(1)}, f32[256,256]{1,0:T(8,128)S(1)}, u32[]{:S(2)}, u32[]{:S(2)}) collective-permute-start(f32[256,256]{1,0:T(8,128)S(1)} %get-tuple-element.116), channel_id=1, source_target_pairs={{0,4},{4,0},{8,12},{12,8},{16,20},{20,16},{24,28},{28,24},{1,5},{5... | collective-permute-start | bytes 786440 | tf_op jit(solution)/shard_map/ppermute | solution.py:379
  118.9 10.6 %collective-permute-start.24 = (f32[256,256]{1,0:T(8,128)S(1)}, f32[256,256]{1,0:T(8,128)S(1)}, u32[]{:S(2)}, u32[]{:S(2)}) collective-permute-start(f32[256,256]{1,0:T(8,128)S(1)} %gate.25.source.refs_6_), channel_id=1, source_target_pairs={{0,1},{1,2},{2,3},{4,5},{5,6},{6,7},{8,9},{9,10},{10,11},{12,13},{... | collective-permute-start | bytes 786440 | tf_op jit(solution)/shard_map/ppermute | solution.py:408
  124.2 5.3 %collective-permute-start.21 = (f32[64,256]{1,0:T(8,128)S(1)}, f32[64,256]{1,0:T(8,128)S(1)}, u32[]{:S(2)}, u32[]{:S(2)}) collective-permute-start(f32[64,256]{1,0:T(8,128)S(1)} %get-tuple-element.118), channel_id=1, source_target_pairs={{0,8},{4,12},{8,0},{12,4},{16,24},{20,28},{24,16},{28,20},{1,9},{5... | collective-permute-start | bytes 196616 | tf_op jit(solution)/shard_map/ppermute | solution.py:382
  125.7 4.9 %collective-permute-start.22 = (f32[64,256]{1,0:T(8,128)S(1)}, f32[64,256]{1,0:T(8,128)S(1)}, u32[]{:S(2)}, u32[]{:S(2)}) collective-permute-start(f32[64,256]{1,0:T(8,128)S(1)} %get-tuple-element.119), channel_id=1, source_target_pairs={{0,16},{4,20},{8,24},{12,28},{16,0},{20,4},{24,8},{28,12},{1,17},{... | collective-permute-start | bytes 196616 | tf_op jit(solution)/shard_map/ppermute | solution.py:382
  126.3 5.2 %collective-permute-start.23 = (f32[64,256]{1,0:T(8,128)S(1)}, f32[64,256]{1,0:T(8,128)S(1)}, u32[]{:S(2)}, u32[]{:S(2)}) collective-permute-start(f32[64,256]{1,0:T(8,128)S(1)} %get-tuple-element.120), channel_id=1, source_target_pairs={{0,24},{4,28},{8,16},{12,20},{16,8},{20,12},{24,0},{28,4},{1,25},{... | collective-permute-start | bytes 196616 | tf_op jit(solution)/shard_map/ppermute | solution.py:382
  (5 other events, 57.3 us)

commit v3 on v2

--- a/solution.py
+++ b/solution.py
@@ -6,8 +6,9 @@
 from jax.sharding import PartitionSpec as P
 
 PANEL = 256
-CHUNKS = 12
-LAG = 2
+CHUNKS = 16
+LAG = 3
+HALF = PANEL // 2
 BLOCK = 32
 HIGHEST = lax.Precision.HIGHEST
 F32, BF16 = jnp.float32, jnp.bfloat16
@@ -39,11 +40,11 @@
     )
 
 
-def pack(matrix):
+def pack(col, row, matrix):
     rows = matrix.shape[0] // CHUNKS
 
-    def body(source, *refs):
-        outs, sems = refs[:CHUNKS], refs[CHUNKS]
+    def body(col_ref, row_ref, source, *refs):
+        outs, sems = refs[:LAG], refs[LAG]
         copies = [
             pltpu.make_async_copy(
                 source.at[pl.ds(k * rows, rows), pl.ds(0, PANEL)], out, sems.at[k]
@@ -57,14 +58,14 @@
 
     return pl.pallas_call(
         body,
-        in_specs=[ANY],
-        out_specs=(VMEM,) * CHUNKS,
-        out_shape=(shape(rows, PANEL),) * CHUNKS,
-        scratch_shapes=[pltpu.SemaphoreType.DMA((CHUNKS,))],
-        compiler_params=params(5),
+        in_specs=[SMEM, SMEM, ANY],
+        out_specs=(VMEM,) * LAG,
+        out_shape=(shape(rows, PANEL),) * LAG,
+        scratch_shapes=[pltpu.SemaphoreType.DMA((LAG,))],
+        compiler_params=params(8),
         cost_estimate=small(),
         name="pack",
-    )(matrix)
+    )(col, row, matrix)
 
 
 def gate(x, *after):
@@ -83,12 +84,19 @@
     )(x, *after)
 
 
-def fill(place, received, own, *after):
-    def body(place_ref, _, own_ref, *refs):
-        @pl.when(place_ref[0] == 0)
+def fill(col, received, source, chunk, *after):
+    rows = received.shape[0]
+
+    def body(col_ref, _, source_ref, *refs):
+        out, sem = refs[-2:]
+
+        @pl.when(col_ref[0] == 0)
         def _():
-            source = own_ref.at[:, pl.ds(own.shape[1] - PANEL, PANEL)]
-            copy = pltpu.make_async_copy(source, refs[-2], refs[-1])
+            if chunk is None:
+                copy = pltpu.make_async_copy(source_ref, out.at[pl.ds(0, source.shape[0]), :], sem)
+            else:
+                own = source_ref.at[pl.ds(chunk * rows, rows), pl.ds(0, PANEL)]
+                copy = pltpu.make_async_copy(own, out, sem)
             copy.start()
             copy.wait()
 
@@ -102,12 +110,12 @@
         compiler_params=params(1),
         cost_estimate=small(),
         name="fill",
-    )(place, received, own, *after)
-
-
-def halve(total, place_ref, keep, give, pairs):
+    )(col, received, source, *after)
+
+
+def halve(total, row_ref, keep, give, pairs):
     size = total.shape[0] // (2 * pairs)
-    core = place_ref[1] % 2
+    core = row_ref[0] % 2
     for k in range(pairs):
         here = slice(k * size, (k + 1) * size)
         mine = pl.multiple_of((2 * k + core) * size, size)
@@ -116,11 +124,11 @@
         give[here, :] = total[pl.ds(other, size), :]
 
 
-def spread(place, keep, got, pairs):
+def spread(row, keep, got, pairs):
     size = keep.shape[0] // pairs
 
-    def body(place_ref, keep_ref, got_ref, *outs):
-        chip = place_ref[1] // 2
+    def body(row_ref, keep_ref, got_ref, *outs):
+        chip = row_ref[0] // 2
         for j, out in enumerate(outs):
             here = pl.ds(pl.multiple_of((chip ^ j) * size, size), size)
             out[...] = keep_ref[here, :] + got_ref[here, :]
@@ -133,7 +141,7 @@
         compiler_params=params(4),
         cost_estimate=small(),
         name="spread",
-    )(place, keep, got)
+    )(row, keep, got)
 
 
 def add(parts):
@@ -154,42 +162,64 @@
     )(*parts)
 
 
-def gram_part(place, chunks, pairs):
-    def body(place_ref, *refs):
-        sources, (keep, give, held) = refs[:-3], refs[-3:]
-
-        @pl.when(place_ref[0] == 0)
+def gram_part(col, row, matrix):
+    tiles = 4
+    rows = matrix.shape[0] // tiles
+
+    def body(col_ref, row_ref, source, keep, give, held, sems):
+        @pl.when(col_ref[0] == 0)
         def _():
-            total = jnp.zeros((PANEL, PANEL), F32)
-            for ref in sources:
-                x = ref[...]
-                total += dot(x, x, ((0,), (0,)), HIGHEST)
-            held[...] = total
-            halve(held, place_ref, keep, give, pairs)
-
-    return pl.pallas_call(
-        body,
-        in_specs=[SMEM] + [VMEM] * len(chunks),
+            copies = [
+                pltpu.make_async_copy(
+                    source.at[pl.ds(t * rows, rows), pl.ds(0, PANEL)], held.at[t], sems.at[t]
+                )
+                for t in range(tiles)
+            ]
+            for copy in copies:
+                copy.start()
+            square = jnp.zeros((PANEL, PANEL), F32)
+            cross = jnp.zeros((PANEL, PANEL), F32)
+            dims = ((0,), (0,))
+            for t in range(tiles):
+                copies[t].wait()
+                high, low = split(held[t])
+                square += dot(high, high, dims) + dot(low, low, dims)
+                cross += dot(high, low, dims)
+            total = square + (cross + cross.T)
+            upper = row_ref[0] % 2 == 0
+            keep[...] = jnp.where(upper, total[:HALF, :], total[HALF:, :])
+            give[...] = jnp.where(upper, total[HALF:, :], total[:HALF, :])
+
+    return pl.pallas_call(
+        body,
+        in_specs=[SMEM, SMEM, ANY],
         out_specs=(VMEM, VMEM),
-        out_shape=(shape(PANEL // 2, PANEL),) * 2,
-        scratch_shapes=[pltpu.VMEM((PANEL, PANEL), F32)],
-        compiler_params=params(8),
+        out_shape=(shape(HALF, PANEL),) * 2,
+        scratch_shapes=[
+            pltpu.VMEM((tiles, rows, PANEL), F32),
+            pltpu.SemaphoreType.DMA((tiles,)),
+        ],
+        compiler_params=params(12),
         cost_estimate=small(),
         name="gram",
-    )(place, *chunks)
-
-
-def eliminate(col, state, block):
+    )(col, row, matrix)
+
+
+def eliminate(col, row, state, block):
     first, last = block * BLOCK, (block + 1) * BLOCK
     width = 2 * PANEL
 
-    def body(col_ref, src, out):
+    def body(col_ref, row_ref, src, *rest):
+        out, packed = (rest[-2:] if last == PANEL else (rest[-1], None))
+
         @pl.when(col_ref[0] == 0)
         def _():
             if block == 0:
                 row = lax.broadcasted_iota(jnp.int32, (PANEL, PANEL), 0)
                 lane = lax.broadcasted_iota(jnp.int32, (PANEL, PANEL), 1)
-                out[:, :PANEL] = src[...]
+                upper = row_ref[0] % 2 == 0
+                out[:HALF, :PANEL] = jnp.where(upper, src[...], rest[0][...])
+                out[HALF:, :PANEL] = jnp.where(upper, rest[0][...], src[...])
                 out[:, PANEL:] = (row == lane).astype(F32)
             else:
                 out[...] = src[...]
@@ -218,7 +248,11 @@
             root = root * (1.5 - 0.5 * scale * root * root)
             rows = dot((work * root)[:, BLOCK:], out[first:last, :], ((1,), (0,)), HIGHEST)
             out[first:last, :] = rows
-            if last < PANEL:
+            if last == PANEL:
+                packed[:HALF, :] = out[HALF:, PANEL:]
+                packed[HALF:, :HALF] = out[: HALF // 2, PANEL : PANEL + HALF]
+                packed[HALF:, HALF:] = out[HALF // 2 : HALF, PANEL : PANEL + HALF]
+            else:
                 left, right = last // 128 * 128, PANEL + -(-last // 128) * 128
                 out[last:, left:right] -= dot(
                     rows[:, last:PANEL], rows[:, left:right], ((0,), (0,)), HIGHEST
@@ -226,32 +260,33 @@
 
     return pl.pallas_call(
         body,
-        in_specs=[SMEM, VMEM],
-        out_specs=VMEM,
-        out_shape=shape(PANEL, width),
-        input_output_aliases={1: 0} if block else {},
+        in_specs=[SMEM, SMEM] + [VMEM] * len(state),
+        out_specs=(VMEM, VMEM) if last == PANEL else VMEM,
+        out_shape=(shape(PANEL, width), shape(HALF + HALF // 2, PANEL))
+        if last == PANEL
+        else shape(PANEL, width),
+        input_output_aliases={2: 0} if block else {},
         compiler_params=params(8),
         cost_estimate=small(),
         name=f"eliminate{block}",
-    )(col, state)
-
-
-def consume(place, matrix, sent, step, before, pairs):
+    )(col, row, *state)
+
+
+def consume(col, row, matrix, sent, step, before, pairs):
     rows, width = sent.shape[0], matrix.shape[1]
 
-    def body(place_ref, block, source, *refs):
+    def body(col_ref, row_ref, block, source, *refs):
         if pairs:
             total, _, keep, give, halves, held, sem, turned = refs
-        elif step:
+        elif step > LAG:
             total, _, out, halves, held, sem = refs
         else:
             out, halves, held, sem = refs
-        chunk = step - LAG * place_ref[0]
-        valid = (chunk >= 0) & (chunk < CHUNKS)
-
-        def part():
+        chunk = step - LAG * col_ref[0]
+
+        def part(chunk, piece):
             here = pl.ds(pl.multiple_of(chunk * rows, rows), rows)
-            high, low = split(source[...])
+            high, low = split(piece)
             held[:, :PANEL] = high
             held[:, PANEL:] = low
             copy = pltpu.make_async_copy(held, halves.at[here, :], sem)
@@ -262,20 +297,30 @@
             copy.wait()
             return value
 
+        valid = (col_ref[0] > 0) & (chunk >= 0) & (chunk < CHUNKS)
         if pairs:
             turned[...] = total[...].T
 
             @pl.when(valid)
             def _():
-                turned[...] += part().T
-
-            halve(turned, place_ref, keep, give, pairs)
+                turned[...] += part(chunk, source[...]).T
+
+            halve(turned, row_ref, keep, give, pairs)
         else:
-            out[...] = total[...] if step else jnp.zeros_like(out)
+            out[...] = total[...] if step > LAG else jnp.zeros_like(out)
 
             @pl.when(valid)
             def _():
-                out[...] += part()
+                out[...] += part(chunk, source[...])
+
+            if step == CHUNKS + 1:
+
+                @pl.when(col_ref[0] == 0)
+                def _():
+                    @pl.loop(0, CHUNKS)
+                    def _(k):
+                        here = pl.ds(pl.multiple_of(k * rows, rows), rows)
+                        out[...] += part(k, block[here, :PANEL])
 
     halves = shape(matrix.shape[0], 2 * PANEL, dtype=BF16)
     if pairs:
@@ -284,19 +329,19 @@
         outs = (shape(PANEL, width), halves)
     return pl.pallas_call(
         body,
-        in_specs=[SMEM, VMEM, VMEM] + ([VMEM, ANY] if step else []),
+        in_specs=[SMEM, SMEM, VMEM, VMEM] + ([VMEM, ANY] if step > LAG else []),
         out_specs=(VMEM,) * (len(outs) - 1) + (ANY,),
         out_shape=outs,
-        input_output_aliases={4: len(outs) - 1} if step else {},
+        input_output_aliases={5: len(outs) - 1} if step > LAG else {},
         scratch_shapes=[pltpu.VMEM((rows, 2 * PANEL), BF16), pltpu.SemaphoreType.DMA(())]
         + ([pltpu.VMEM((width, PANEL), F32)] if pairs else []),
         compiler_params=params(16),
         cost_estimate=small(),
         name="consume",
-    )(place, matrix, sent, *before)
-
-
-def solve(place, parts, hops):
+    )(col, row, matrix, sent, *before)
+
+
+def solve(col, parts, hops):
     n, rows = len(parts), parts[0].shape[0]
 
     def body(col_ref, *refs):
@@ -305,7 +350,10 @@
 
             @pl.when(col_ref[0] == h)
             def _():
-                inverse[...] = source[...]
+                inverse[HALF:, :] = source[:HALF, :]
+                inverse[: HALF // 2, :HALF] = source[HALF : HALF + HALF // 2, :HALF]
+                inverse[HALF // 2 : HALF, :HALF] = source[HALF : HALF + HALF // 2, HALF:]
+                inverse[:HALF, HALF:] = jnp.zeros((HALF, HALF), F32)
 
         total = refs[0][...]
         for ref in refs[1:n]:
@@ -323,7 +371,7 @@
         compiler_params=params(4),
         cost_estimate=small(),
         name="solve",
-    )(place, *parts, *hops)
+    )(col, *parts, *hops)
 
 
 def subtract(matrix, halves, coeffs):
@@ -372,61 +420,67 @@
 
 
 def program(n_row, n_col):
-    shift = [(h, h + 1) for h in range(n_col - 1)]
     pairs = n_row // 2
 
-    def scatter(place, keep, give):
-        got = lax.ppermute(give, "row", [(r, r ^ 1) for r in range(n_row)])
-        parts = spread(place, keep, got, pairs)
-        return [parts[0]] + [
-            lax.ppermute(parts[j], "row", [(r, r ^ (2 * j)) for r in range(n_row)])
-            for j in range(1, pairs)
-        ]
+    def swap(x, bit):
+        return lax.ppermute(x, "row", [(r, r ^ bit) for r in range(n_row)])
+
+    def scatter(row, keep, give):
+        parts = spread(row, keep, swap(give, 1), pairs)
+        return [parts[0]] + [swap(parts[j], 2 * j) for j in range(1, pairs)]
 
     def shards(matrix):
-        place = jnp.stack([lax.axis_index("col"), lax.axis_index("row")]).astype(jnp.int32)
+        col = lax.axis_index("col").astype(jnp.int32).reshape(1)
+        row = lax.axis_index("row").astype(jnp.int32).reshape(1)
         blocks = PANEL // BLOCK
         shifts = CHUNKS + 1 + LAG * (n_col - 2)
         last = CHUNKS - 1 + LAG * (n_col - 1)
-        own = pack(matrix)
-        sent, received, sums = [], [], []
-        state = None
+        own = pack(col, row, matrix)
+        keep, give = gram_part(col, row, matrix)
+        half = add([keep, swap(give, 1)])
+        sent, received, sums = [], [], {}
+        state = packed = None
         done = 0
         for s in range(max(shifts, last + 1) + 1):
             if s < LAG:
                 sent.append(own[s])
             elif s < shifts:
-                after = [sums[s - LAG][0]] if s - LAG < len(sums) else []
-                if state is not None:
-                    after.append(state)
-                source = own[s] if s < CHUNKS else state if s == CHUNKS else None
+                after = [sums[s - 2 * LAG][0]] if s - 2 * LAG in sums else []
+                if s == LAG:
+                    after.append(half)
+                elif state is not None:
+                    after.append(state[0])
                 x = received[s - LAG]
-                sent.append(gate(x, *after) if source is None else fill(place, x, source, *after))
+                if s < CHUNKS:
+                    sent.append(fill(col, x, matrix, s, *after))
+                elif s == CHUNKS:
+                    sent.append(fill(col, x, packed, None, *after))
+                else:
+                    sent.append(gate(x, *after))
             elif s - LAG < shifts:
                 sent.append(received[s - LAG])
             if s < shifts:
-                received.append(lax.ppermute(sent[s], "col", shift))
-            if s <= last:
-                sums.append(
-                    consume(
-                        place,
-                        matrix,
-                        sent[s],
-                        s,
-                        sums[-1] if s else (),
-                        pairs if s == last else 0,
-                    )
+                hops = [(h, h + 1) for h in range(n_col - 1) if 0 <= s - LAG * h <= CHUNKS]
+                received.append(lax.ppermute(sent[s], "col", hops))
+            if LAG <= s <= last:
+                before = sums[s - 1] if s > LAG else ()
+                sums[s] = consume(
+                    col, row, matrix, sent[s], s, before, pairs if s == last else 0
                 )
-            if s == LAG - 1:
-                state = add(scatter(place, *gram_part(place, own, pairs)))
-            elif s == 2 * LAG - 1:
-                state = lax.all_gather(gate(state, received[s - LAG]), "row", axis=0, tiled=True)
-            elif s >= 2 * LAG and done < blocks:
-                state = eliminate(place, gate(state, received[s - LAG]), done)
+            if s == LAG:
+                state = [add([half] + [swap(half, 2 * j) for j in range(1, pairs)])]
+            elif s == LAG + 1:
+                mine = gate(state[0], sent[s])
+                state = [mine, swap(mine, 1)]
+            elif s > LAG + 1 and done < blocks and (s - LAG) % 4:
+                state = eliminate(col, row, [gate(state[0], sent[s]), *state[1:]], done)
                 done += 1
-        keep, give, halves = sums[-1]
-        parts = scatter(place, keep, give)
-        top_rows, coeffs = solve(place, parts, [sent[CHUNKS + LAG * h] for h in range(n_col)])
+                state = [state] if done < blocks else state
+                if done == blocks:
+                    packed = state[1]
+        keep, give, halves = sums[last]
+        parts = scatter(row, keep, give)
+        top_rows, coeffs = solve(col, parts, [sent[CHUNKS + LAG * h] for h in range(n_col)])
         coeffs = lax.all_gather(coeffs, "row", axis=0, tiled=True)
         return top_rows, subtract(matrix, halves, coeffs)
 

time: 150 us -> 125 us (0.83)
  the two profiles are of different devices: /device:TPU:0 before, /device:TPU:17 now
where the time goes in v3:
time: 125 us
  starting transfers between devices  49.9 us (40%)
  waiting for transfers between devices  36.9 us (30%)
  Pallas kernels  20.7 us (17%)
  blocking collectives  10.7 us (9%)
  local copies, waits for them, and re-layouts  4.78 us (4%)
  between operations  1.52 us (1%)
    ppermute x23, starting transfers between devices, shards(): received.append(lax.ppermute(sent[s], 'col', hops))  39.5 us
    ppermute x23, waiting for transfers between devices, shards(): received.append(lax.ppermute(sent[s], 'col', hops))  30.1 us
    pallas_call x22, Pallas kernels, consume(): pl.pallas_call(body, in_specs=[SMEM, SMEM, VMEM, VMEM] + ([VMEM, ANY] if...  13.4 us
    all_gather x1, blocking collectives, shards(): coeffs = lax.all_gather(coeffs, 'row', axis=0, tiled=True)  10.7 us
    ppermute x9, starting transfers between devices, swap(): return lax.ppermute(x, 'row', [(r, r ^ bit) for r in range(n_row)])  10.4 us
    ppermute x9, waiting for transfers between devices, swap(): return lax.ppermute(x, 'row', [(r, r ^ bit) for r in range(n_row)])  6.79 us
    pallas_call x1, Pallas kernels, subtract(): pl.pallas_call(body, in_specs=[VMEM] * 3, out_specs=ANY, out_shape=shape(...  5.48 us
    unnamed x4, local copies, waits for them, and re-layouts  4.78 us
  transfers between devices with their start and end apart: 32, of which 22 were waited for; matrix products, arithmetic and copies ran while one was open for 0% of the time, Pallas kernels for 11%

profile of v3, /device:TPU:17, one launch (start us, length us, event | category | flops | bytes accessed | tf_op | source)
XLA Modules:
  0.0 124.5 jit_solution(13021234555599526975)
XLA Ops:
  0.6 2.8 %copy-done = f32[3072,512]{1,0:T(8,128)S(1)} copy-done((f32[3072,512]{1,0:T(8,128)S(1)}, f32[3072,512]{1,0:T(8,128)}, u32[]{:S(2)}) %copy-start) | copy-done | bytes 6291480
  4.2 2.0 %copy-done.1 = f32[3072,512]{1,0:T(8,128)S(1)} copy-done((f32[3072,512]{1,0:T(8,128)S(1)}, f32[3072,512]{1,0:T(8,128)}, u32[]{:S(2)}) %copy-start.1) | copy-done | bytes 6291480
  7.7 2.2 %collective-permute-start.5 = (f32[128,256]{1,0:T(8,128)S(1)}, f32[128,256]{1,0:T(8,128)S(1)}, u32[]{:S(2)}, u32[]{:S(2)}) collective-permute-start(f32[128,256]{1,0:T(8,128)S(1)} %add.2.refs_0_), channel_id=1, source_target_pairs={{0,24},{4,28},{8,16},{12,20},{16,8},{20,12},{24,0},{28,4},{1,25},{... | collective-permute-start | bytes 393224 | tf_op jit(solution)/shard_map/ppermute | solution.py:426
  14.3 2.6 %collective-permute-done.4.refs_2_ = f32[128,256]{1,0:T(8,128)S(1)} collective-permute-done((f32[128,256]{1,0:T(8,128)S(1)}, f32[128,256]{1,0:T(8,128)S(1)}, u32[]{:S(2)}, u32[]{:S(2)}) %collective-permute-start.4) | collective-permute-done | bytes 131104 | tf_op jit(solution)/shard_map/ppermute | solution.py:426
  20.5 1.9 %collective-permute-start.9 = (f32[192,256]{1,0:T(8,128)S(1)}, f32[192,256]{1,0:T(8,128)S(1)}, u32[]{:S(2)}, u32[]{:S(2)}) collective-permute-start(f32[192,256]{1,0:T(8,128)S(1)} %fill.17.refs_1_.source), channel_id=1, source_target_pairs={{0,1},{1,2},{2,3},{4,5},{5,6},{6,7},{8,9},{9,10},{10,11},{12,13},{... | collective-permute-start | bytes 589832 | tf_op jit(solution)/shard_map/ppermute | solution.py:464
  22.4 5.4 %collective-permute-done.12._ = f32[192,256]{1,0:T(8,128)S(1)} collective-permute-done((f32[192,256]{1,0:T(8,128)S(1)}, f32[192,256]{1,0:T(8,128)S(1)}, u32[]{:S(2)}, u32[]{:S(2)}) %collective-permute-start.12) | collective-permute-done | bytes 196640 | tf_op jit(solution)/shard_map/ppermute | solution.py:464
  27.9 1.9 %collective-permute-start.13 = (f32[192,256]{1,0:T(8,128)S(1)}, f32[192,256]{1,0:T(8,128)S(1)}, u32[]{:S(2)}, u32[]{:S(2)}) collective-permute-start(f32[192,256]{1,0:T(8,128)S(1)} %fill.20.source), channel_id=1, source_target_pairs={{0,1},{1,2},{2,3},{4,5},{5,6},{6,7},{8,9},{9,10},{10,11},{12,13},{... | collective-permute-start | bytes 589832 | tf_op jit(solution)/shard_map/ppermute | solution.py:464
  30.4 1.9 %collective-permute-start.16 = (f32[192,256]{1,0:T(8,128)S(1)}, f32[192,256]{1,0:T(8,128)S(1)}, u32[]{:S(2)}, u32[]{:S(2)}) collective-permute-start(f32[192,256]{1,0:T(8,128)S(1)} %fill.18.refs_1_.source), channel_id=1, source_target_pairs={{0,1},{1,2},{2,3},{4,5},{5,6},{6,7},{8,9},{9,10},{10,11},{12,13},{... | collective-permute-start | bytes 589832 | tf_op jit(solution)/shard_map/ppermute | solution.py:464
  32.4 2.2 %collective-permute-done.9._ = f32[192,256]{1,0:T(8,128)S(1)} collective-permute-done((f32[192,256]{1,0:T(8,128)S(1)}, f32[192,256]{1,0:T(8,128)S(1)}, u32[]{:S(2)}, u32[]{:S(2)}) %collective-permute-start.9) | collective-permute-done | bytes 196640 | tf_op jit(solution)/shard_map/ppermute | solution.py:464
  34.6 1.9 %collective-permute-start.11 = (f32[192,256]{1,0:T(8,128)S(1)}, f32[192,256]{1,0:T(8,128)S(1)}, u32[]{:S(2)}, u32[]{:S(2)}) collective-permute-start(f32[192,256]{1,0:T(8,128)S(1)} %fill.19.refs_1_.source), channel_id=1, source_target_pairs={{0,1},{1,2},{2,3},{4,5},{5,6},{6,7},{8,9},{9,10},{10,11},{12,13},{... | collective-permute-start | bytes 589832 | tf_op jit(solution)/shard_map/ppermute | solution.py:464
  36.6 2.2 %collective-permute-done.13._ = f32[192,256]{1,0:T(8,128)S(1)} collective-permute-done((f32[192,256]{1,0:T(8,128)S(1)}, f32[192,256]{1,0:T(8,128)S(1)}, u32[]{:S(2)}, u32[]{:S(2)}) %collective-permute-start.13) | collective-permute-done | bytes 196640 | tf_op jit(solution)/shard_map/ppermute | solution.py:464
  38.8 1.9 %collective-permute-start.15 = (f32[192,256]{1,0:T(8,128)S(1)}, f32[192,256]{1,0:T(8,128)S(1)}, u32[]{:S(2)}, u32[]{:S(2)}) collective-permute-start(f32[192,256]{1,0:T(8,128)S(1)} %fill.21.refs_1_.source), channel_id=1, source_target_pairs={{0,1},{1,2},{2,3},{4,5},{5,6},{6,7},{8,9},{9,10},{10,11},{12,13},{... | collective-permute-start | bytes 589832 | tf_op jit(solution)/shard_map/ppermute | solution.py:464
  40.8 2.2 %collective-permute-done.16._ = f32[192,256]{1,0:T(8,128)S(1)} collective-permute-done((f32[192,256]{1,0:T(8,128)S(1)}, f32[192,256]{1,0:T(8,128)S(1)}, u32[]{:S(2)}, u32[]{:S(2)}) %collective-permute-start.16) | collective-permute-done | bytes 196640 | tf_op jit(solution)/shard_map/ppermute | solution.py:464
  43.0 1.9 %collective-permute-start.17 = (f32[192,256]{1,0:T(8,128)S(1)}, f32[192,256]{1,0:T(8,128)S(1)}, u32[]{:S(2)}, u32[]{:S(2)}) collective-permute-start(f32[192,256]{1,0:T(8,128)S(1)} %fill.24.source), channel_id=1, source_target_pairs={{0,1},{1,2},{2,3},{4,5},{5,6},{6,7},{8,9},{9,10},{10,11},{12,13},{... | collective-permute-start | bytes 589832 | tf_op jit(solution)/shard_map/ppermute | solution.py:464
  47.2 1.9 %collective-permute-start.14 = (f32[192,256]{1,0:T(8,128)S(1)}, f32[192,256]{1,0:T(8,128)S(1)}, u32[]{:S(2)}, u32[]{:S(2)}) collective-permute-start(f32[192,256]{1,0:T(8,128)S(1)} %fill.22.refs_1_.source), channel_id=1, source_target_pairs={{0,1},{1,2},{2,3},{4,5},{5,6},{6,7},{8,9},{9,10},{10,11},{12,13},{... | collective-permute-start | bytes 589832 | tf_op jit(solution)/shard_map/ppermute | solution.py:464
  52.3 1.9 %collective-permute-start.24 = (f32[192,256]{1,0:T(8,128)S(1)}, f32[192,256]{1,0:T(8,128)S(1)}, u32[]{:S(2)}, u32[]{:S(2)}) collective-permute-start(f32[192,256]{1,0:T(8,128)S(1)} %fill.23.refs_1_.source), channel_id=1, source_target_pairs={{0,1},{1,2},{2,3},{4,5},{5,6},{6,7},{8,9},{9,10},{10,11},{12,13},{... | collective-permute-start | bytes 589832 | tf_op jit(solution)/shard_map/ppermute | solution.py:464
  56.5 1.9 %collective-permute-start.21 = (f32[192,256]{1,0:T(8,128)S(1)}, f32[192,256]{1,0:T(8,128)S(1)}, u32[]{:S(2)}, u32[]{:S(2)}) collective-permute-start(f32[192,256]{1,0:T(8,128)S(1)} %fill.25.refs_1_.source), channel_id=1, source_target_pairs={{0,1},{1,2},{2,3},{4,5},{5,6},{6,7},{8,9},{9,10},{10,11},{12,13},{... | collective-permute-start | bytes 589832 | tf_op jit(solution)/shard_map/ppermute | solution.py:464
  69.4 2.3 %collective-permute-done.18.refs_0_ = f32[192,256]{1,0:T(8,128)S(1)} collective-permute-done((f32[192,256]{1,0:T(8,128)S(1)}, f32[192,256]{1,0:T(8,128)S(1)}, u32[]{:S(2)}, u32[]{:S(2)}) %collective-permute-start.18) | collective-permute-done | bytes 196640 | tf_op jit(solution)/shard_map/ppermute | solution.py:464
  81.4 2.9 %collective-permute-done.19.refs_0_ = f32[192,256]{1,0:T(8,128)S(1)} collective-permute-done((f32[192,256]{1,0:T(8,128)S(1)}, f32[192,256]{1,0:T(8,128)S(1)}, u32[]{:S(2)}, u32[]{:S(2)}) %collective-permute-start.19) | collective-permute-done | bytes 196640 | tf_op jit(solution)/shard_map/ppermute | solution.py:464
  92.7 3.6 %collective-permute-start.27 = (f32[256,256]{1,0:T(8,128)S(1)}, f32[256,256]{1,0:T(8,128)S(1)}, u32[]{:S(2)}, u32[]{:S(2)}) collective-permute-start(f32[256,256]{1,0:T(8,128)S(1)} %get-tuple-element.110), channel_id=1, source_target_pairs={{0,4},{4,0},{8,12},{12,8},{16,20},{20,16},{24,28},{28,24},{1,5},{5... | collective-permute-start | bytes 786440 | tf_op jit(solution)/shard_map/ppermute | solution.py:426
  96.2 4.2 %collective-permute-start.31 = (f32[192,256]{1,0:T(8,128)S(1)}, f32[192,256]{1,0:T(8,128)S(1)}, u32[]{:S(2)}, u32[]{:S(2)}) collective-permute-start(f32[192,256]{1,0:T(8,128)S(1)} %gate.29.source.refs_6_), channel_id=1, source_target_pairs={{2,3},{6,7},{10,11},{14,15},{18,19},{22,23},{26,27},{30,31}} | collective-permute-start | bytes 589832 | tf_op jit(solution)/shard_map/ppermute | solution.py:464
  104.9 2.1 %collective-permute-done.30.refs_3_ = f32[64,256]{1,0:T(8,128)S(1)} collective-permute-done((f32[64,256]{1,0:T(8,128)S(1)}, f32[64,256]{1,0:T(8,128)S(1)}, u32[]{:S(2)}, u32[]{:S(2)}) %collective-permute-start.30) | collective-permute-done | bytes 65568 | tf_op jit(solution)/shard_map/ppermute | solution.py:426
  108.2 10.7 %all_gather.3.c = f32[512,256]{1,0:T(8,128)S(1)} all-gather(f32[64,256]{1,0:T(8,128)S(1)} %get-tuple-element.117), channel_id=1, replica_groups=mesh['row'=8,'col'=4] {'row'}, dimensions={0}, use_global_device_ids=true | all-gather | bytes 589824 | tf_op jit(solution)/shard_map/all_gather | solution.py:484
  118.9 5.5 %subtract.1 = f32[3072,512]{1,0:T(8,128)} custom-call(f32[3072,512]{1,0:T(8,128)S(1)} %copy-done.1, bf16[3072,512]{1,0:T(8,128)(2,1)S(1)} %get-tuple-element.116.p, f32[512,256]{1,0:T(8,128)S(1)} %all_gather.3.c), custom_call_target="tpu_custom_call" | custom-call | flops 1 | bytes 1 | tf_op jit(solution)/shard_map/subtract/pallas_call | solution.py:406
  (111 shorter events, 52.8 us)
Async XLA Ops:
  7.0 9.9 %collective-permute-start.6 = (f32[192,256]{1,0:T(8,128)S(1)}, f32[192,256]{1,0:T(8,128)S(1)}, u32[]{:S(2)}, u32[]{:S(2)}) collective-permute-start(f32[192,256]{1,0:T(8,128)S(1)} %get-tuple-element.63), channel_id=1, source_target_pairs={{0,1},{4,5},{8,9},{12,13},{16,17},{20,21},{24,25},{28,29}} | collective-permute-start | bytes 589832 | tf_op jit(solution)/shard_map/ppermute | solution.py:464
  10.0 7.0 %collective-permute-start.4 = (f32[128,256]{1,0:T(8,128)S(1)}, f32[128,256]{1,0:T(8,128)S(1)}, u32[]{:S(2)}, u32[]{:S(2)}) collective-permute-start(f32[128,256]{1,0:T(8,128)S(1)} %add.2.refs_0_), channel_id=1, source_target_pairs={{0,16},{4,20},{8,24},{12,28},{16,0},{20,4},{24,8},{28,12},{1,17},{... | collective-permute-start | bytes 393224 | tf_op jit(solution)/shard_map/ppermute | solution.py:426
  10.4 8.5 %collective-permute-start.7 = (f32[192,256]{1,0:T(8,128)S(1)}, f32[192,256]{1,0:T(8,128)S(1)}, u32[]{:S(2)}, u32[]{:S(2)}) collective-permute-start(f32[192,256]{1,0:T(8,128)S(1)} %get-tuple-element.64), channel_id=1, source_target_pairs={{0,1},{4,5},{8,9},{12,13},{16,17},{20,21},{24,25},{28,29}} | collective-permute-start | bytes 589832 | tf_op jit(solution)/shard_map/ppermute | solution.py:464
  13.1 7.4 %collective-permute-start.2 = (f32[192,256]{1,0:T(8,128)S(1)}, f32[192,256]{1,0:T(8,128)S(1)}, u32[]{:S(2)}, u32[]{:S(2)}) collective-permute-start(f32[192,256]{1,0:T(8,128)S(1)} %fill.14.source), channel_id=1, source_target_pairs={{0,1},{1,2},{4,5},{5,6},{8,9},{9,10},{12,13},{13,14},{16,17},{17,1... | collective-permute-start | bytes 589832 | tf_op jit(solution)/shard_map/ppermute | solution.py:464
  17.6 10.2 %collective-permute-start.12 = (f32[192,256]{1,0:T(8,128)S(1)}, f32[192,256]{1,0:T(8,128)S(1)}, u32[]{:S(2)}, u32[]{:S(2)}) collective-permute-start(f32[192,256]{1,0:T(8,128)S(1)} %fill.15.refs_1_.source), channel_id=1, source_target_pairs={{0,1},{1,2},{4,5},{5,6},{8,9},{9,10},{12,13},{13,14},{16,17},{17,1... | collective-permute-start | bytes 589832 | tf_op jit(solution)/shard_map/ppermute | solution.py:464
  18.9 11.4 %collective-permute-start.10 = (f32[192,256]{1,0:T(8,128)S(1)}, f32[192,256]{1,0:T(8,128)S(1)}, u32[]{:S(2)}, u32[]{:S(2)}) collective-permute-start(f32[192,256]{1,0:T(8,128)S(1)} %fill.16.refs_1_.source), channel_id=1, source_target_pairs={{0,1},{1,2},{4,5},{5,6},{8,9},{9,10},{12,13},{13,14},{16,17},{17,1... | collective-permute-start | bytes 589832 | tf_op jit(solution)/shard_map/ppermute | solution.py:464
  20.5 14.1 %collective-permute-start.9 = (f32[192,256]{1,0:T(8,128)S(1)}, f32[192,256]{1,0:T(8,128)S(1)}, u32[]{:S(2)}, u32[]{:S(2)}) collective-permute-start(f32[192,256]{1,0:T(8,128)S(1)} %fill.17.refs_1_.source), channel_id=1, source_target_pairs={{0,1},{1,2},{2,3},{4,5},{5,6},{6,7},{8,9},{9,10},{10,11},{12,13},{... | collective-permute-start | bytes 589832 | tf_op jit(solution)/shard_map/ppermute | solution.py:464
  27.9 10.9 %collective-permute-start.13 = (f32[192,256]{1,0:T(8,128)S(1)}, f32[192,256]{1,0:T(8,128)S(1)}, u32[]{:S(2)}, u32[]{:S(2)}) collective-permute-start(f32[192,256]{1,0:T(8,128)S(1)} %fill.20.source), channel_id=1, source_target_pairs={{0,1},{1,2},{2,3},{4,5},{5,6},{6,7},{8,9},{9,10},{10,11},{12,13},{... | collective-permute-start | bytes 589832 | tf_op jit(solution)/shard_map/ppermute | solution.py:464
  30.4 12.6 %collective-permute-start.16 = (f32[192,256]{1,0:T(8,128)S(1)}, f32[192,256]{1,0:T(8,128)S(1)}, u32[]{:S(2)}, u32[]{:S(2)}) collective-permute-start(f32[192,256]{1,0:T(8,128)S(1)} %fill.18.refs_1_.source), channel_id=1, source_target_pairs={{0,1},{1,2},{2,3},{4,5},{5,6},{6,7},{8,9},{9,10},{10,11},{12,13},{... | collective-permute-start | bytes 589832 | tf_op jit(solution)/shard_map/ppermute | solution.py:464
  34.6 12.6 %collective-permute-start.11 = (f32[192,256]{1,0:T(8,128)S(1)}, f32[192,256]{1,0:T(8,128)S(1)}, u32[]{:S(2)}, u32[]{:S(2)}) collective-permute-start(f32[192,256]{1,0:T(8,128)S(1)} %fill.19.refs_1_.source), channel_id=1, source_target_pairs={{0,1},{1,2},{2,3},{4,5},{5,6},{6,7},{8,9},{9,10},{10,11},{12,13},{... | collective-permute-start | bytes 589832 | tf_op jit(solution)/shard_map/ppermute | solution.py:464
  38.8 12.6 %collective-permute-start.15 = (f32[192,256]{1,0:T(8,128)S(1)}, f32[192,256]{1,0:T(8,128)S(1)}, u32[]{:S(2)}, u32[]{:S(2)}) collective-permute-start(f32[192,256]{1,0:T(8,128)S(1)} %fill.21.refs_1_.source), channel_id=1, source_target_pairs={{0,1},{1,2},{2,3},{4,5},{5,6},{6,7},{8,9},{9,10},{10,11},{12,13},{... | collective-permute-start | bytes 589832 | tf_op jit(solution)/shard_map/ppermute | solution.py:464
  43.0 12.6 %collective-permute-start.17 = (f32[192,256]{1,0:T(8,128)S(1)}, f32[192,256]{1,0:T(8,128)S(1)}, u32[]{:S(2)}, u32[]{:S(2)}) collective-permute-start(f32[192,256]{1,0:T(8,128)S(1)} %fill.24.source), channel_id=1, source_target_pairs={{0,1},{1,2},{2,3},{4,5},{5,6},{6,7},{8,9},{9,10},{10,11},{12,13},{... | collective-permute-start | bytes 589832 | tf_op jit(solution)/shard_map/ppermute | solution.py:464
  47.2 12.6 %collective-permute-start.14 = (f32[192,256]{1,0:T(8,128)S(1)}, f32[192,256]{1,0:T(8,128)S(1)}, u32[]{:S(2)}, u32[]{:S(2)}) collective-permute-start(f32[192,256]{1,0:T(8,128)S(1)} %fill.22.refs_1_.source), channel_id=1, source_target_pairs={{0,1},{1,2},{2,3},{4,5},{5,6},{6,7},{8,9},{9,10},{10,11},{12,13},{... | collective-permute-start | bytes 589832 | tf_op jit(solution)/shard_map/ppermute | solution.py:464
  52.3 11.4 %collective-permute-start.24 = (f32[192,256]{1,0:T(8,128)S(1)}, f32[192,256]{1,0:T(8,128)S(1)}, u32[]{:S(2)}, u32[]{:S(2)}) collective-permute-start(f32[192,256]{1,0:T(8,128)S(1)} %fill.23.refs_1_.source), channel_id=1, source_target_pairs={{0,1},{1,2},{2,3},{4,5},{5,6},{6,7},{8,9},{9,10},{10,11},{12,13},{... | collective-permute-start | bytes 589832 | tf_op jit(solution)/shard_map/ppermute | solution.py:464
  56.5 11.0 %collective-permute-start.21 = (f32[192,256]{1,0:T(8,128)S(1)}, f32[192,256]{1,0:T(8,128)S(1)}, u32[]{:S(2)}, u32[]{:S(2)}) collective-permute-start(f32[192,256]{1,0:T(8,128)S(1)} %fill.25.refs_1_.source), channel_id=1, source_target_pairs={{0,1},{1,2},{2,3},{4,5},{5,6},{6,7},{8,9},{9,10},{10,11},{12,13},{... | collective-permute-start | bytes 589832 | tf_op jit(solution)/shard_map/ppermute | solution.py:464
  59.9 11.8 %collective-permute-start.18 = (f32[192,256]{1,0:T(8,128)S(1)}, f32[192,256]{1,0:T(8,128)S(1)}, u32[]{:S(2)}, u32[]{:S(2)}) collective-permute-start(f32[192,256]{1,0:T(8,128)S(1)} %fill.26.source), channel_id=1, source_target_pairs={{0,1},{1,2},{2,3},{4,5},{5,6},{6,7},{8,9},{9,10},{10,11},{12,13},{... | collective-permute-start | bytes 589832 | tf_op jit(solution)/shard_map/ppermute | solution.py:464
  63.7 12.2 %collective-permute-start.25 = (f32[192,256]{1,0:T(8,128)S(1)}, f32[192,256]{1,0:T(8,128)S(1)}, u32[]{:S(2)}, u32[]{:S(2)}) collective-permute-start(f32[192,256]{1,0:T(8,128)S(1)} %fill.27.source.refs_4_), channel_id=1, source_target_pairs={{0,1},{1,2},{2,3},{4,5},{5,6},{6,7},{8,9},{9,10},{10,11},{12,13},{... | collective-permute-start | bytes 589832 | tf_op jit(solution)/shard_map/ppermute | solution.py:464
  67.5 12.6 %collective-permute-start.22 = (f32[192,256]{1,0:T(8,128)S(1)}, f32[192,256]{1,0:T(8,128)S(1)}, u32[]{:S(2)}, u32[]{:S(2)}) collective-permute-start(f32[192,256]{1,0:T(8,128)S(1)} %gate.26.source), channel_id=1, source_target_pairs={{1,2},{2,3},{5,6},{6,7},{9,10},{10,11},{13,14},{14,15},{17,18},{18... | collective-permute-start | bytes 589832 | tf_op jit(solution)/shard_map/ppermute | solution.py:464
  71.7 12.6 %collective-permute-start.19 = (f32[192,256]{1,0:T(8,128)S(1)}, f32[192,256]{1,0:T(8,128)S(1)}, u32[]{:S(2)}, u32[]{:S(2)}) collective-permute-start(f32[192,256]{1,0:T(8,128)S(1)} %gate.24.source), channel_id=1, source_target_pairs={{1,2},{2,3},{5,6},{6,7},{9,10},{10,11},{13,14},{14,15},{17,18},{18... | collective-permute-start | bytes 589832 | tf_op jit(solution)/shard_map/ppermute | solution.py:464
  75.9 14.6 %collective-permute-start.26 = (f32[192,256]{1,0:T(8,128)S(1)}, f32[192,256]{1,0:T(8,128)S(1)}, u32[]{:S(2)}, u32[]{:S(2)}) collective-permute-start(f32[192,256]{1,0:T(8,128)S(1)} %gate.28.source.refs_5_), channel_id=1, source_target_pairs={{1,2},{2,3},{5,6},{6,7},{9,10},{10,11},{13,14},{14,15},{17,18},{18... | collective-permute-start | bytes 589832 | tf_op jit(solution)/shard_map/ppermute | solution.py:464
  80.1 10.5 %collective-permute-start.23 = (f32[192,256]{1,0:T(8,128)S(1)}, f32[192,256]{1,0:T(8,128)S(1)}, u32[]{:S(2)}, u32[]{:S(2)}) collective-permute-start(f32[192,256]{1,0:T(8,128)S(1)} %gate.27.source), channel_id=1, source_target_pairs={{2,3},{6,7},{10,11},{14,15},{18,19},{22,23},{26,27},{30,31}} | collective-permute-start | bytes 589832 | tf_op jit(solution)/shard_map/ppermute | solution.py:464
  84.3 8.1 %collective-permute-start.20 = (f32[192,256]{1,0:T(8,128)S(1)}, f32[192,256]{1,0:T(8,128)S(1)}, u32[]{:S(2)}, u32[]{:S(2)}) collective-permute-start(f32[192,256]{1,0:T(8,128)S(1)} %gate.25.source), channel_id=1, source_target_pairs={{2,3},{6,7},{10,11},{14,15},{18,19},{22,23},{26,27},{30,31}} | collective-permute-start | bytes 589832 | tf_op jit(solution)/shard_map/ppermute | solution.py:464
  92.7 7.8 %collective-permute-start.27 = (f32[256,256]{1,0:T(8,128)S(1)}, f32[256,256]{1,0:T(8,128)S(1)}, u32[]{:S(2)}, u32[]{:S(2)}) collective-permute-start(f32[256,256]{1,0:T(8,128)S(1)} %get-tuple-element.110), channel_id=1, source_target_pairs={{0,4},{4,0},{8,12},{12,8},{16,20},{20,16},{24,28},{28,24},{1,5},{5... | collective-permute-start | bytes 786440 | tf_op jit(solution)/shard_map/ppermute | solution.py:426
  96.2 8.5 %collective-permute-start.31 = (f32[192,256]{1,0:T(8,128)S(1)}, f32[192,256]{1,0:T(8,128)S(1)}, u32[]{:S(2)}, u32[]{:S(2)}) collective-permute-start(f32[192,256]{1,0:T(8,128)S(1)} %gate.29.source.refs_6_), channel_id=1, source_target_pairs={{2,3},{6,7},{10,11},{14,15},{18,19},{22,23},{26,27},{30,31}} | collective-permute-start | bytes 589832 | tf_op jit(solution)/shard_map/ppermute | solution.py:464
  (10 other events, 40.6 us)

commit v4 on v3

--- a/solution.py
+++ b/solution.py
@@ -40,34 +40,6 @@
     )
 
 
-def pack(col, row, matrix):
-    rows = matrix.shape[0] // CHUNKS
-
-    def body(col_ref, row_ref, source, *refs):
-        outs, sems = refs[:LAG], refs[LAG]
-        copies = [
-            pltpu.make_async_copy(
-                source.at[pl.ds(k * rows, rows), pl.ds(0, PANEL)], out, sems.at[k]
-            )
-            for k, out in enumerate(outs)
-        ]
-        for copy in copies:
-            copy.start()
-        for copy in copies:
-            copy.wait()
-
-    return pl.pallas_call(
-        body,
-        in_specs=[SMEM, SMEM, ANY],
-        out_specs=(VMEM,) * LAG,
-        out_shape=(shape(rows, PANEL),) * LAG,
-        scratch_shapes=[pltpu.SemaphoreType.DMA((LAG,))],
-        compiler_params=params(8),
-        cost_estimate=small(),
-        name="pack",
-    )(col, row, matrix)
-
-
 def gate(x, *after):
     def body(*refs):
         pass
@@ -84,19 +56,16 @@
     )(x, *after)
 
 
-def fill(col, received, source, chunk, *after):
-    rows = received.shape[0]
+def fill(col, received, source, first, *after):
+    rows = min(received.shape[0], source.shape[0] - first)
 
     def body(col_ref, _, source_ref, *refs):
         out, sem = refs[-2:]
 
         @pl.when(col_ref[0] == 0)
         def _():
-            if chunk is None:
-                copy = pltpu.make_async_copy(source_ref, out.at[pl.ds(0, source.shape[0]), :], sem)
-            else:
-                own = source_ref.at[pl.ds(chunk * rows, rows), pl.ds(0, PANEL)]
-                copy = pltpu.make_async_copy(own, out, sem)
+            own = source_ref.at[pl.ds(first, rows), pl.ds(0, PANEL)]
+            copy = pltpu.make_async_copy(own, out.at[pl.ds(0, rows), :], sem)
             copy.start()
             copy.wait()
 
@@ -163,7 +132,7 @@
 
 
 def gram_part(col, row, matrix):
-    tiles = 4
+    tiles = 8
     rows = matrix.shape[0] // tiles
 
     def body(col_ref, row_ref, source, keep, give, held, sems):
@@ -199,7 +168,7 @@
             pltpu.VMEM((tiles, rows, PANEL), F32),
             pltpu.SemaphoreType.DMA((tiles,)),
         ],
-        compiler_params=params(12),
+        compiler_params=params(55),
         cost_estimate=small(),
         name="gram",
     )(col, row, matrix)
@@ -343,18 +312,21 @@
 
 def solve(col, parts, hops):
     n, rows = len(parts), parts[0].shape[0]
+    pieces, size = len(hops[0]), hops[0][0].shape[0]
 
     def body(col_ref, *refs):
-        sources, (top, coeffs, inverse) = refs[n : n + len(hops)], refs[n + len(hops) :]
-        for h, source in enumerate(sources):
+        sources, (top, coeffs, inverse, packed) = refs[n:-4], refs[-4:]
+        for h in range(len(hops)):
 
             @pl.when(col_ref[0] == h)
             def _():
-                inverse[HALF:, :] = source[:HALF, :]
-                inverse[: HALF // 2, :HALF] = source[HALF : HALF + HALF // 2, :HALF]
-                inverse[HALF // 2 : HALF, :HALF] = source[HALF : HALF + HALF // 2, HALF:]
-                inverse[:HALF, HALF:] = jnp.zeros((HALF, HALF), F32)
-
+                for p in range(pieces):
+                    packed[p * size : (p + 1) * size, :] = sources[h * pieces + p][...]
+
+        inverse[HALF:, :] = packed[:HALF, :]
+        inverse[: HALF // 2, :HALF] = packed[HALF : HALF + HALF // 2, :HALF]
+        inverse[HALF // 2 : HALF, :HALF] = packed[HALF : HALF + HALF // 2, HALF:]
+        inverse[:HALF, HALF:] = jnp.zeros((HALF, HALF), F32)
         total = refs[0][...]
         for ref in refs[1:n]:
             total += ref[...]
@@ -364,21 +336,20 @@
 
     return pl.pallas_call(
         body,
-        in_specs=[SMEM] + [VMEM] * (n + len(hops)),
+        in_specs=[SMEM] + [VMEM] * (n + len(hops) * pieces),
         out_specs=(VMEM, VMEM),
         out_shape=(shape(rows, PANEL),) * 2,
-        scratch_shapes=[pltpu.VMEM((PANEL, PANEL), F32)],
-        compiler_params=params(4),
+        scratch_shapes=[pltpu.VMEM((PANEL, PANEL), F32), pltpu.VMEM((pieces * size, PANEL), F32)],
+        compiler_params=params(6),
         cost_estimate=small(),
         name="solve",
-    )(col, *parts, *hops)
+    )(col, *parts, *[piece for hop in hops for piece in hop])
 
 
 def subtract(matrix, halves, coeffs):
     rows, width = matrix.shape
     tiles = 12
     size = rows // tiles
-    slots = 3
 
     def body(a, p, c, out, ct, held, sems):
         ct_high, ct_low = split(c[...].T)
@@ -386,9 +357,7 @@
         ct[PANEL : 2 * PANEL, :] = ct_high
         ct[2 * PANEL :, :] = ct_low
         copies = [
-            pltpu.make_async_copy(
-                held.at[t % slots], out.at[pl.ds(t * size, size), :], sems.at[t % slots]
-            )
+            pltpu.make_async_copy(held.at[t], out.at[pl.ds(t * size, size), :], sems.at[t])
             for t in range(tiles)
         ]
         for t in range(tiles):
@@ -396,12 +365,10 @@
             both = p[here, :]
             thrice = jnp.concatenate([both, both[:, :PANEL]], axis=1)
             value = a[here, :] - dot(thrice, ct[...], ((1,), (0,)))
-            if t >= slots:
-                copies[t - slots].wait()
-            held[t % slots] = value
+            held[t] = value
             copies[t].start()
-        for t in range(tiles - slots, tiles):
-            copies[t].wait()
+        for copy in copies:
+            copy.wait()
 
     return pl.pallas_call(
         body,
@@ -410,8 +377,8 @@
         out_shape=shape(rows, width),
         scratch_shapes=[
             pltpu.VMEM((3 * PANEL, width), BF16),
-            pltpu.VMEM((slots, size, width), F32),
-            pltpu.SemaphoreType.DMA((slots,)),
+            pltpu.VMEM((tiles, size, width), F32),
+            pltpu.SemaphoreType.DMA((tiles,)),
         ],
         compiler_params=params(20),
         cost_estimate=small(),
@@ -433,34 +400,36 @@
         col = lax.axis_index("col").astype(jnp.int32).reshape(1)
         row = lax.axis_index("row").astype(jnp.int32).reshape(1)
         blocks = PANEL // BLOCK
-        shifts = CHUNKS + 1 + LAG * (n_col - 2)
+        rows = matrix.shape[0] // CHUNKS
+        pieces = -(-(HALF + HALF // 2) // rows)
+        shifts = CHUNKS + pieces + LAG * (n_col - 2)
         last = CHUNKS - 1 + LAG * (n_col - 1)
-        own = pack(col, row, matrix)
-        keep, give = gram_part(col, row, matrix)
-        half = add([keep, swap(give, 1)])
+        first = LAG + 2
+        due = [first + i * (CHUNKS - 1 - first) // (blocks - 1) for i in range(blocks)]
         sent, received, sums = [], [], {}
-        state = packed = None
-        done = 0
-        for s in range(max(shifts, last + 1) + 1):
+        half = state = packed = None
+        for s in range(shifts + LAG):
             if s < LAG:
-                sent.append(own[s])
+                sent.append(matrix[s * rows : (s + 1) * rows, :PANEL])
             elif s < shifts:
                 after = [sums[s - 2 * LAG][0]] if s - 2 * LAG in sums else []
                 if s == LAG:
+                    keep, give = gram_part(col, row, matrix)
+                    half = add([keep, swap(give, 1)])
                     after.append(half)
                 elif state is not None:
                     after.append(state[0])
                 x = received[s - LAG]
                 if s < CHUNKS:
-                    sent.append(fill(col, x, matrix, s, *after))
-                elif s == CHUNKS:
-                    sent.append(fill(col, x, packed, None, *after))
+                    sent.append(fill(col, x, matrix, s * rows, *after))
+                elif s < CHUNKS + pieces:
+                    sent.append(fill(col, x, packed, (s - CHUNKS) * rows, *after))
                 else:
                     sent.append(gate(x, *after))
-            elif s - LAG < shifts:
+            else:
                 sent.append(received[s - LAG])
             if s < shifts:
-                hops = [(h, h + 1) for h in range(n_col - 1) if 0 <= s - LAG * h <= CHUNKS]
+                hops = [(h, h + 1) for h in range(n_col - 1) if 0 <= s - LAG * h < CHUNKS + pieces]
                 received.append(lax.ppermute(sent[s], "col", hops))
             if LAG <= s <= last:
                 before = sums[s - 1] if s > LAG else ()
@@ -472,15 +441,19 @@
             elif s == LAG + 1:
                 mine = gate(state[0], sent[s])
                 state = [mine, swap(mine, 1)]
-            elif s > LAG + 1 and done < blocks and (s - LAG) % 4:
-                state = eliminate(col, row, [gate(state[0], sent[s]), *state[1:]], done)
-                done += 1
-                state = [state] if done < blocks else state
-                if done == blocks:
-                    packed = state[1]
+            elif s in due:
+                block = due.index(s)
+                state = eliminate(col, row, [gate(state[0], sent[s]), *state[1:]], block)
+                if block == blocks - 1:
+                    state, packed = [state[0]], state[1]
+                else:
+                    state = [state]
         keep, give, halves = sums[last]
         parts = scatter(row, keep, give)
-        top_rows, coeffs = solve(col, parts, [sent[CHUNKS + LAG * h] for h in range(n_col)])
+        inverse = [
+            [sent[CHUNKS + p + LAG * h] for p in range(pieces)] for h in range(n_col)
+        ]
+        top_rows, coeffs = solve(col, parts, inverse)
         coeffs = lax.all_gather(coeffs, "row", axis=0, tiled=True)
         return top_rows, subtract(matrix, halves, coeffs)
 

time: 125 us -> 120 us (0.960)
  local copies, waits for them, and re-layouts: 4.78 us -> 2.28 us
  waiting for transfers between devices: 36.9 us -> 35 us
  Pallas kernels: 20.7 us -> 19.4 us
    unnamed x4, local copies, waits for them, and re-layouts: 4.78 us -> 2.24 us
    ppermute x23, waiting for transfers between devices: 30.1 us -> 28 us  [shards(): received.append(lax.ppermute(sent[s], 'col', hops))]
    pallas_call x1, Pallas kernels: 5.48 us -> 3.68 us  [subtract(): pl.pallas_call(body, in_specs=[VMEM] * 3, out_specs=ANY, out_shape=shape(...]
  transfers between devices with their start and end apart: 32 -> 32, of which waited for: 22 -> 20; matrix products, arithmetic and copies ran while one was open for 0% -> 0% of each run, Pallas kernels for 11% -> 11%
where the time goes in v4:
time: 120 us; the launch traced here: 119 us
  starting transfers between devices  50.4 us (42%)
  waiting for transfers between devices  35 us (29%)
  Pallas kernels  19.4 us (16%)
  blocking collectives  10.7 us (9%)
  local copies, waits for them, and re-layouts  2.28 us (2%)
  between operations  1.52 us (1%)
    ppermute x23, starting transfers between devices, shards(): received.append(lax.ppermute(sent[s], 'col', hops))  39.3 us
    ppermute x23, waiting for transfers between devices, shards(): received.append(lax.ppermute(sent[s], 'col', hops))  28 us
    pallas_call x22, Pallas kernels, consume(): pl.pallas_call(body, in_specs=[SMEM, SMEM, VMEM, VMEM] + ([VMEM, ANY] if...  13.4 us
    ppermute x9, starting transfers between devices, swap(): return lax.ppermute(x, 'row', [(r, r ^ bit) for r in range(n_row)])  11.1 us
    all_gather x1, blocking collectives, shards(): coeffs = lax.all_gather(coeffs, 'row', axis=0, tiled=True)  10.7 us
    ppermute x9, waiting for transfers between devices, swap(): return lax.ppermute(x, 'row', [(r, r ^ bit) for r in range(n_row)])  7 us
    pallas_call x1, Pallas kernels, subtract(): pl.pallas_call(body, in_specs=[VMEM] * 3, out_specs=ANY, out_shape=shape(...  3.68 us
  transfers between devices with their start and end apart: 32, of which 20 were waited for; matrix products, arithmetic and copies ran while one was open for 0% of the time, Pallas kernels for 11%

profile of v4, /device:TPU:17, one launch (start us, length us, event | category | flops | bytes accessed | tf_op | source)
XLA Modules:
  0.0 119.3 jit_solution(1121655346830259310)
XLA Ops:
  5.9 2.2 %collective-permute-start.5 = (f32[128,256]{1,0:T(8,128)S(1)}, f32[128,256]{1,0:T(8,128)S(1)}, u32[]{:S(2)}, u32[]{:S(2)}) collective-permute-start(f32[128,256]{1,0:T(8,128)S(1)} %add.2.refs_0_), channel_id=1, source_target_pairs={{0,24},{4,28},{8,16},{12,20},{16,8},{20,12},{24,0},{28,4},{1,25},{... | collective-permute-start | bytes 393224 | tf_op jit(solution)/shard_map/ppermute | solution.py:393
  12.5 2.6 %collective-permute-done.4.refs_2_ = f32[128,256]{1,0:T(8,128)S(1)} collective-permute-done((f32[128,256]{1,0:T(8,128)S(1)}, f32[128,256]{1,0:T(8,128)S(1)}, u32[]{:S(2)}, u32[]{:S(2)}) %collective-permute-start.4) | collective-permute-done | bytes 131104 | tf_op jit(solution)/shard_map/ppermute | solution.py:393
  18.5 2.2 %collective-permute-start.9 = (f32[192,256]{1,0:T(8,128)S(1)}, f32[192,256]{1,0:T(8,128)S(1)}, u32[]{:S(2)}, u32[]{:S(2)}) collective-permute-start(f32[192,256]{1,0:T(8,128)S(1)} %fill.17.refs_1_.source), channel_id=1, source_target_pairs={{0,1},{1,2},{2,3},{4,5},{5,6},{6,7},{8,9},{9,10},{10,11},{12,13},{... | collective-permute-start | bytes 589832 | tf_op jit(solution)/shard_map/ppermute | solution.py:433
  20.7 4.4 %collective-permute-done.10._ = f32[192,256]{1,0:T(8,128)S(1)} collective-permute-done((f32[192,256]{1,0:T(8,128)S(1)}, f32[192,256]{1,0:T(8,128)S(1)}, u32[]{:S(2)}, u32[]{:S(2)}) %collective-permute-start.10) | collective-permute-done | bytes 196640 | tf_op jit(solution)/shard_map/ppermute | solution.py:433
  25.1 1.9 %collective-permute-start.12 = (f32[192,256]{1,0:T(8,128)S(1)}, f32[192,256]{1,0:T(8,128)S(1)}, u32[]{:S(2)}, u32[]{:S(2)}) collective-permute-start(f32[192,256]{1,0:T(8,128)S(1)} %fill.18.refs_1_.source), channel_id=1, source_target_pairs={{0,1},{1,2},{2,3},{4,5},{5,6},{6,7},{8,9},{9,10},{10,11},{12,13},{... | collective-permute-start | bytes 589832 | tf_op jit(solution)/shard_map/ppermute | solution.py:433
  27.6 1.9 %collective-permute-start.17 = (f32[192,256]{1,0:T(8,128)S(1)}, f32[192,256]{1,0:T(8,128)S(1)}, u32[]{:S(2)}, u32[]{:S(2)}) collective-permute-start(f32[192,256]{1,0:T(8,128)S(1)} %fill.22.source), channel_id=1, source_target_pairs={{0,1},{1,2},{2,3},{4,5},{5,6},{6,7},{8,9},{9,10},{10,11},{12,13},{... | collective-permute-start | bytes 589832 | tf_op jit(solution)/shard_map/ppermute | solution.py:433
  29.5 2.3 %collective-permute-done.9._ = f32[192,256]{1,0:T(8,128)S(1)} collective-permute-done((f32[192,256]{1,0:T(8,128)S(1)}, f32[192,256]{1,0:T(8,128)S(1)}, u32[]{:S(2)}, u32[]{:S(2)}) %collective-permute-start.9) | collective-permute-done | bytes 196640 | tf_op jit(solution)/shard_map/ppermute | solution.py:433
  31.8 1.9 %collective-permute-start.11 = (f32[192,256]{1,0:T(8,128)S(1)}, f32[192,256]{1,0:T(8,128)S(1)}, u32[]{:S(2)}, u32[]{:S(2)}) collective-permute-start(f32[192,256]{1,0:T(8,128)S(1)} %fill.19.refs_1_.source), channel_id=1, source_target_pairs={{0,1},{1,2},{2,3},{4,5},{5,6},{6,7},{8,9},{9,10},{10,11},{12,13},{... | collective-permute-start | bytes 589832 | tf_op jit(solution)/shard_map/ppermute | solution.py:433
  33.8 2.2 %collective-permute-done.12._ = f32[192,256]{1,0:T(8,128)S(1)} collective-permute-done((f32[192,256]{1,0:T(8,128)S(1)}, f32[192,256]{1,0:T(8,128)S(1)}, u32[]{:S(2)}, u32[]{:S(2)}) %collective-permute-start.12) | collective-permute-done | bytes 196640 | tf_op jit(solution)/shard_map/ppermute | solution.py:433
  36.0 1.9 %collective-permute-start.15 = (f32[192,256]{1,0:T(8,128)S(1)}, f32[192,256]{1,0:T(8,128)S(1)}, u32[]{:S(2)}, u32[]{:S(2)}) collective-permute-start(f32[192,256]{1,0:T(8,128)S(1)} %fill.20.refs_1_.source), channel_id=1, source_target_pairs={{0,1},{1,2},{2,3},{4,5},{5,6},{6,7},{8,9},{9,10},{10,11},{12,13},{... | collective-permute-start | bytes 589832 | tf_op jit(solution)/shard_map/ppermute | solution.py:433
  40.2 1.9 %collective-permute-start.19 = (f32[192,256]{1,0:T(8,128)S(1)}, f32[192,256]{1,0:T(8,128)S(1)}, u32[]{:S(2)}, u32[]{:S(2)}) collective-permute-start(f32[192,256]{1,0:T(8,128)S(1)} %fill.25.source), channel_id=1, source_target_pairs={{0,1},{1,2},{2,3},{4,5},{5,6},{6,7},{8,9},{9,10},{10,11},{12,13},{... | collective-permute-start | bytes 589832 | tf_op jit(solution)/shard_map/ppermute | solution.py:433
  42.2 2.3 %collective-permute-done.11._ = f32[192,256]{1,0:T(8,128)S(1)} collective-permute-done((f32[192,256]{1,0:T(8,128)S(1)}, f32[192,256]{1,0:T(8,128)S(1)}, u32[]{:S(2)}, u32[]{:S(2)}) %collective-permute-start.11) | collective-permute-done | bytes 196640 | tf_op jit(solution)/shard_map/ppermute | solution.py:433
  44.5 1.9 %collective-permute-start.13 = (f32[192,256]{1,0:T(8,128)S(1)}, f32[192,256]{1,0:T(8,128)S(1)}, u32[]{:S(2)}, u32[]{:S(2)}) collective-permute-start(f32[192,256]{1,0:T(8,128)S(1)} %fill.21.refs_1_.source), channel_id=1, source_target_pairs={{0,1},{1,2},{2,3},{4,5},{5,6},{6,7},{8,9},{9,10},{10,11},{12,13},{... | collective-permute-start | bytes 589832 | tf_op jit(solution)/shard_map/ppermute | solution.py:433
  48.7 1.9 %collective-permute-start.24 = (f32[192,256]{1,0:T(8,128)S(1)}, f32[192,256]{1,0:T(8,128)S(1)}, u32[]{:S(2)}, u32[]{:S(2)}) collective-permute-start(f32[192,256]{1,0:T(8,128)S(1)} %fill.23.refs_1_.source), channel_id=1, source_target_pairs={{0,1},{1,2},{2,3},{4,5},{5,6},{6,7},{8,9},{9,10},{10,11},{12,13},{... | collective-permute-start | bytes 589832 | tf_op jit(solution)/shard_map/ppermute | solution.py:433
  52.9 2.1 %collective-permute-start.21 = (f32[192,256]{1,0:T(8,128)S(1)}, f32[192,256]{1,0:T(8,128)S(1)}, u32[]{:S(2)}, u32[]{:S(2)}) collective-permute-start(f32[192,256]{1,0:T(8,128)S(1)} %fill.26.source), channel_id=1, source_target_pairs={{0,1},{1,2},{2,3},{4,5},{5,6},{6,7},{8,9},{9,10},{10,11},{12,13},{... | collective-permute-start | bytes 589832 | tf_op jit(solution)/shard_map/ppermute | solution.py:433
  55.0 2.1 %collective-permute-done.13._ = f32[192,256]{1,0:T(8,128)S(1)} collective-permute-done((f32[192,256]{1,0:T(8,128)S(1)}, f32[192,256]{1,0:T(8,128)S(1)}, u32[]{:S(2)}, u32[]{:S(2)}) %collective-permute-start.13) | collective-permute-done | bytes 196640 | tf_op jit(solution)/shard_map/ppermute | solution.py:433
  57.1 1.9 %collective-permute-start.16 = (f32[192,256]{1,0:T(8,128)S(1)}, f32[192,256]{1,0:T(8,128)S(1)}, u32[]{:S(2)}, u32[]{:S(2)}) collective-permute-start(f32[192,256]{1,0:T(8,128)S(1)} %fill.24.refs_1_.source), channel_id=1, source_target_pairs={{0,1},{1,2},{2,3},{4,5},{5,6},{6,7},{8,9},{9,10},{10,11},{12,13},{... | collective-permute-start | bytes 589832 | tf_op jit(solution)/shard_map/ppermute | solution.py:433
  67.4 2.3 %collective-permute-done.16.refs_0_ = f32[192,256]{1,0:T(8,128)S(1)} collective-permute-done((f32[192,256]{1,0:T(8,128)S(1)}, f32[192,256]{1,0:T(8,128)S(1)}, u32[]{:S(2)}, u32[]{:S(2)}) %collective-permute-start.16) | collective-permute-done | bytes 196640 | tf_op jit(solution)/shard_map/ppermute | solution.py:433
  79.4 2.9 %collective-permute-done.18.refs_0_ = f32[192,256]{1,0:T(8,128)S(1)} collective-permute-done((f32[192,256]{1,0:T(8,128)S(1)}, f32[192,256]{1,0:T(8,128)S(1)}, u32[]{:S(2)}, u32[]{:S(2)}) %collective-permute-start.18) | collective-permute-done | bytes 196640 | tf_op jit(solution)/shard_map/ppermute | solution.py:433
  89.0 4.3 %collective-permute-start.27 = (f32[256,256]{1,0:T(8,128)S(1)}, f32[256,256]{1,0:T(8,128)S(1)}, u32[]{:S(2)}, u32[]{:S(2)}) collective-permute-start(f32[256,256]{1,0:T(8,128)S(1)} %get-tuple-element.104), channel_id=1, source_target_pairs={{0,4},{4,0},{8,12},{12,8},{16,20},{20,16},{24,28},{28,24},{1,5},{5... | collective-permute-start | bytes 786440 | tf_op jit(solution)/shard_map/ppermute | solution.py:393
  93.3 3.5 %collective-permute-start.31 = (f32[192,256]{1,0:T(8,128)S(1)}, f32[192,256]{1,0:T(8,128)S(1)}, u32[]{:S(2)}, u32[]{:S(2)}) collective-permute-start(f32[192,256]{1,0:T(8,128)S(1)} %gate.29.source.refs_6_), channel_id=1, source_target_pairs={{2,3},{6,7},{10,11},{14,15},{18,19},{22,23},{26,27},{30,31}} | collective-permute-start | bytes 589832 | tf_op jit(solution)/shard_map/ppermute | solution.py:433
  101.5 2.1 %collective-permute-done.30.refs_3_ = f32[64,256]{1,0:T(8,128)S(1)} collective-permute-done((f32[64,256]{1,0:T(8,128)S(1)}, f32[64,256]{1,0:T(8,128)S(1)}, u32[]{:S(2)}, u32[]{:S(2)}) %collective-permute-start.30) | collective-permute-done | bytes 65568 | tf_op jit(solution)/shard_map/ppermute | solution.py:393
  104.8 10.7 %all_gather.3.c = f32[512,256]{1,0:T(8,128)S(1)} all-gather(f32[64,256]{1,0:T(8,128)S(1)} %get-tuple-element.111), channel_id=1, replica_groups=mesh['row'=8,'col'=4] {'row'}, dimensions={0}, use_global_device_ids=true | all-gather | bytes 589824 | tf_op jit(solution)/shard_map/all_gather | solution.py:457
  115.5 3.7 %subtract.1 = f32[3072,512]{1,0:T(8,128)} custom-call(f32[3072,512]{1,0:T(8,128)S(1)} %copy-done, bf16[3072,512]{1,0:T(8,128)(2,1)S(1)} %get-tuple-element.110.p, f32[512,256]{1,0:T(8,128)S(1)} %all_gather.3.c), custom_call_target="tpu_custom_call" | custom-call | flops 1 | bytes 1 | tf_op jit(solution)/shard_map/subtract/pallas_call | solution.py:373
  (111 shorter events, 50.5 us)
Async XLA Ops:
  4.2 10.9 %collective-permute-start.6 = (f32[192,256]{1,0:T(8,128)S(1)}, f32[192,256]{1,0:T(8,128)S(1)}, u32[]{:S(2)}, u32[]{:S(2)}) collective-permute-start(f32[192,256]{1,0:T(8,128)S(1)} %get-tuple-element.113), channel_id=1, source_target_pairs={{0,1},{4,5},{8,9},{12,13},{16,17},{20,21},{24,25},{28,29}} | collective-permute-start | bytes 589832 | tf_op jit(solution)/shard_map/ppermute | solution.py:433
  8.1 7.0 %collective-permute-start.4 = (f32[128,256]{1,0:T(8,128)S(1)}, f32[128,256]{1,0:T(8,128)S(1)}, u32[]{:S(2)}, u32[]{:S(2)}) collective-permute-start(f32[128,256]{1,0:T(8,128)S(1)} %add.2.refs_0_), channel_id=1, source_target_pairs={{0,16},{4,20},{8,24},{12,28},{16,0},{20,4},{24,8},{28,12},{1,17},{... | collective-permute-start | bytes 393224 | tf_op jit(solution)/shard_map/ppermute | solution.py:393
  8.3 6.7 %collective-permute-start.3 = (f32[128,256]{1,0:T(8,128)S(1)}, f32[128,256]{1,0:T(8,128)S(1)}, u32[]{:S(2)}, u32[]{:S(2)}) collective-permute-start(f32[128,256]{1,0:T(8,128)S(1)} %add.2.refs_0_), channel_id=1, source_target_pairs={{0,8},{4,12},{8,0},{12,4},{16,24},{20,28},{24,16},{28,20},{1,9},{5... | collective-permute-start | bytes 393224 | tf_op jit(solution)/shard_map/ppermute | solution.py:393
  8.6 8.5 %collective-permute-start.7 = (f32[192,256]{1,0:T(8,128)S(1)}, f32[192,256]{1,0:T(8,128)S(1)}, u32[]{:S(2)}, u32[]{:S(2)}) collective-permute-start(f32[192,256]{1,0:T(8,128)S(1)} %get-tuple-element.112), channel_id=1, source_target_pairs={{0,1},{4,5},{8,9},{12,13},{16,17},{20,21},{24,25},{28,29}} | collective-permute-start | bytes 589832 | tf_op jit(solution)/shard_map/ppermute | solution.py:433
  11.2 7.2 %collective-permute-start.2 = (f32[192,256]{1,0:T(8,128)S(1)}, f32[192,256]{1,0:T(8,128)S(1)}, u32[]{:S(2)}, u32[]{:S(2)}) collective-permute-start(f32[192,256]{1,0:T(8,128)S(1)} %fill.14.source), channel_id=1, source_target_pairs={{0,1},{1,2},{4,5},{5,6},{8,9},{9,10},{12,13},{13,14},{16,17},{17,1... | collective-permute-start | bytes 589832 | tf_op jit(solution)/shard_map/ppermute | solution.py:433
  15.8 9.3 %collective-permute-start.10 = (f32[192,256]{1,0:T(8,128)S(1)}, f32[192,256]{1,0:T(8,128)S(1)}, u32[]{:S(2)}, u32[]{:S(2)}) collective-permute-start(f32[192,256]{1,0:T(8,128)S(1)} %fill.15.refs_1_.source), channel_id=1, source_target_pairs={{0,1},{1,2},{4,5},{5,6},{8,9},{9,10},{12,13},{13,14},{16,17},{17,1... | collective-permute-start | bytes 589832 | tf_op jit(solution)/shard_map/ppermute | solution.py:433
  17.1 10.5 %collective-permute-start.14 = (f32[192,256]{1,0:T(8,128)S(1)}, f32[192,256]{1,0:T(8,128)S(1)}, u32[]{:S(2)}, u32[]{:S(2)}) collective-permute-start(f32[192,256]{1,0:T(8,128)S(1)} %fill.16.refs_1_.source), channel_id=1, source_target_pairs={{0,1},{1,2},{4,5},{5,6},{8,9},{9,10},{12,13},{13,14},{16,17},{17,1... | collective-permute-start | bytes 589832 | tf_op jit(solution)/shard_map/ppermute | solution.py:433
  18.5 13.3 %collective-permute-start.9 = (f32[192,256]{1,0:T(8,128)S(1)}, f32[192,256]{1,0:T(8,128)S(1)}, u32[]{:S(2)}, u32[]{:S(2)}) collective-permute-start(f32[192,256]{1,0:T(8,128)S(1)} %fill.17.refs_1_.source), channel_id=1, source_target_pairs={{0,1},{1,2},{2,3},{4,5},{5,6},{6,7},{8,9},{9,10},{10,11},{12,13},{... | collective-permute-start | bytes 589832 | tf_op jit(solution)/shard_map/ppermute | solution.py:433
  25.1 10.9 %collective-permute-start.12 = (f32[192,256]{1,0:T(8,128)S(1)}, f32[192,256]{1,0:T(8,128)S(1)}, u32[]{:S(2)}, u32[]{:S(2)}) collective-permute-start(f32[192,256]{1,0:T(8,128)S(1)} %fill.18.refs_1_.source), channel_id=1, source_target_pairs={{0,1},{1,2},{2,3},{4,5},{5,6},{6,7},{8,9},{9,10},{10,11},{12,13},{... | collective-permute-start | bytes 589832 | tf_op jit(solution)/shard_map/ppermute | solution.py:433
  27.6 12.6 %collective-permute-start.17 = (f32[192,256]{1,0:T(8,128)S(1)}, f32[192,256]{1,0:T(8,128)S(1)}, u32[]{:S(2)}, u32[]{:S(2)}) collective-permute-start(f32[192,256]{1,0:T(8,128)S(1)} %fill.22.source), channel_id=1, source_target_pairs={{0,1},{1,2},{2,3},{4,5},{5,6},{6,7},{8,9},{9,10},{10,11},{12,13},{... | collective-permute-start | bytes 589832 | tf_op jit(solution)/shard_map/ppermute | solution.py:433
  31.8 12.6 %collective-permute-start.11 = (f32[192,256]{1,0:T(8,128)S(1)}, f32[192,256]{1,0:T(8,128)S(1)}, u32[]{:S(2)}, u32[]{:S(2)}) collective-permute-start(f32[192,256]{1,0:T(8,128)S(1)} %fill.19.refs_1_.source), channel_id=1, source_target_pairs={{0,1},{1,2},{2,3},{4,5},{5,6},{6,7},{8,9},{9,10},{10,11},{12,13},{... | collective-permute-start | bytes 589832 | tf_op jit(solution)/shard_map/ppermute | solution.py:433
  36.0 12.6 %collective-permute-start.15 = (f32[192,256]{1,0:T(8,128)S(1)}, f32[192,256]{1,0:T(8,128)S(1)}, u32[]{:S(2)}, u32[]{:S(2)}) collective-permute-start(f32[192,256]{1,0:T(8,128)S(1)} %fill.20.refs_1_.source), channel_id=1, source_target_pairs={{0,1},{1,2},{2,3},{4,5},{5,6},{6,7},{8,9},{9,10},{10,11},{12,13},{... | collective-permute-start | bytes 589832 | tf_op jit(solution)/shard_map/ppermute | solution.py:433
  40.2 12.6 %collective-permute-start.19 = (f32[192,256]{1,0:T(8,128)S(1)}, f32[192,256]{1,0:T(8,128)S(1)}, u32[]{:S(2)}, u32[]{:S(2)}) collective-permute-start(f32[192,256]{1,0:T(8,128)S(1)} %fill.25.source), channel_id=1, source_target_pairs={{0,1},{1,2},{2,3},{4,5},{5,6},{6,7},{8,9},{9,10},{10,11},{12,13},{... | collective-permute-start | bytes 589832 | tf_op jit(solution)/shard_map/ppermute | solution.py:433
  44.5 12.6 %collective-permute-start.13 = (f32[192,256]{1,0:T(8,128)S(1)}, f32[192,256]{1,0:T(8,128)S(1)}, u32[]{:S(2)}, u32[]{:S(2)}) collective-permute-start(f32[192,256]{1,0:T(8,128)S(1)} %fill.21.refs_1_.source), channel_id=1, source_target_pairs={{0,1},{1,2},{2,3},{4,5},{5,6},{6,7},{8,9},{9,10},{10,11},{12,13},{... | collective-permute-start | bytes 589832 | tf_op jit(solution)/shard_map/ppermute | solution.py:433
  48.7 12.6 %collective-permute-start.24 = (f32[192,256]{1,0:T(8,128)S(1)}, f32[192,256]{1,0:T(8,128)S(1)}, u32[]{:S(2)}, u32[]{:S(2)}) collective-permute-start(f32[192,256]{1,0:T(8,128)S(1)} %fill.23.refs_1_.source), channel_id=1, source_target_pairs={{0,1},{1,2},{2,3},{4,5},{5,6},{6,7},{8,9},{9,10},{10,11},{12,13},{... | collective-permute-start | bytes 589832 | tf_op jit(solution)/shard_map/ppermute | solution.py:433
  52.9 12.6 %collective-permute-start.21 = (f32[192,256]{1,0:T(8,128)S(1)}, f32[192,256]{1,0:T(8,128)S(1)}, u32[]{:S(2)}, u32[]{:S(2)}) collective-permute-start(f32[192,256]{1,0:T(8,128)S(1)} %fill.26.source), channel_id=1, source_target_pairs={{0,1},{1,2},{2,3},{4,5},{5,6},{6,7},{8,9},{9,10},{10,11},{12,13},{... | collective-permute-start | bytes 589832 | tf_op jit(solution)/shard_map/ppermute | solution.py:433
  57.1 12.6 %collective-permute-start.16 = (f32[192,256]{1,0:T(8,128)S(1)}, f32[192,256]{1,0:T(8,128)S(1)}, u32[]{:S(2)}, u32[]{:S(2)}) collective-permute-start(f32[192,256]{1,0:T(8,128)S(1)} %fill.24.refs_1_.source), channel_id=1, source_target_pairs={{0,1},{1,2},{2,3},{4,5},{5,6},{6,7},{8,9},{9,10},{10,11},{12,13},{... | collective-permute-start | bytes 589832 | tf_op jit(solution)/shard_map/ppermute | solution.py:433
  61.3 12.6 %collective-permute-start.25 = (f32[192,256]{1,0:T(8,128)S(1)}, f32[192,256]{1,0:T(8,128)S(1)}, u32[]{:S(2)}, u32[]{:S(2)}) collective-permute-start(f32[192,256]{1,0:T(8,128)S(1)} %fill.27.source.refs_4_), channel_id=1, source_target_pairs={{0,1},{1,2},{2,3},{4,5},{5,6},{6,7},{8,9},{9,10},{10,11},{12,13},{... | collective-permute-start | bytes 589832 | tf_op jit(solution)/shard_map/ppermute | solution.py:433
  65.5 12.6 %collective-permute-start.22 = (f32[192,256]{1,0:T(8,128)S(1)}, f32[192,256]{1,0:T(8,128)S(1)}, u32[]{:S(2)}, u32[]{:S(2)}) collective-permute-start(f32[192,256]{1,0:T(8,128)S(1)} %gate.26.source), channel_id=1, source_target_pairs={{1,2},{2,3},{5,6},{6,7},{9,10},{10,11},{13,14},{14,15},{17,18},{18... | collective-permute-start | bytes 589832 | tf_op jit(solution)/shard_map/ppermute | solution.py:433
  69.7 12.6 %collective-permute-start.18 = (f32[192,256]{1,0:T(8,128)S(1)}, f32[192,256]{1,0:T(8,128)S(1)}, u32[]{:S(2)}, u32[]{:S(2)}) collective-permute-start(f32[192,256]{1,0:T(8,128)S(1)} %gate.24.source), channel_id=1, source_target_pairs={{1,2},{2,3},{5,6},{6,7},{9,10},{10,11},{13,14},{14,15},{17,18},{18... | collective-permute-start | bytes 589832 | tf_op jit(solution)/shard_map/ppermute | solution.py:433
  73.9 14.6 %collective-permute-start.26 = (f32[192,256]{1,0:T(8,128)S(1)}, f32[192,256]{1,0:T(8,128)S(1)}, u32[]{:S(2)}, u32[]{:S(2)}) collective-permute-start(f32[192,256]{1,0:T(8,128)S(1)} %gate.28.source.refs_5_), channel_id=1, source_target_pairs={{1,2},{2,3},{5,6},{6,7},{9,10},{10,11},{13,14},{14,15},{17,18},{18... | collective-permute-start | bytes 589832 | tf_op jit(solution)/shard_map/ppermute | solution.py:433
  78.1 10.5 %collective-permute-start.23 = (f32[192,256]{1,0:T(8,128)S(1)}, f32[192,256]{1,0:T(8,128)S(1)}, u32[]{:S(2)}, u32[]{:S(2)}) collective-permute-start(f32[192,256]{1,0:T(8,128)S(1)} %gate.27.source), channel_id=1, source_target_pairs={{2,3},{6,7},{10,11},{14,15},{18,19},{22,23},{26,27},{30,31}} | collective-permute-start | bytes 589832 | tf_op jit(solution)/shard_map/ppermute | solution.py:433
  89.0 7.9 %collective-permute-start.27 = (f32[256,256]{1,0:T(8,128)S(1)}, f32[256,256]{1,0:T(8,128)S(1)}, u32[]{:S(2)}, u32[]{:S(2)}) collective-permute-start(f32[256,256]{1,0:T(8,128)S(1)} %get-tuple-element.104), channel_id=1, source_target_pairs={{0,4},{4,0},{8,12},{12,8},{16,20},{20,16},{24,28},{28,24},{1,5},{5... | collective-permute-start | bytes 786440 | tf_op jit(solution)/shard_map/ppermute | solution.py:393
  93.3 7.8 %collective-permute-start.31 = (f32[192,256]{1,0:T(8,128)S(1)}, f32[192,256]{1,0:T(8,128)S(1)}, u32[]{:S(2)}, u32[]{:S(2)}) collective-permute-start(f32[192,256]{1,0:T(8,128)S(1)} %gate.29.source.refs_6_), channel_id=1, source_target_pairs={{2,3},{6,7},{10,11},{14,15},{18,19},{22,23},{26,27},{30,31}} | collective-permute-start | bytes 589832 | tf_op jit(solution)/shard_map/ppermute | solution.py:433
  (10 other events, 37.3 us)

commit v5 on v4

--- a/solution.py
+++ b/solution.py
@@ -9,6 +9,7 @@
 CHUNKS = 16
 LAG = 3
 HALF = PANEL // 2
+OWN = 4
 BLOCK = 32
 HIGHEST = lax.Precision.HIGHEST
 F32, BF16 = jnp.float32, jnp.bfloat16
@@ -253,12 +254,13 @@
             out, halves, held, sem = refs
         chunk = step - LAG * col_ref[0]
 
-        def part(chunk, piece):
-            here = pl.ds(pl.multiple_of(chunk * rows, rows), rows)
+        def part(first, piece):
+            count = piece.shape[0]
+            here = pl.ds(pl.multiple_of(first, rows), count)
             high, low = split(piece)
-            held[:, :PANEL] = high
-            held[:, PANEL:] = low
-            copy = pltpu.make_async_copy(held, halves.at[here, :], sem)
+            held[:count, :PANEL] = high
+            held[:count, PANEL:] = low
+            copy = pltpu.make_async_copy(held.at[pl.ds(0, count), :], halves.at[here, :], sem)
             copy.start()
             a_high, a_low = split(block[here, :])
             dims = ((0,), (0,))
@@ -272,7 +274,7 @@
 
             @pl.when(valid)
             def _():
-                turned[...] += part(chunk, source[...]).T
+                turned[...] += part(chunk * rows, source[...]).T
 
             halve(turned, row_ref, keep, give, pairs)
         else:
@@ -280,16 +282,18 @@
 
             @pl.when(valid)
             def _():
-                out[...] += part(chunk, source[...])
+                out[...] += part(chunk * rows, source[...])
 
             if step == CHUNKS + 1:
 
                 @pl.when(col_ref[0] == 0)
                 def _():
-                    @pl.loop(0, CHUNKS)
+                    size = OWN * rows
+
+                    @pl.loop(0, CHUNKS // OWN)
                     def _(k):
-                        here = pl.ds(pl.multiple_of(k * rows, rows), rows)
-                        out[...] += part(k, block[here, :PANEL])
+                        here = pl.ds(pl.multiple_of(k * size, size), size)
+                        out[...] += part(k * size, block[here, :PANEL])
 
     halves = shape(matrix.shape[0], 2 * PANEL, dtype=BF16)
     if pairs:
@@ -302,7 +306,10 @@
         out_specs=(VMEM,) * (len(outs) - 1) + (ANY,),
         out_shape=outs,
         input_output_aliases={5: len(outs) - 1} if step > LAG else {},
-        scratch_shapes=[pltpu.VMEM((rows, 2 * PANEL), BF16), pltpu.SemaphoreType.DMA(())]
+        scratch_shapes=[
+            pltpu.VMEM((OWN * rows if step == CHUNKS + 1 else rows, 2 * PANEL), BF16),
+            pltpu.SemaphoreType.DMA(()),
+        ]
         + ([pltpu.VMEM((width, PANEL), F32)] if pairs else []),
         compiler_params=params(16),
         cost_estimate=small(),
@@ -394,7 +401,7 @@
 
     def scatter(row, keep, give):
         parts = spread(row, keep, swap(give, 1), pairs)
-        return [parts[0]] + [swap(parts[j], 2 * j) for j in range(1, pairs)]
+        return [parts[0]] + [swap(parts[j], 2 * j) for j in reversed(range(1, pairs))]
 
     def shards(matrix):
         col = lax.axis_index("col").astype(jnp.int32).reshape(1)
@@ -404,7 +411,7 @@
         pieces = -(-(HALF + HALF // 2) // rows)
         shifts = CHUNKS + pieces + LAG * (n_col - 2)
         last = CHUNKS - 1 + LAG * (n_col - 1)
-        first = LAG + 2
+        first = LAG + 3
         due = [first + i * (CHUNKS - 1 - first) // (blocks - 1) for i in range(blocks)]
         sent, received, sums = [], [], {}
         half = state = packed = None
@@ -416,7 +423,6 @@
                 if s == LAG:
                     keep, give = gram_part(col, row, matrix)
                     half = add([keep, swap(give, 1)])
-                    after.append(half)
                 elif state is not None:
                     after.append(state[0])
                 x = received[s - LAG]
@@ -436,9 +442,10 @@
                 sums[s] = consume(
                     col, row, matrix, sent[s], s, before, pairs if s == last else 0
                 )
-            if s == LAG:
+            if s == LAG + 1:
+                half = gate(half, sent[LAG])
                 state = [add([half] + [swap(half, 2 * j) for j in range(1, pairs)])]
-            elif s == LAG + 1:
+            elif s == LAG + 2:
                 mine = gate(state[0], sent[s])
                 state = [mine, swap(mine, 1)]
             elif s in due:

time: 120 us -> 119 us (level)
    unnamed x4, local copies, waits for them, and re-layouts: 2.24 us -> 0.53 us
    ppermute x23, waiting for transfers between devices: 28 us -> 26.7 us  [shards(): received.append(lax.ppermute(sent[s], 'col', hops))]
  transfers between devices with their start and end apart: 32 -> 32, of which waited for: 20 -> 21; matrix products, arithmetic and copies ran while one was open for 0% -> 0% of each run, Pallas kernels for 11% -> 12%
where the time goes in v5:
time: 119 us
  starting transfers between devices  50.1 us (42%)
  waiting for transfers between devices  34.4 us (29%)
  Pallas kernels  19.3 us (16%)
  blocking collectives  11.7 us (10%)
  local copies, waits for them, and re-layouts  1.69 us (1%)
  between operations  1.51 us (1%)
    ppermute x23, starting transfers between devices, shards(): received.append(lax.ppermute(sent[s], 'col', hops))  39.8 us
    ppermute x23, waiting for transfers between devices, shards(): received.append(lax.ppermute(sent[s], 'col', hops))  26.7 us
    pallas_call x22, Pallas kernels, consume(): pl.pallas_call(body, in_specs=[SMEM, SMEM, VMEM, VMEM] + ([VMEM, ANY] if...  13.4 us
    all_gather x1, blocking collectives, shards(): coeffs = lax.all_gather(coeffs, 'row', axis=0, tiled=True)  11.7 us
    ppermute x9, starting transfers between devices, swap(): return lax.ppermute(x, 'row', [(r, r ^ bit) for r in range(n_row)])  10.3 us
    ppermute x9, waiting for transfers between devices, swap(): return lax.ppermute(x, 'row', [(r, r ^ bit) for r in range(n_row)])  7.66 us
    pallas_call x1, Pallas kernels, subtract(): pl.pallas_call(body, in_specs=[VMEM] * 3, out_specs=ANY, out_shape=shape(...  3.68 us
  transfers between devices with their start and end apart: 32, of which 21 were waited for; matrix products, arithmetic and copies ran while one was open for 0% of the time, Pallas kernels for 12%

profile of v5, /device:TPU:17, one launch (start us, length us, event | category | flops | bytes accessed | tf_op | source)
XLA Modules:
  0.0 118.7 jit_solution(10919501180634151184)
XLA Ops:
  7.4 2.2 %collective-permute-start.5 = (f32[128,256]{1,0:T(8,128)S(1)}, f32[128,256]{1,0:T(8,128)S(1)}, u32[]{:S(2)}, u32[]{:S(2)}) collective-permute-start(f32[128,256]{1,0:T(8,128)S(1)} %gate.16.refs_0_), channel_id=1, source_target_pairs={{0,24},{4,28},{8,16},{12,20},{16,8},{20,12},{24,0},{28,4},{1,25},{... | collective-permute-start | bytes 393224 | tf_op jit(solution)/shard_map/ppermute | solution.py:400
  10.1 2.6 %collective-permute-done.5.refs_3_ = f32[128,256]{1,0:T(8,128)S(1)} collective-permute-done((f32[128,256]{1,0:T(8,128)S(1)}, f32[128,256]{1,0:T(8,128)S(1)}, u32[]{:S(2)}, u32[]{:S(2)}) %collective-permute-start.5) | collective-permute-done | bytes 131104 | tf_op jit(solution)/shard_map/ppermute | solution.py:400
  14.0 2.6 %collective-permute-done.4.refs_2_ = f32[128,256]{1,0:T(8,128)S(1)} collective-permute-done((f32[128,256]{1,0:T(8,128)S(1)}, f32[128,256]{1,0:T(8,128)S(1)}, u32[]{:S(2)}, u32[]{:S(2)}) %collective-permute-start.4) | collective-permute-done | bytes 131104 | tf_op jit(solution)/shard_map/ppermute | solution.py:400
  18.0 2.0 %collective-permute-start.7 = (f32[192,256]{1,0:T(8,128)S(1)}, f32[192,256]{1,0:T(8,128)S(1)}, u32[]{:S(2)}, u32[]{:S(2)}) collective-permute-start(f32[192,256]{1,0:T(8,128)S(1)} %fill.16.refs_1_.source), channel_id=1, source_target_pairs={{0,1},{1,2},{2,3},{4,5},{5,6},{6,7},{8,9},{9,10},{10,11},{12,13},{... | collective-permute-start | bytes 589832 | tf_op jit(solution)/shard_map/ppermute | solution.py:439
  21.9 1.9 %collective-permute-start.15 = (f32[192,256]{1,0:T(8,128)S(1)}, f32[192,256]{1,0:T(8,128)S(1)}, u32[]{:S(2)}, u32[]{:S(2)}) collective-permute-start(f32[192,256]{1,0:T(8,128)S(1)} %fill.18.refs_1_.source), channel_id=1, source_target_pairs={{0,1},{1,2},{2,3},{4,5},{5,6},{6,7},{8,9},{9,10},{10,11},{12,13},{... | collective-permute-start | bytes 589832 | tf_op jit(solution)/shard_map/ppermute | solution.py:439
  24.6 1.9 %collective-permute-start.13 = (f32[192,256]{1,0:T(8,128)S(1)}, f32[192,256]{1,0:T(8,128)S(1)}, u32[]{:S(2)}, u32[]{:S(2)}) collective-permute-start(f32[192,256]{1,0:T(8,128)S(1)} %fill.19.refs_1_.source), channel_id=1, source_target_pairs={{0,1},{1,2},{2,3},{4,5},{5,6},{6,7},{8,9},{9,10},{10,11},{12,13},{... | collective-permute-start | bytes 589832 | tf_op jit(solution)/shard_map/ppermute | solution.py:439
  26.7 4.2 %collective-permute-done.7._ = f32[192,256]{1,0:T(8,128)S(1)} collective-permute-done((f32[192,256]{1,0:T(8,128)S(1)}, f32[192,256]{1,0:T(8,128)S(1)}, u32[]{:S(2)}, u32[]{:S(2)}) %collective-permute-start.7) | collective-permute-done | bytes 196640 | tf_op jit(solution)/shard_map/ppermute | solution.py:439
  30.9 1.9 %collective-permute-start.12 = (f32[192,256]{1,0:T(8,128)S(1)}, f32[192,256]{1,0:T(8,128)S(1)}, u32[]{:S(2)}, u32[]{:S(2)}) collective-permute-start(f32[192,256]{1,0:T(8,128)S(1)} %fill.20.refs_1_.source), channel_id=1, source_target_pairs={{0,1},{1,2},{2,3},{4,5},{5,6},{6,7},{8,9},{9,10},{10,11},{12,13},{... | collective-permute-start | bytes 589832 | tf_op jit(solution)/shard_map/ppermute | solution.py:439
  32.9 2.5 %collective-permute-done.15._ = f32[192,256]{1,0:T(8,128)S(1)} collective-permute-done((f32[192,256]{1,0:T(8,128)S(1)}, f32[192,256]{1,0:T(8,128)S(1)}, u32[]{:S(2)}, u32[]{:S(2)}) %collective-permute-start.15) | collective-permute-done | bytes 196640 | tf_op jit(solution)/shard_map/ppermute | solution.py:439
  35.5 1.9 %collective-permute-start.16 = (f32[192,256]{1,0:T(8,128)S(1)}, f32[192,256]{1,0:T(8,128)S(1)}, u32[]{:S(2)}, u32[]{:S(2)}) collective-permute-start(f32[192,256]{1,0:T(8,128)S(1)} %fill.23.source), channel_id=1, source_target_pairs={{0,1},{1,2},{2,3},{4,5},{5,6},{6,7},{8,9},{9,10},{10,11},{12,13},{... | collective-permute-start | bytes 589832 | tf_op jit(solution)/shard_map/ppermute | solution.py:439
  37.4 2.2 %collective-permute-done.13._ = f32[192,256]{1,0:T(8,128)S(1)} collective-permute-done((f32[192,256]{1,0:T(8,128)S(1)}, f32[192,256]{1,0:T(8,128)S(1)}, u32[]{:S(2)}, u32[]{:S(2)}) %collective-permute-start.13) | collective-permute-done | bytes 196640 | tf_op jit(solution)/shard_map/ppermute | solution.py:439
  40.5 1.9 %collective-permute-start.19 = (f32[192,256]{1,0:T(8,128)S(1)}, f32[192,256]{1,0:T(8,128)S(1)}, u32[]{:S(2)}, u32[]{:S(2)}) collective-permute-start(f32[192,256]{1,0:T(8,128)S(1)} %fill.21.refs_1_.source), channel_id=1, source_target_pairs={{0,1},{1,2},{2,3},{4,5},{5,6},{6,7},{8,9},{9,10},{10,11},{12,13},{... | collective-permute-start | bytes 589832 | tf_op jit(solution)/shard_map/ppermute | solution.py:439
  43.9 1.9 %collective-permute-start.14 = (f32[192,256]{1,0:T(8,128)S(1)}, f32[192,256]{1,0:T(8,128)S(1)}, u32[]{:S(2)}, u32[]{:S(2)}) collective-permute-start(f32[192,256]{1,0:T(8,128)S(1)} %fill.22.refs_1_.source), channel_id=1, source_target_pairs={{0,1},{1,2},{2,3},{4,5},{5,6},{6,7},{8,9},{9,10},{10,11},{12,13},{... | collective-permute-start | bytes 589832 | tf_op jit(solution)/shard_map/ppermute | solution.py:439
  52.5 2.1 %collective-permute-start.21 = (f32[192,256]{1,0:T(8,128)S(1)}, f32[192,256]{1,0:T(8,128)S(1)}, u32[]{:S(2)}, u32[]{:S(2)}) collective-permute-start(f32[192,256]{1,0:T(8,128)S(1)} %fill.26.source), channel_id=1, source_target_pairs={{0,1},{1,2},{2,3},{4,5},{5,6},{6,7},{8,9},{9,10},{10,11},{12,13},{... | collective-permute-start | bytes 589832 | tf_op jit(solution)/shard_map/ppermute | solution.py:439
  54.6 2.1 %collective-permute-done.14._ = f32[192,256]{1,0:T(8,128)S(1)} collective-permute-done((f32[192,256]{1,0:T(8,128)S(1)}, f32[192,256]{1,0:T(8,128)S(1)}, u32[]{:S(2)}, u32[]{:S(2)}) %collective-permute-start.14) | collective-permute-done | bytes 196640 | tf_op jit(solution)/shard_map/ppermute | solution.py:439
  56.7 1.9 %collective-permute-start.17 = (f32[192,256]{1,0:T(8,128)S(1)}, f32[192,256]{1,0:T(8,128)S(1)}, u32[]{:S(2)}, u32[]{:S(2)}) collective-permute-start(f32[192,256]{1,0:T(8,128)S(1)} %fill.25.refs_1_.source), channel_id=1, source_target_pairs={{0,1},{1,2},{2,3},{4,5},{5,6},{6,7},{8,9},{9,10},{10,11},{12,13},{... | collective-permute-start | bytes 589832 | tf_op jit(solution)/shard_map/ppermute | solution.py:439
  60.9 1.9 %collective-permute-start.25 = (f32[192,256]{1,0:T(8,128)S(1)}, f32[192,256]{1,0:T(8,128)S(1)}, u32[]{:S(2)}, u32[]{:S(2)}) collective-permute-start(f32[192,256]{1,0:T(8,128)S(1)} %fill.27.source.refs_4_), channel_id=1, source_target_pairs={{0,1},{1,2},{2,3},{4,5},{5,6},{6,7},{8,9},{9,10},{10,11},{12,13},{... | collective-permute-start | bytes 589832 | tf_op jit(solution)/shard_map/ppermute | solution.py:439
  67.0 2.3 %collective-permute-done.17.refs_0_ = f32[192,256]{1,0:T(8,128)S(1)} collective-permute-done((f32[192,256]{1,0:T(8,128)S(1)}, f32[192,256]{1,0:T(8,128)S(1)}, u32[]{:S(2)}, u32[]{:S(2)}) %collective-permute-start.17) | collective-permute-done | bytes 196640 | tf_op jit(solution)/shard_map/ppermute | solution.py:439
  79.0 2.9 %collective-permute-done.18.refs_0_ = f32[192,256]{1,0:T(8,128)S(1)} collective-permute-done((f32[192,256]{1,0:T(8,128)S(1)}, f32[192,256]{1,0:T(8,128)S(1)}, u32[]{:S(2)}, u32[]{:S(2)}) %collective-permute-start.18) | collective-permute-done | bytes 196640 | tf_op jit(solution)/shard_map/ppermute | solution.py:439
  88.9 3.3 %collective-permute-start.27 = (f32[256,256]{1,0:T(8,128)S(1)}, f32[256,256]{1,0:T(8,128)S(1)}, u32[]{:S(2)}, u32[]{:S(2)}) collective-permute-start(f32[256,256]{1,0:T(8,128)S(1)} %get-tuple-element.104), channel_id=1, source_target_pairs={{0,4},{4,0},{8,12},{12,8},{16,20},{20,16},{24,28},{28,24},{1,5},{5... | collective-permute-start | bytes 786440 | tf_op jit(solution)/shard_map/ppermute | solution.py:400
  92.1 4.1 %collective-permute-start.31 = (f32[192,256]{1,0:T(8,128)S(1)}, f32[192,256]{1,0:T(8,128)S(1)}, u32[]{:S(2)}, u32[]{:S(2)}) collective-permute-start(f32[192,256]{1,0:T(8,128)S(1)} %gate.31.source.refs_6_), channel_id=1, source_target_pairs={{2,3},{6,7},{10,11},{14,15},{18,19},{22,23},{26,27},{30,31}} | collective-permute-start | bytes 589832 | tf_op jit(solution)/shard_map/ppermute | solution.py:439
  96.3 2.4 %collective-permute-start.28 = (f32[64,256]{1,0:T(8,128)S(1)}, f32[64,256]{1,0:T(8,128)S(1)}, u32[]{:S(2)}, u32[]{:S(2)}) collective-permute-start(f32[64,256]{1,0:T(8,128)S(1)} %get-tuple-element.106), channel_id=1, source_target_pairs={{0,24},{4,28},{8,16},{12,20},{16,8},{20,12},{24,0},{28,4},{1,25},{... | collective-permute-start | bytes 196616 | tf_op jit(solution)/shard_map/ppermute | solution.py:400
  103.2 11.7 %all_gather.3.c = f32[512,256]{1,0:T(8,128)S(1)} all-gather(f32[64,256]{1,0:T(8,128)S(1)} %get-tuple-element.111), channel_id=1, replica_groups=mesh['row'=8,'col'=4] {'row'}, dimensions={0}, use_global_device_ids=true | all-gather | bytes 589824 | tf_op jit(solution)/shard_map/all_gather | solution.py:464
  114.9 3.7 %subtract.1 = f32[3072,512]{1,0:T(8,128)} custom-call(f32[3072,512]{1,0:T(8,128)S(1)} %copy-done, bf16[3072,512]{1,0:T(8,128)(2,1)S(1)} %get-tuple-element.110.p, f32[512,256]{1,0:T(8,128)S(1)} %all_gather.3.c), custom_call_target="tpu_custom_call" | custom-call | flops 1 | bytes 1 | tf_op jit(solution)/shard_map/subtract/pallas_call | solution.py:380
  (112 shorter events, 49.0 us)
Async XLA Ops:
  2.5 7.4 %collective-permute-start.9 = (f32[192,256]{1,0:T(8,128)S(1)}, f32[192,256]{1,0:T(8,128)S(1)}, u32[]{:S(2)}, u32[]{:S(2)}) collective-permute-start(f32[192,256]{1,0:T(8,128)S(1)} %get-tuple-element.112), channel_id=1, source_target_pairs={{0,1},{4,5},{8,9},{12,13},{16,17},{20,21},{24,25},{28,29}} | collective-permute-start | bytes 589832 | tf_op jit(solution)/shard_map/ppermute | solution.py:439
  4.7 11.9 %collective-permute-start.6 = (f32[192,256]{1,0:T(8,128)S(1)}, f32[192,256]{1,0:T(8,128)S(1)}, u32[]{:S(2)}, u32[]{:S(2)}) collective-permute-start(f32[192,256]{1,0:T(8,128)S(1)} %get-tuple-element.113), channel_id=1, source_target_pairs={{0,1},{4,5},{8,9},{12,13},{16,17},{20,21},{24,25},{28,29}} | collective-permute-start | bytes 589832 | tf_op jit(solution)/shard_map/ppermute | solution.py:439
  6.1 11.9 %collective-permute-start.1 = (f32[192,256]{1,0:T(8,128)S(1)}, f32[192,256]{1,0:T(8,128)S(1)}, u32[]{:S(2)}, u32[]{:S(2)}) collective-permute-start(f32[192,256]{1,0:T(8,128)S(1)} %fill.14.refs_1_.source), channel_id=1, source_target_pairs={{0,1},{1,2},{4,5},{5,6},{8,9},{9,10},{12,13},{13,14},{16,17},{17,1... | collective-permute-start | bytes 589832 | tf_op jit(solution)/shard_map/ppermute | solution.py:439
  9.6 7.0 %collective-permute-start.4 = (f32[128,256]{1,0:T(8,128)S(1)}, f32[128,256]{1,0:T(8,128)S(1)}, u32[]{:S(2)}, u32[]{:S(2)}) collective-permute-start(f32[128,256]{1,0:T(8,128)S(1)} %gate.16.refs_0_), channel_id=1, source_target_pairs={{0,16},{4,20},{8,24},{12,28},{16,0},{20,4},{24,8},{28,12},{1,17},{... | collective-permute-start | bytes 393224 | tf_op jit(solution)/shard_map/ppermute | solution.py:400
  9.9 6.7 %collective-permute-start.3 = (f32[128,256]{1,0:T(8,128)S(1)}, f32[128,256]{1,0:T(8,128)S(1)}, u32[]{:S(2)}, u32[]{:S(2)}) collective-permute-start(f32[128,256]{1,0:T(8,128)S(1)} %gate.16.refs_0_), channel_id=1, source_target_pairs={{0,8},{4,12},{8,0},{12,4},{16,24},{20,28},{24,16},{28,20},{1,9},{5... | collective-permute-start | bytes 393224 | tf_op jit(solution)/shard_map/ppermute | solution.py:400
  12.7 9.1 %collective-permute-start.10 = (f32[192,256]{1,0:T(8,128)S(1)}, f32[192,256]{1,0:T(8,128)S(1)}, u32[]{:S(2)}, u32[]{:S(2)}) collective-permute-start(f32[192,256]{1,0:T(8,128)S(1)} %fill.17.source), channel_id=1, source_target_pairs={{0,1},{1,2},{4,5},{5,6},{8,9},{9,10},{12,13},{13,14},{16,17},{17,1... | collective-permute-start | bytes 589832 | tf_op jit(solution)/shard_map/ppermute | solution.py:439
  16.7 7.9 %collective-permute-start.11 = (f32[192,256]{1,0:T(8,128)S(1)}, f32[192,256]{1,0:T(8,128)S(1)}, u32[]{:S(2)}, u32[]{:S(2)}) collective-permute-start(f32[192,256]{1,0:T(8,128)S(1)} %fill.15.refs_1_.source), channel_id=1, source_target_pairs={{0,1},{1,2},{4,5},{5,6},{8,9},{9,10},{12,13},{13,14},{16,17},{17,1... | collective-permute-start | bytes 589832 | tf_op jit(solution)/shard_map/ppermute | solution.py:439
  18.0 12.9 %collective-permute-start.7 = (f32[192,256]{1,0:T(8,128)S(1)}, f32[192,256]{1,0:T(8,128)S(1)}, u32[]{:S(2)}, u32[]{:S(2)}) collective-permute-start(f32[192,256]{1,0:T(8,128)S(1)} %fill.16.refs_1_.source), channel_id=1, source_target_pairs={{0,1},{1,2},{2,3},{4,5},{5,6},{6,7},{8,9},{9,10},{10,11},{12,13},{... | collective-permute-start | bytes 589832 | tf_op jit(solution)/shard_map/ppermute | solution.py:439
  21.9 13.5 %collective-permute-start.15 = (f32[192,256]{1,0:T(8,128)S(1)}, f32[192,256]{1,0:T(8,128)S(1)}, u32[]{:S(2)}, u32[]{:S(2)}) collective-permute-start(f32[192,256]{1,0:T(8,128)S(1)} %fill.18.refs_1_.source), channel_id=1, source_target_pairs={{0,1},{1,2},{2,3},{4,5},{5,6},{6,7},{8,9},{9,10},{10,11},{12,13},{... | collective-permute-start | bytes 589832 | tf_op jit(solution)/shard_map/ppermute | solution.py:439
  24.6 15.0 %collective-permute-start.13 = (f32[192,256]{1,0:T(8,128)S(1)}, f32[192,256]{1,0:T(8,128)S(1)}, u32[]{:S(2)}, u32[]{:S(2)}) collective-permute-start(f32[192,256]{1,0:T(8,128)S(1)} %fill.19.refs_1_.source), channel_id=1, source_target_pairs={{0,1},{1,2},{2,3},{4,5},{5,6},{6,7},{8,9},{9,10},{10,11},{12,13},{... | collective-permute-start | bytes 589832 | tf_op jit(solution)/shard_map/ppermute | solution.py:439
  30.9 13.0 %collective-permute-start.12 = (f32[192,256]{1,0:T(8,128)S(1)}, f32[192,256]{1,0:T(8,128)S(1)}, u32[]{:S(2)}, u32[]{:S(2)}) collective-permute-start(f32[192,256]{1,0:T(8,128)S(1)} %fill.20.refs_1_.source), channel_id=1, source_target_pairs={{0,1},{1,2},{2,3},{4,5},{5,6},{6,7},{8,9},{9,10},{10,11},{12,13},{... | collective-permute-start | bytes 589832 | tf_op jit(solution)/shard_map/ppermute | solution.py:439
  35.5 12.6 %collective-permute-start.16 = (f32[192,256]{1,0:T(8,128)S(1)}, f32[192,256]{1,0:T(8,128)S(1)}, u32[]{:S(2)}, u32[]{:S(2)}) collective-permute-start(f32[192,256]{1,0:T(8,128)S(1)} %fill.23.source), channel_id=1, source_target_pairs={{0,1},{1,2},{2,3},{4,5},{5,6},{6,7},{8,9},{9,10},{10,11},{12,13},{... | collective-permute-start | bytes 589832 | tf_op jit(solution)/shard_map/ppermute | solution.py:439
  40.5 11.9 %collective-permute-start.19 = (f32[192,256]{1,0:T(8,128)S(1)}, f32[192,256]{1,0:T(8,128)S(1)}, u32[]{:S(2)}, u32[]{:S(2)}) collective-permute-start(f32[192,256]{1,0:T(8,128)S(1)} %fill.21.refs_1_.source), channel_id=1, source_target_pairs={{0,1},{1,2},{2,3},{4,5},{5,6},{6,7},{8,9},{9,10},{10,11},{12,13},{... | collective-permute-start | bytes 589832 | tf_op jit(solution)/shard_map/ppermute | solution.py:439
  43.9 12.8 %collective-permute-start.14 = (f32[192,256]{1,0:T(8,128)S(1)}, f32[192,256]{1,0:T(8,128)S(1)}, u32[]{:S(2)}, u32[]{:S(2)}) collective-permute-start(f32[192,256]{1,0:T(8,128)S(1)} %fill.22.refs_1_.source), channel_id=1, source_target_pairs={{0,1},{1,2},{2,3},{4,5},{5,6},{6,7},{8,9},{9,10},{10,11},{12,13},{... | collective-permute-start | bytes 589832 | tf_op jit(solution)/shard_map/ppermute | solution.py:439
  48.1 12.8 %collective-permute-start.24 = (f32[192,256]{1,0:T(8,128)S(1)}, f32[192,256]{1,0:T(8,128)S(1)}, u32[]{:S(2)}, u32[]{:S(2)}) collective-permute-start(f32[192,256]{1,0:T(8,128)S(1)} %fill.24.refs_1_.source), channel_id=1, source_target_pairs={{0,1},{1,2},{2,3},{4,5},{5,6},{6,7},{8,9},{9,10},{10,11},{12,13},{... | collective-permute-start | bytes 589832 | tf_op jit(solution)/shard_map/ppermute | solution.py:439
  52.5 12.6 %collective-permute-start.21 = (f32[192,256]{1,0:T(8,128)S(1)}, f32[192,256]{1,0:T(8,128)S(1)}, u32[]{:S(2)}, u32[]{:S(2)}) collective-permute-start(f32[192,256]{1,0:T(8,128)S(1)} %fill.26.source), channel_id=1, source_target_pairs={{0,1},{1,2},{2,3},{4,5},{5,6},{6,7},{8,9},{9,10},{10,11},{12,13},{... | collective-permute-start | bytes 589832 | tf_op jit(solution)/shard_map/ppermute | solution.py:439
  56.7 12.6 %collective-permute-start.17 = (f32[192,256]{1,0:T(8,128)S(1)}, f32[192,256]{1,0:T(8,128)S(1)}, u32[]{:S(2)}, u32[]{:S(2)}) collective-permute-start(f32[192,256]{1,0:T(8,128)S(1)} %fill.25.refs_1_.source), channel_id=1, source_target_pairs={{0,1},{1,2},{2,3},{4,5},{5,6},{6,7},{8,9},{9,10},{10,11},{12,13},{... | collective-permute-start | bytes 589832 | tf_op jit(solution)/shard_map/ppermute | solution.py:439
  60.9 12.6 %collective-permute-start.25 = (f32[192,256]{1,0:T(8,128)S(1)}, f32[192,256]{1,0:T(8,128)S(1)}, u32[]{:S(2)}, u32[]{:S(2)}) collective-permute-start(f32[192,256]{1,0:T(8,128)S(1)} %fill.27.source.refs_4_), channel_id=1, source_target_pairs={{0,1},{1,2},{2,3},{4,5},{5,6},{6,7},{8,9},{9,10},{10,11},{12,13},{... | collective-permute-start | bytes 589832 | tf_op jit(solution)/shard_map/ppermute | solution.py:439
  65.1 12.6 %collective-permute-start.22 = (f32[192,256]{1,0:T(8,128)S(1)}, f32[192,256]{1,0:T(8,128)S(1)}, u32[]{:S(2)}, u32[]{:S(2)}) collective-permute-start(f32[192,256]{1,0:T(8,128)S(1)} %gate.28.source), channel_id=1, source_target_pairs={{1,2},{2,3},{5,6},{6,7},{9,10},{10,11},{13,14},{14,15},{17,18},{18... | collective-permute-start | bytes 589832 | tf_op jit(solution)/shard_map/ppermute | solution.py:439
  69.3 12.6 %collective-permute-start.18 = (f32[192,256]{1,0:T(8,128)S(1)}, f32[192,256]{1,0:T(8,128)S(1)}, u32[]{:S(2)}, u32[]{:S(2)}) collective-permute-start(f32[192,256]{1,0:T(8,128)S(1)} %gate.26.source), channel_id=1, source_target_pairs={{1,2},{2,3},{5,6},{6,7},{9,10},{10,11},{13,14},{14,15},{17,18},{18... | collective-permute-start | bytes 589832 | tf_op jit(solution)/shard_map/ppermute | solution.py:439
  73.5 14.6 %collective-permute-start.26 = (f32[192,256]{1,0:T(8,128)S(1)}, f32[192,256]{1,0:T(8,128)S(1)}, u32[]{:S(2)}, u32[]{:S(2)}) collective-permute-start(f32[192,256]{1,0:T(8,128)S(1)} %gate.30.source.refs_5_), channel_id=1, source_target_pairs={{1,2},{2,3},{5,6},{6,7},{9,10},{10,11},{13,14},{14,15},{17,18},{18... | collective-permute-start | bytes 589832 | tf_op jit(solution)/shard_map/ppermute | solution.py:439
  77.7 10.5 %collective-permute-start.23 = (f32[192,256]{1,0:T(8,128)S(1)}, f32[192,256]{1,0:T(8,128)S(1)}, u32[]{:S(2)}, u32[]{:S(2)}) collective-permute-start(f32[192,256]{1,0:T(8,128)S(1)} %gate.29.source), channel_id=1, source_target_pairs={{2,3},{6,7},{10,11},{14,15},{18,19},{22,23},{26,27},{30,31}} | collective-permute-start | bytes 589832 | tf_op jit(solution)/shard_map/ppermute | solution.py:439
  88.9 7.4 %collective-permute-start.27 = (f32[256,256]{1,0:T(8,128)S(1)}, f32[256,256]{1,0:T(8,128)S(1)}, u32[]{:S(2)}, u32[]{:S(2)}) collective-permute-start(f32[256,256]{1,0:T(8,128)S(1)} %get-tuple-element.104), channel_id=1, source_target_pairs={{0,4},{4,0},{8,12},{12,8},{16,20},{20,16},{24,28},{28,24},{1,5},{5... | collective-permute-start | bytes 786440 | tf_op jit(solution)/shard_map/ppermute | solution.py:400
  92.1 8.4 %collective-permute-start.31 = (f32[192,256]{1,0:T(8,128)S(1)}, f32[192,256]{1,0:T(8,128)S(1)}, u32[]{:S(2)}, u32[]{:S(2)}) collective-permute-start(f32[192,256]{1,0:T(8,128)S(1)} %gate.31.source.refs_6_), channel_id=1, source_target_pairs={{2,3},{6,7},{10,11},{14,15},{18,19},{22,23},{26,27},{30,31}} | collective-permute-start | bytes 589832 | tf_op jit(solution)/shard_map/ppermute | solution.py:439
  (10 other events, 37.2 us)

commit v6 on v5

--- a/solution.py
+++ b/solution.py
@@ -353,13 +353,38 @@
     )(col, *parts, *[piece for hop in hops for piece in hop])
 
 
-def subtract(matrix, halves, coeffs):
+def stack(parts):
+    size = parts[0].shape[0]
+
+    def body(*refs):
+        for k, ref in enumerate(refs[:-1]):
+            refs[-1][k * size : (k + 1) * size, :] = ref[...]
+
+    return pl.pallas_call(
+        body,
+        in_specs=[VMEM] * len(parts),
+        out_specs=VMEM,
+        out_shape=shape(len(parts) * size, PANEL),
+        compiler_params=params(4),
+        cost_estimate=small(),
+        name="stack",
+    )(*parts)
+
+
+def subtract(row, matrix, halves, mine, other, pairs):
     rows, width = matrix.shape
     tiles = 12
     size = rows // tiles
-
-    def body(a, p, c, out, ct, held, sems):
-        ct_high, ct_low = split(c[...].T)
+    block = width // (2 * pairs)
+
+    def body(row_ref, a, p, mine_ref, other_ref, out, coeffs, ct, held, sems):
+        chip, first = row_ref[0] // 2, row_ref[0] % 2 == 0
+        for k in range(pairs):
+            here = pl.ds(pl.multiple_of((chip ^ k) * block, block), block)
+            one, two = mine_ref[here, :], other_ref[here, :]
+            coeffs[2 * k * block : (2 * k + 1) * block, :] = jnp.where(first, one, two)
+            coeffs[(2 * k + 1) * block : (2 * k + 2) * block, :] = jnp.where(first, two, one)
+        ct_high, ct_low = split(coeffs[...].T)
         ct[:PANEL, :] = ct_high
         ct[PANEL : 2 * PANEL, :] = ct_high
         ct[2 * PANEL :, :] = ct_low
@@ -379,18 +404,19 @@
 
     return pl.pallas_call(
         body,
-        in_specs=[VMEM] * 3,
+        in_specs=[SMEM] + [VMEM] * 4,
         out_specs=ANY,
         out_shape=shape(rows, width),
         scratch_shapes=[
+            pltpu.VMEM((width, PANEL), F32),
             pltpu.VMEM((3 * PANEL, width), BF16),
             pltpu.VMEM((tiles, size, width), F32),
             pltpu.SemaphoreType.DMA((tiles,)),
         ],
-        compiler_params=params(20),
+        compiler_params=params(22),
         cost_estimate=small(),
         name="subtract",
-    )(matrix, halves, coeffs)
+    )(row, matrix, halves, mine, other)
 
 
 def program(n_row, n_col):
@@ -461,8 +487,9 @@
             [sent[CHUNKS + p + LAG * h] for p in range(pieces)] for h in range(n_col)
         ]
         top_rows, coeffs = solve(col, parts, inverse)
-        coeffs = lax.all_gather(coeffs, "row", axis=0, tiled=True)
-        return top_rows, subtract(matrix, halves, coeffs)
+        far = [swap(coeffs, 2 * j) for j in reversed(range(1, pairs))]
+        mine = stack([coeffs] + far[::-1])
+        return top_rows, subtract(row, matrix, halves, mine, swap(mine, 1), pairs)
 
     return shards
 

time: 119 us -> 118 us (level)
  blocking collectives: 11.7 us -> 0 us
  starting transfers between devices: 50.1 us -> 55.1 us
  waiting for transfers between devices: 34.4 us -> 39.2 us
    all_gather x1 -> x0, blocking collectives: 11.7 us -> none  [shards(): coeffs = lax.all_gather(coeffs, 'row', axis=0, tiled=True)]
    ppermute x9 -> x13, starting transfers between devices: 10.3 us -> 15.3 us  [swap(): return lax.ppermute(x, 'row', [(r, r ^ bit) for r in range(n_row)])]
    ppermute x9 -> x13, waiting for transfers between devices: 7.66 us -> 12.5 us  [swap(): return lax.ppermute(x, 'row', [(r, r ^ bit) for r in range(n_row)])]
    pallas_call x1 -> x2, Pallas kernels: 3.68 us -> 3.82 us  [the longest x1 3.8 us: subtract(): pl.pallas_call(body, in_specs=[SMEM] + [VMEM] * 4, out_specs=ANY, out_sha...]
  transfers between devices with their start and end apart: 32 -> 36, of which waited for: 21 -> 25; matrix products, arithmetic and copies ran while one was open for 0% -> 0% of each run, Pallas kernels for 12% -> 12%
where the time goes in v6:
time: 118 us; the launch traced here: 117 us
  starting transfers between devices  55.1 us (47%)
  waiting for transfers between devices  39.2 us (33%)
  Pallas kernels  19.5 us (17%)
  local copies, waits for them, and re-layouts  1.7 us (1%)
  between operations  1.52 us (1%)
    ppermute x23, starting transfers between devices, shards(): received.append(lax.ppermute(sent[s], 'col', hops))  39.8 us
    ppermute x23, waiting for transfers between devices, shards(): received.append(lax.ppermute(sent[s], 'col', hops))  26.7 us
    ppermute x13, starting transfers between devices, swap(): return lax.ppermute(x, 'row', [(r, r ^ bit) for r in range(n_row)])  15.3 us
    pallas_call x22, Pallas kernels, consume(): pl.pallas_call(body, in_specs=[SMEM, SMEM, VMEM, VMEM] + ([VMEM, ANY] if...  13.4 us
    ppermute x13, waiting for transfers between devices, swap(): return lax.ppermute(x, 'row', [(r, r ^ bit) for r in range(n_row)])  12.5 us
    pallas_call x1, Pallas kernels, subtract(): pl.pallas_call(body, in_specs=[SMEM] + [VMEM] * 4, out_specs=ANY, out_sha...  3.8 us
  transfers between devices with their start and end apart: 36, of which 25 were waited for; matrix products, arithmetic and copies ran while one was open for 0% of the time, Pallas kernels for 12%

profile of v6, /device:TPU:17, one launch (start us, length us, event | category | flops | bytes accessed | tf_op | source)
XLA Modules:
  0.0 116.9 jit_solution(11051462698005102811)
XLA Ops:
  7.4 2.2 %collective-permute-start.5 = (f32[128,256]{1,0:T(8,128)S(1)}, f32[128,256]{1,0:T(8,128)S(1)}, u32[]{:S(2)}, u32[]{:S(2)}) collective-permute-start(f32[128,256]{1,0:T(8,128)S(1)} %gate.16.refs_0_), channel_id=1, source_target_pairs={{0,24},{4,28},{8,16},{12,20},{16,8},{20,12},{24,0},{28,4},{1,25},{... | collective-permute-start | bytes 393224 | tf_op jit(solution)/shard_map/ppermute | solution.py:426
  10.1 2.6 %collective-permute-done.5.refs_3_ = f32[128,256]{1,0:T(8,128)S(1)} collective-permute-done((f32[128,256]{1,0:T(8,128)S(1)}, f32[128,256]{1,0:T(8,128)S(1)}, u32[]{:S(2)}, u32[]{:S(2)}) %collective-permute-start.5) | collective-permute-done | bytes 131104 | tf_op jit(solution)/shard_map/ppermute | solution.py:426
  14.0 2.6 %collective-permute-done.4.refs_2_ = f32[128,256]{1,0:T(8,128)S(1)} collective-permute-done((f32[128,256]{1,0:T(8,128)S(1)}, f32[128,256]{1,0:T(8,128)S(1)}, u32[]{:S(2)}, u32[]{:S(2)}) %collective-permute-start.4) | collective-permute-done | bytes 131104 | tf_op jit(solution)/shard_map/ppermute | solution.py:426
  18.0 2.0 %collective-permute-start.7 = (f32[192,256]{1,0:T(8,128)S(1)}, f32[192,256]{1,0:T(8,128)S(1)}, u32[]{:S(2)}, u32[]{:S(2)}) collective-permute-start(f32[192,256]{1,0:T(8,128)S(1)} %fill.16.refs_1_.source), channel_id=1, source_target_pairs={{0,1},{1,2},{2,3},{4,5},{5,6},{6,7},{8,9},{9,10},{10,11},{12,13},{... | collective-permute-start | bytes 589832 | tf_op jit(solution)/shard_map/ppermute | solution.py:465
  21.9 1.9 %collective-permute-start.15 = (f32[192,256]{1,0:T(8,128)S(1)}, f32[192,256]{1,0:T(8,128)S(1)}, u32[]{:S(2)}, u32[]{:S(2)}) collective-permute-start(f32[192,256]{1,0:T(8,128)S(1)} %fill.18.refs_1_.source), channel_id=1, source_target_pairs={{0,1},{1,2},{2,3},{4,5},{5,6},{6,7},{8,9},{9,10},{10,11},{12,13},{... | collective-permute-start | bytes 589832 | tf_op jit(solution)/shard_map/ppermute | solution.py:465
  24.6 1.9 %collective-permute-start.13 = (f32[192,256]{1,0:T(8,128)S(1)}, f32[192,256]{1,0:T(8,128)S(1)}, u32[]{:S(2)}, u32[]{:S(2)}) collective-permute-start(f32[192,256]{1,0:T(8,128)S(1)} %fill.19.refs_1_.source), channel_id=1, source_target_pairs={{0,1},{1,2},{2,3},{4,5},{5,6},{6,7},{8,9},{9,10},{10,11},{12,13},{... | collective-permute-start | bytes 589832 | tf_op jit(solution)/shard_map/ppermute | solution.py:465
  26.6 4.2 %collective-permute-done.7._ = f32[192,256]{1,0:T(8,128)S(1)} collective-permute-done((f32[192,256]{1,0:T(8,128)S(1)}, f32[192,256]{1,0:T(8,128)S(1)}, u32[]{:S(2)}, u32[]{:S(2)}) %collective-permute-start.7) | collective-permute-done | bytes 196640 | tf_op jit(solution)/shard_map/ppermute | solution.py:465
  30.9 1.9 %collective-permute-start.12 = (f32[192,256]{1,0:T(8,128)S(1)}, f32[192,256]{1,0:T(8,128)S(1)}, u32[]{:S(2)}, u32[]{:S(2)}) collective-permute-start(f32[192,256]{1,0:T(8,128)S(1)} %fill.20.refs_1_.source), channel_id=1, source_target_pairs={{0,1},{1,2},{2,3},{4,5},{5,6},{6,7},{8,9},{9,10},{10,11},{12,13},{... | collective-permute-start | bytes 589832 | tf_op jit(solution)/shard_map/ppermute | solution.py:465
  32.9 2.5 %collective-permute-done.15._ = f32[192,256]{1,0:T(8,128)S(1)} collective-permute-done((f32[192,256]{1,0:T(8,128)S(1)}, f32[192,256]{1,0:T(8,128)S(1)}, u32[]{:S(2)}, u32[]{:S(2)}) %collective-permute-start.15) | collective-permute-done | bytes 196640 | tf_op jit(solution)/shard_map/ppermute | solution.py:465
  35.5 1.9 %collective-permute-start.16 = (f32[192,256]{1,0:T(8,128)S(1)}, f32[192,256]{1,0:T(8,128)S(1)}, u32[]{:S(2)}, u32[]{:S(2)}) collective-permute-start(f32[192,256]{1,0:T(8,128)S(1)} %fill.23.source), channel_id=1, source_target_pairs={{0,1},{1,2},{2,3},{4,5},{5,6},{6,7},{8,9},{9,10},{10,11},{12,13},{... | collective-permute-start | bytes 589832 | tf_op jit(solution)/shard_map/ppermute | solution.py:465
  37.4 2.2 %collective-permute-done.13._ = f32[192,256]{1,0:T(8,128)S(1)} collective-permute-done((f32[192,256]{1,0:T(8,128)S(1)}, f32[192,256]{1,0:T(8,128)S(1)}, u32[]{:S(2)}, u32[]{:S(2)}) %collective-permute-start.13) | collective-permute-done | bytes 196640 | tf_op jit(solution)/shard_map/ppermute | solution.py:465
  40.5 1.9 %collective-permute-start.19 = (f32[192,256]{1,0:T(8,128)S(1)}, f32[192,256]{1,0:T(8,128)S(1)}, u32[]{:S(2)}, u32[]{:S(2)}) collective-permute-start(f32[192,256]{1,0:T(8,128)S(1)} %fill.21.refs_1_.source), channel_id=1, source_target_pairs={{0,1},{1,2},{2,3},{4,5},{5,6},{6,7},{8,9},{9,10},{10,11},{12,13},{... | collective-permute-start | bytes 589832 | tf_op jit(solution)/shard_map/ppermute | solution.py:465
  43.9 1.9 %collective-permute-start.14 = (f32[192,256]{1,0:T(8,128)S(1)}, f32[192,256]{1,0:T(8,128)S(1)}, u32[]{:S(2)}, u32[]{:S(2)}) collective-permute-start(f32[192,256]{1,0:T(8,128)S(1)} %fill.22.refs_1_.source), channel_id=1, source_target_pairs={{0,1},{1,2},{2,3},{4,5},{5,6},{6,7},{8,9},{9,10},{10,11},{12,13},{... | collective-permute-start | bytes 589832 | tf_op jit(solution)/shard_map/ppermute | solution.py:465
  48.1 1.9 %collective-permute-start.24 = (f32[192,256]{1,0:T(8,128)S(1)}, f32[192,256]{1,0:T(8,128)S(1)}, u32[]{:S(2)}, u32[]{:S(2)}) collective-permute-start(f32[192,256]{1,0:T(8,128)S(1)} %fill.24.refs_1_.source), channel_id=1, source_target_pairs={{0,1},{1,2},{2,3},{4,5},{5,6},{6,7},{8,9},{9,10},{10,11},{12,13},{... | collective-permute-start | bytes 589832 | tf_op jit(solution)/shard_map/ppermute | solution.py:465
  52.4 2.1 %collective-permute-start.21 = (f32[192,256]{1,0:T(8,128)S(1)}, f32[192,256]{1,0:T(8,128)S(1)}, u32[]{:S(2)}, u32[]{:S(2)}) collective-permute-start(f32[192,256]{1,0:T(8,128)S(1)} %fill.26.source), channel_id=1, source_target_pairs={{0,1},{1,2},{2,3},{4,5},{5,6},{6,7},{8,9},{9,10},{10,11},{12,13},{... | collective-permute-start | bytes 589832 | tf_op jit(solution)/shard_map/ppermute | solution.py:465
  54.6 2.1 %collective-permute-done.14._ = f32[192,256]{1,0:T(8,128)S(1)} collective-permute-done((f32[192,256]{1,0:T(8,128)S(1)}, f32[192,256]{1,0:T(8,128)S(1)}, u32[]{:S(2)}, u32[]{:S(2)}) %collective-permute-start.14) | collective-permute-done | bytes 196640 | tf_op jit(solution)/shard_map/ppermute | solution.py:465
  56.7 1.9 %collective-permute-start.17 = (f32[192,256]{1,0:T(8,128)S(1)}, f32[192,256]{1,0:T(8,128)S(1)}, u32[]{:S(2)}, u32[]{:S(2)}) collective-permute-start(f32[192,256]{1,0:T(8,128)S(1)} %fill.25.refs_1_.source), channel_id=1, source_target_pairs={{0,1},{1,2},{2,3},{4,5},{5,6},{6,7},{8,9},{9,10},{10,11},{12,13},{... | collective-permute-start | bytes 589832 | tf_op jit(solution)/shard_map/ppermute | solution.py:465
  67.0 2.3 %collective-permute-done.17.refs_0_ = f32[192,256]{1,0:T(8,128)S(1)} collective-permute-done((f32[192,256]{1,0:T(8,128)S(1)}, f32[192,256]{1,0:T(8,128)S(1)}, u32[]{:S(2)}, u32[]{:S(2)}) %collective-permute-start.17) | collective-permute-done | bytes 196640 | tf_op jit(solution)/shard_map/ppermute | solution.py:465
  79.0 2.9 %collective-permute-done.18.refs_0_ = f32[192,256]{1,0:T(8,128)S(1)} collective-permute-done((f32[192,256]{1,0:T(8,128)S(1)}, f32[192,256]{1,0:T(8,128)S(1)}, u32[]{:S(2)}, u32[]{:S(2)}) %collective-permute-start.18) | collective-permute-done | bytes 196640 | tf_op jit(solution)/shard_map/ppermute | solution.py:465
  88.9 3.3 %collective-permute-start.27 = (f32[256,256]{1,0:T(8,128)S(1)}, f32[256,256]{1,0:T(8,128)S(1)}, u32[]{:S(2)}, u32[]{:S(2)}) collective-permute-start(f32[256,256]{1,0:T(8,128)S(1)} %get-tuple-element.104), channel_id=1, source_target_pairs={{0,4},{4,0},{8,12},{12,8},{16,20},{20,16},{24,28},{28,24},{1,5},{5... | collective-permute-start | bytes 786440 | tf_op jit(solution)/shard_map/ppermute | solution.py:426
  92.1 4.1 %collective-permute-start.31 = (f32[192,256]{1,0:T(8,128)S(1)}, f32[192,256]{1,0:T(8,128)S(1)}, u32[]{:S(2)}, u32[]{:S(2)}) collective-permute-start(f32[192,256]{1,0:T(8,128)S(1)} %gate.31.source.refs_6_), channel_id=1, source_target_pairs={{2,3},{6,7},{10,11},{14,15},{18,19},{22,23},{26,27},{30,31}} | collective-permute-start | bytes 589832 | tf_op jit(solution)/shard_map/ppermute | solution.py:465
  96.3 2.3 %collective-permute-start.28 = (f32[64,256]{1,0:T(8,128)S(1)}, f32[64,256]{1,0:T(8,128)S(1)}, u32[]{:S(2)}, u32[]{:S(2)}) collective-permute-start(f32[64,256]{1,0:T(8,128)S(1)} %get-tuple-element.106), channel_id=1, source_target_pairs={{0,24},{4,28},{8,16},{12,20},{16,8},{20,12},{24,0},{28,4},{1,25},{... | collective-permute-start | bytes 196616 | tf_op jit(solution)/shard_map/ppermute | solution.py:426
  108.0 2.0 %collective-permute-done.32.refs_1_ = f32[64,256]{1,0:T(8,128)S(1)} collective-permute-done((f32[64,256]{1,0:T(8,128)S(1)}, f32[64,256]{1,0:T(8,128)S(1)}, u32[]{:S(2)}, u32[]{:S(2)}) %collective-permute-start.32) | collective-permute-done | bytes 65568 | tf_op jit(solution)/shard_map/ppermute | solution.py:426
  113.0 3.8 %subtract.1 = f32[3072,512]{1,0:T(8,128)} custom-call(s32[1]{0:T(128)} %bitcast.1.row_ref, f32[3072,512]{1,0:T(8,128)S(1)} %copy-done, bf16[3072,512]{1,0:T(8,128)(2,1)S(1)} %get-tuple-element.110.p, f32[256,256]{1,0:T(8,128)S(1)} %stack.1.mine_ref, f32[256,256]{1,0:T(8,128)S(1)} %collective-permute-done.35.other_ref), custom_call_target="tpu_custom_call" | custom-call | flops 1 | bytes 1 | tf_op jit(solution)/shard_map/subtract/pallas_call | solution.py:405
  (120 shorter events, 56.8 us)
Async XLA Ops:
  2.5 7.4 %collective-permute-start.9 = (f32[192,256]{1,0:T(8,128)S(1)}, f32[192,256]{1,0:T(8,128)S(1)}, u32[]{:S(2)}, u32[]{:S(2)}) collective-permute-start(f32[192,256]{1,0:T(8,128)S(1)} %get-tuple-element.112), channel_id=1, source_target_pairs={{0,1},{4,5},{8,9},{12,13},{16,17},{20,21},{24,25},{28,29}} | collective-permute-start | bytes 589832 | tf_op jit(solution)/shard_map/ppermute | solution.py:465
  4.7 11.9 %collective-permute-start.6 = (f32[192,256]{1,0:T(8,128)S(1)}, f32[192,256]{1,0:T(8,128)S(1)}, u32[]{:S(2)}, u32[]{:S(2)}) collective-permute-start(f32[192,256]{1,0:T(8,128)S(1)} %get-tuple-element.113), channel_id=1, source_target_pairs={{0,1},{4,5},{8,9},{12,13},{16,17},{20,21},{24,25},{28,29}} | collective-permute-start | bytes 589832 | tf_op jit(solution)/shard_map/ppermute | solution.py:465
  6.1 11.9 %collective-permute-start.1 = (f32[192,256]{1,0:T(8,128)S(1)}, f32[192,256]{1,0:T(8,128)S(1)}, u32[]{:S(2)}, u32[]{:S(2)}) collective-permute-start(f32[192,256]{1,0:T(8,128)S(1)} %fill.14.refs_1_.source), channel_id=1, source_target_pairs={{0,1},{1,2},{4,5},{5,6},{8,9},{9,10},{12,13},{13,14},{16,17},{17,1... | collective-permute-start | bytes 589832 | tf_op jit(solution)/shard_map/ppermute | solution.py:465
  9.6 7.0 %collective-permute-start.4 = (f32[128,256]{1,0:T(8,128)S(1)}, f32[128,256]{1,0:T(8,128)S(1)}, u32[]{:S(2)}, u32[]{:S(2)}) collective-permute-start(f32[128,256]{1,0:T(8,128)S(1)} %gate.16.refs_0_), channel_id=1, source_target_pairs={{0,16},{4,20},{8,24},{12,28},{16,0},{20,4},{24,8},{28,12},{1,17},{... | collective-permute-start | bytes 393224 | tf_op jit(solution)/shard_map/ppermute | solution.py:426
  9.9 6.7 %collective-permute-start.3 = (f32[128,256]{1,0:T(8,128)S(1)}, f32[128,256]{1,0:T(8,128)S(1)}, u32[]{:S(2)}, u32[]{:S(2)}) collective-permute-start(f32[128,256]{1,0:T(8,128)S(1)} %gate.16.refs_0_), channel_id=1, source_target_pairs={{0,8},{4,12},{8,0},{12,4},{16,24},{20,28},{24,16},{28,20},{1,9},{5... | collective-permute-start | bytes 393224 | tf_op jit(solution)/shard_map/ppermute | solution.py:426
  12.7 9.1 %collective-permute-start.10 = (f32[192,256]{1,0:T(8,128)S(1)}, f32[192,256]{1,0:T(8,128)S(1)}, u32[]{:S(2)}, u32[]{:S(2)}) collective-permute-start(f32[192,256]{1,0:T(8,128)S(1)} %fill.17.source), channel_id=1, source_target_pairs={{0,1},{1,2},{4,5},{5,6},{8,9},{9,10},{12,13},{13,14},{16,17},{17,1... | collective-permute-start | bytes 589832 | tf_op jit(solution)/shard_map/ppermute | solution.py:465
  16.7 7.9 %collective-permute-start.11 = (f32[192,256]{1,0:T(8,128)S(1)}, f32[192,256]{1,0:T(8,128)S(1)}, u32[]{:S(2)}, u32[]{:S(2)}) collective-permute-start(f32[192,256]{1,0:T(8,128)S(1)} %fill.15.refs_1_.source), channel_id=1, source_target_pairs={{0,1},{1,2},{4,5},{5,6},{8,9},{9,10},{12,13},{13,14},{16,17},{17,1... | collective-permute-start | bytes 589832 | tf_op jit(solution)/shard_map/ppermute | solution.py:465
  18.0 12.9 %collective-permute-start.7 = (f32[192,256]{1,0:T(8,128)S(1)}, f32[192,256]{1,0:T(8,128)S(1)}, u32[]{:S(2)}, u32[]{:S(2)}) collective-permute-start(f32[192,256]{1,0:T(8,128)S(1)} %fill.16.refs_1_.source), channel_id=1, source_target_pairs={{0,1},{1,2},{2,3},{4,5},{5,6},{6,7},{8,9},{9,10},{10,11},{12,13},{... | collective-permute-start | bytes 589832 | tf_op jit(solution)/shard_map/ppermute | solution.py:465
  21.9 13.5 %collective-permute-start.15 = (f32[192,256]{1,0:T(8,128)S(1)}, f32[192,256]{1,0:T(8,128)S(1)}, u32[]{:S(2)}, u32[]{:S(2)}) collective-permute-start(f32[192,256]{1,0:T(8,128)S(1)} %fill.18.refs_1_.source), channel_id=1, source_target_pairs={{0,1},{1,2},{2,3},{4,5},{5,6},{6,7},{8,9},{9,10},{10,11},{12,13},{... | collective-permute-start | bytes 589832 | tf_op jit(solution)/shard_map/ppermute | solution.py:465
  24.6 15.0 %collective-permute-start.13 = (f32[192,256]{1,0:T(8,128)S(1)}, f32[192,256]{1,0:T(8,128)S(1)}, u32[]{:S(2)}, u32[]{:S(2)}) collective-permute-start(f32[192,256]{1,0:T(8,128)S(1)} %fill.19.refs_1_.source), channel_id=1, source_target_pairs={{0,1},{1,2},{2,3},{4,5},{5,6},{6,7},{8,9},{9,10},{10,11},{12,13},{... | collective-permute-start | bytes 589832 | tf_op jit(solution)/shard_map/ppermute | solution.py:465
  30.9 13.0 %collective-permute-start.12 = (f32[192,256]{1,0:T(8,128)S(1)}, f32[192,256]{1,0:T(8,128)S(1)}, u32[]{:S(2)}, u32[]{:S(2)}) collective-permute-start(f32[192,256]{1,0:T(8,128)S(1)} %fill.20.refs_1_.source), channel_id=1, source_target_pairs={{0,1},{1,2},{2,3},{4,5},{5,6},{6,7},{8,9},{9,10},{10,11},{12,13},{... | collective-permute-start | bytes 589832 | tf_op jit(solution)/shard_map/ppermute | solution.py:465
  35.5 12.6 %collective-permute-start.16 = (f32[192,256]{1,0:T(8,128)S(1)}, f32[192,256]{1,0:T(8,128)S(1)}, u32[]{:S(2)}, u32[]{:S(2)}) collective-permute-start(f32[192,256]{1,0:T(8,128)S(1)} %fill.23.source), channel_id=1, source_target_pairs={{0,1},{1,2},{2,3},{4,5},{5,6},{6,7},{8,9},{9,10},{10,11},{12,13},{... | collective-permute-start | bytes 589832 | tf_op jit(solution)/shard_map/ppermute | solution.py:465
  40.5 11.9 %collective-permute-start.19 = (f32[192,256]{1,0:T(8,128)S(1)}, f32[192,256]{1,0:T(8,128)S(1)}, u32[]{:S(2)}, u32[]{:S(2)}) collective-permute-start(f32[192,256]{1,0:T(8,128)S(1)} %fill.21.refs_1_.source), channel_id=1, source_target_pairs={{0,1},{1,2},{2,3},{4,5},{5,6},{6,7},{8,9},{9,10},{10,11},{12,13},{... | collective-permute-start | bytes 589832 | tf_op jit(solution)/shard_map/ppermute | solution.py:465
  43.9 12.8 %collective-permute-start.14 = (f32[192,256]{1,0:T(8,128)S(1)}, f32[192,256]{1,0:T(8,128)S(1)}, u32[]{:S(2)}, u32[]{:S(2)}) collective-permute-start(f32[192,256]{1,0:T(8,128)S(1)} %fill.22.refs_1_.source), channel_id=1, source_target_pairs={{0,1},{1,2},{2,3},{4,5},{5,6},{6,7},{8,9},{9,10},{10,11},{12,13},{... | collective-permute-start | bytes 589832 | tf_op jit(solution)/shard_map/ppermute | solution.py:465
  48.1 12.8 %collective-permute-start.24 = (f32[192,256]{1,0:T(8,128)S(1)}, f32[192,256]{1,0:T(8,128)S(1)}, u32[]{:S(2)}, u32[]{:S(2)}) collective-permute-start(f32[192,256]{1,0:T(8,128)S(1)} %fill.24.refs_1_.source), channel_id=1, source_target_pairs={{0,1},{1,2},{2,3},{4,5},{5,6},{6,7},{8,9},{9,10},{10,11},{12,13},{... | collective-permute-start | bytes 589832 | tf_op jit(solution)/shard_map/ppermute | solution.py:465
  52.4 12.6 %collective-permute-start.21 = (f32[192,256]{1,0:T(8,128)S(1)}, f32[192,256]{1,0:T(8,128)S(1)}, u32[]{:S(2)}, u32[]{:S(2)}) collective-permute-start(f32[192,256]{1,0:T(8,128)S(1)} %fill.26.source), channel_id=1, source_target_pairs={{0,1},{1,2},{2,3},{4,5},{5,6},{6,7},{8,9},{9,10},{10,11},{12,13},{... | collective-permute-start | bytes 589832 | tf_op jit(solution)/shard_map/ppermute | solution.py:465
  56.7 12.6 %collective-permute-start.17 = (f32[192,256]{1,0:T(8,128)S(1)}, f32[192,256]{1,0:T(8,128)S(1)}, u32[]{:S(2)}, u32[]{:S(2)}) collective-permute-start(f32[192,256]{1,0:T(8,128)S(1)} %fill.25.refs_1_.source), channel_id=1, source_target_pairs={{0,1},{1,2},{2,3},{4,5},{5,6},{6,7},{8,9},{9,10},{10,11},{12,13},{... | collective-permute-start | bytes 589832 | tf_op jit(solution)/shard_map/ppermute | solution.py:465
  60.9 12.6 %collective-permute-start.25 = (f32[192,256]{1,0:T(8,128)S(1)}, f32[192,256]{1,0:T(8,128)S(1)}, u32[]{:S(2)}, u32[]{:S(2)}) collective-permute-start(f32[192,256]{1,0:T(8,128)S(1)} %fill.27.source.refs_4_), channel_id=1, source_target_pairs={{0,1},{1,2},{2,3},{4,5},{5,6},{6,7},{8,9},{9,10},{10,11},{12,13},{... | collective-permute-start | bytes 589832 | tf_op jit(solution)/shard_map/ppermute | solution.py:465
  65.1 12.6 %collective-permute-start.22 = (f32[192,256]{1,0:T(8,128)S(1)}, f32[192,256]{1,0:T(8,128)S(1)}, u32[]{:S(2)}, u32[]{:S(2)}) collective-permute-start(f32[192,256]{1,0:T(8,128)S(1)} %gate.28.source), channel_id=1, source_target_pairs={{1,2},{2,3},{5,6},{6,7},{9,10},{10,11},{13,14},{14,15},{17,18},{18... | collective-permute-start | bytes 589832 | tf_op jit(solution)/shard_map/ppermute | solution.py:465
  69.3 12.6 %collective-permute-start.18 = (f32[192,256]{1,0:T(8,128)S(1)}, f32[192,256]{1,0:T(8,128)S(1)}, u32[]{:S(2)}, u32[]{:S(2)}) collective-permute-start(f32[192,256]{1,0:T(8,128)S(1)} %gate.26.source), channel_id=1, source_target_pairs={{1,2},{2,3},{5,6},{6,7},{9,10},{10,11},{13,14},{14,15},{17,18},{18... | collective-permute-start | bytes 589832 | tf_op jit(solution)/shard_map/ppermute | solution.py:465
  73.5 14.6 %collective-permute-start.26 = (f32[192,256]{1,0:T(8,128)S(1)}, f32[192,256]{1,0:T(8,128)S(1)}, u32[]{:S(2)}, u32[]{:S(2)}) collective-permute-start(f32[192,256]{1,0:T(8,128)S(1)} %gate.30.source.refs_5_), channel_id=1, source_target_pairs={{1,2},{2,3},{5,6},{6,7},{9,10},{10,11},{13,14},{14,15},{17,18},{18... | collective-permute-start | bytes 589832 | tf_op jit(solution)/shard_map/ppermute | solution.py:465
  77.7 10.5 %collective-permute-start.23 = (f32[192,256]{1,0:T(8,128)S(1)}, f32[192,256]{1,0:T(8,128)S(1)}, u32[]{:S(2)}, u32[]{:S(2)}) collective-permute-start(f32[192,256]{1,0:T(8,128)S(1)} %gate.29.source), channel_id=1, source_target_pairs={{2,3},{6,7},{10,11},{14,15},{18,19},{22,23},{26,27},{30,31}} | collective-permute-start | bytes 589832 | tf_op jit(solution)/shard_map/ppermute | solution.py:465
  88.9 7.4 %collective-permute-start.27 = (f32[256,256]{1,0:T(8,128)S(1)}, f32[256,256]{1,0:T(8,128)S(1)}, u32[]{:S(2)}, u32[]{:S(2)}) collective-permute-start(f32[256,256]{1,0:T(8,128)S(1)} %get-tuple-element.104), channel_id=1, source_target_pairs={{0,4},{4,0},{8,12},{12,8},{16,20},{20,16},{24,28},{28,24},{1,5},{5... | collective-permute-start | bytes 786440 | tf_op jit(solution)/shard_map/ppermute | solution.py:426
  92.1 8.4 %collective-permute-start.31 = (f32[192,256]{1,0:T(8,128)S(1)}, f32[192,256]{1,0:T(8,128)S(1)}, u32[]{:S(2)}, u32[]{:S(2)}) collective-permute-start(f32[192,256]{1,0:T(8,128)S(1)} %gate.31.source.refs_6_), channel_id=1, source_target_pairs={{2,3},{6,7},{10,11},{14,15},{18,19},{22,23},{26,27},{30,31}} | collective-permute-start | bytes 589832 | tf_op jit(solution)/shard_map/ppermute | solution.py:465
  (14 other events, 51.4 us)

commit v7 on v6

--- a/solution.py
+++ b/solution.py
@@ -9,6 +9,8 @@
 CHUNKS = 16
 LAG = 3
 HALF = PANEL // 2
+QUARTER = PANEL // 4
+PACKED = 2 * QUARTER + QUARTER // 2
 OWN = 4
 BLOCK = 32
 HIGHEST = lax.Precision.HIGHEST
@@ -169,7 +171,7 @@
             pltpu.VMEM((tiles, rows, PANEL), F32),
             pltpu.SemaphoreType.DMA((tiles,)),
         ],
-        compiler_params=params(55),
+        compiler_params=params(53),
         cost_estimate=small(),
         name="gram",
     )(col, row, matrix)
@@ -219,9 +221,13 @@
             rows = dot((work * root)[:, BLOCK:], out[first:last, :], ((1,), (0,)), HIGHEST)
             out[first:last, :] = rows
             if last == PANEL:
-                packed[:HALF, :] = out[HALF:, PANEL:]
-                packed[HALF:, :HALF] = out[: HALF // 2, PANEL : PANEL + HALF]
-                packed[HALF:, HALF:] = out[HALF // 2 : HALF, PANEL : PANEL + HALF]
+                q = QUARTER
+                packed[:q, :] = out[3 * q :, PANEL:]
+                packed[q : 2 * q, : 3 * q] = out[2 * q : 3 * q, PANEL : PANEL + 3 * q]
+                packed[q : 2 * q, 3 * q :] = out[:q, PANEL : PANEL + q]
+                for k in range(4):
+                    high, left = q + k % 2 * (q // 2), PANEL + k // 2 * q
+                    packed[2 * q :, k * q : (k + 1) * q] = out[high : high + q // 2, left : left + q]
             else:
                 left, right = last // 128 * 128, PANEL + -(-last // 128) * 128
                 out[last:, left:right] -= dot(
@@ -232,7 +238,7 @@
         body,
         in_specs=[SMEM, SMEM] + [VMEM] * len(state),
         out_specs=(VMEM, VMEM) if last == PANEL else VMEM,
-        out_shape=(shape(PANEL, width), shape(HALF + HALF // 2, PANEL))
+        out_shape=(shape(PANEL, width), shape(PACKED, PANEL))
         if last == PANEL
         else shape(PANEL, width),
         input_output_aliases={2: 0} if block else {},
@@ -247,7 +253,7 @@
 
     def body(col_ref, row_ref, block, source, *refs):
         if pairs:
-            total, _, keep, give, halves, held, sem, turned = refs
+            total, _, keep, give, halves, held, sem, summed, turned = refs
         elif step > LAG:
             total, _, out, halves, held, sem = refs
         else:
@@ -270,12 +276,13 @@
 
         valid = (col_ref[0] > 0) & (chunk >= 0) & (chunk < CHUNKS)
         if pairs:
-            turned[...] = total[...].T
+            summed[...] = total[...]
 
             @pl.when(valid)
             def _():
-                turned[...] += part(chunk * rows, source[...]).T
-
+                summed[...] += part(chunk * rows, source[...])
+
+            turned[...] = summed[...].T
             halve(turned, row_ref, keep, give, pairs)
         else:
             out[...] = total[...] if step > LAG else jnp.zeros_like(out)
@@ -310,30 +317,51 @@
             pltpu.VMEM((OWN * rows if step == CHUNKS + 1 else rows, 2 * PANEL), BF16),
             pltpu.SemaphoreType.DMA(()),
         ]
-        + ([pltpu.VMEM((width, PANEL), F32)] if pairs else []),
+        + ([pltpu.VMEM(dims, F32) for dims in ((PANEL, width), (width, PANEL))] if pairs else []),
         compiler_params=params(16),
         cost_estimate=small(),
         name="consume",
     )(col, row, matrix, sent, *before)
 
 
+def cut(col, x, where):
+    def body(col_ref, source, out):
+        @pl.when(col_ref[0] == where)
+        def _():
+            out[...] = source[:PACKED, :]
+
+    return pl.pallas_call(
+        body,
+        in_specs=[SMEM, VMEM],
+        out_specs=VMEM,
+        out_shape=shape(PACKED, PANEL),
+        compiler_params=params(2),
+        cost_estimate=small(),
+        name="cut",
+    )(col, x)
+
+
 def solve(col, parts, hops):
     n, rows = len(parts), parts[0].shape[0]
-    pieces, size = len(hops[0]), hops[0][0].shape[0]
 
     def body(col_ref, *refs):
-        sources, (top, coeffs, inverse, packed) = refs[n:-4], refs[-4:]
-        for h in range(len(hops)):
+        sources, (top, coeffs, inverse) = refs[n:-3], refs[-3:]
+        q = QUARTER
+        inverse[:HALF, HALF:] = jnp.zeros((HALF, HALF), F32)
+        inverse[:q, q:HALF] = jnp.zeros((q, q), F32)
+        inverse[HALF : 3 * q, 3 * q :] = jnp.zeros((q, q), F32)
+        for h, source in enumerate(sources):
 
             @pl.when(col_ref[0] == h)
             def _():
-                for p in range(pieces):
-                    packed[p * size : (p + 1) * size, :] = sources[h * pieces + p][...]
-
-        inverse[HALF:, :] = packed[:HALF, :]
-        inverse[: HALF // 2, :HALF] = packed[HALF : HALF + HALF // 2, :HALF]
-        inverse[HALF // 2 : HALF, :HALF] = packed[HALF : HALF + HALF // 2, HALF:]
-        inverse[:HALF, HALF:] = jnp.zeros((HALF, HALF), F32)
+                inverse[3 * q :, :] = source[:q, :]
+                inverse[2 * q : 3 * q, : 3 * q] = source[q : 2 * q, : 3 * q]
+                inverse[:q, :q] = source[q : 2 * q, 3 * q :]
+                for k in range(4):
+                    high, left = q + k % 2 * (q // 2), k // 2 * q
+                    piece = source[2 * q : PACKED, k * q : (k + 1) * q]
+                    inverse[high : high + q // 2, left : left + q] = piece
+
         total = refs[0][...]
         for ref in refs[1:n]:
             total += ref[...]
@@ -343,14 +371,14 @@
 
     return pl.pallas_call(
         body,
-        in_specs=[SMEM] + [VMEM] * (n + len(hops) * pieces),
+        in_specs=[SMEM] + [VMEM] * (n + len(hops)),
         out_specs=(VMEM, VMEM),
         out_shape=(shape(rows, PANEL),) * 2,
-        scratch_shapes=[pltpu.VMEM((PANEL, PANEL), F32), pltpu.VMEM((pieces * size, PANEL), F32)],
+        scratch_shapes=[pltpu.VMEM((PANEL, PANEL), F32)],
         compiler_params=params(6),
         cost_estimate=small(),
         name="solve",
-    )(col, *parts, *[piece for hop in hops for piece in hop])
+    )(col, *parts, *hops)
 
 
 def stack(parts):
@@ -434,8 +462,7 @@
         row = lax.axis_index("row").astype(jnp.int32).reshape(1)
         blocks = PANEL // BLOCK
         rows = matrix.shape[0] // CHUNKS
-        pieces = -(-(HALF + HALF // 2) // rows)
-        shifts = CHUNKS + pieces + LAG * (n_col - 2)
+        shifts = CHUNKS + 1 + LAG * (n_col - 2)
         last = CHUNKS - 1 + LAG * (n_col - 1)
         first = LAG + 3
         due = [first + i * (CHUNKS - 1 - first) // (blocks - 1) for i in range(blocks)]
@@ -454,22 +481,25 @@
                 x = received[s - LAG]
                 if s < CHUNKS:
                     sent.append(fill(col, x, matrix, s * rows, *after))
-                elif s < CHUNKS + pieces:
-                    sent.append(fill(col, x, packed, (s - CHUNKS) * rows, *after))
+                elif s == CHUNKS:
+                    sent.append(fill(col, x, packed, 0, *after))
                 else:
                     sent.append(gate(x, *after))
             else:
                 sent.append(received[s - LAG])
             if s < shifts:
-                hops = [(h, h + 1) for h in range(n_col - 1) if 0 <= s - LAG * h < CHUNKS + pieces]
-                received.append(lax.ppermute(sent[s], "col", hops))
+                hops = [(h, h + 1) for h in range(n_col - 1) if 0 <= s - LAG * h <= CHUNKS]
+                x = sent[s]
+                if s == shifts - 1 and n_col > 2:
+                    x = cut(col, x, n_col - 2)
+                received.append(lax.ppermute(x, "col", hops))
             if LAG <= s <= last:
                 before = sums[s - 1] if s > LAG else ()
                 sums[s] = consume(
                     col, row, matrix, sent[s], s, before, pairs if s == last else 0
                 )
             if s == LAG + 1:
-                half = gate(half, sent[LAG])
+                half = gate(half, received[0])
                 state = [add([half] + [swap(half, 2 * j) for j in range(1, pairs)])]
             elif s == LAG + 2:
                 mine = gate(state[0], sent[s])
@@ -483,9 +513,7 @@
                     state = [state]
         keep, give, halves = sums[last]
         parts = scatter(row, keep, give)
-        inverse = [
-            [sent[CHUNKS + p + LAG * h] for p in range(pieces)] for h in range(n_col)
-        ]
+        inverse = [sent[CHUNKS + LAG * h] for h in range(n_col)]
         top_rows, coeffs = solve(col, parts, inverse)
         far = [swap(coeffs, 2 * j) for j in reversed(range(1, pairs))]
         mine = stack([coeffs] + far[::-1])

time: 118 us -> 117 us (level)
    ppermute x13, waiting for transfers between devices: 12.5 us -> 13.9 us  [swap(): return lax.ppermute(x, 'row', [(r, r ^ bit) for r in range(n_row)])]
where the time goes in v7:
time: 117 us
  starting transfers between devices  54.2 us (46%)
  waiting for transfers between devices  39.8 us (34%)
  Pallas kernels  19.1 us (16%)
  local copies, waits for them, and re-layouts  2.08 us (2%)
  between operations  1.51 us (1%)
    ppermute x23, starting transfers between devices, shards(): received.append(lax.ppermute(x, 'col', hops))  39.8 us
    ppermute x23, waiting for transfers between devices, shards(): received.append(lax.ppermute(x, 'col', hops))  25.9 us
    ppermute x13, starting transfers between devices, swap(): return lax.ppermute(x, 'row', [(r, r ^ bit) for r in range(n_row)])  14.3 us
    ppermute x13, waiting for transfers between devices, swap(): return lax.ppermute(x, 'row', [(r, r ^ bit) for r in range(n_row)])  13.9 us
    pallas_call x22, Pallas kernels, consume(): pl.pallas_call(body, in_specs=[SMEM, SMEM, VMEM, VMEM] + ([VMEM, ANY] if...  13.5 us
    pallas_call x1, Pallas kernels, subtract(): pl.pallas_call(body, in_specs=[SMEM] + [VMEM] * 4, out_specs=ANY, out_sha...  3.88 us
  transfers between devices with their start and end apart: 36, of which 25 were waited for; matrix products, arithmetic and copies ran while one was open for 0% of the time, Pallas kernels for 12%

profile of v7, /device:TPU:17, one launch (start us, length us, event | category | flops | bytes accessed | tf_op | source)
XLA Modules:
  0.0 116.6 jit_solution(15065592217996152593)
XLA Ops:
  7.3 2.2 %collective-permute-start.5 = (f32[128,256]{1,0:T(8,128)S(1)}, f32[128,256]{1,0:T(8,128)S(1)}, u32[]{:S(2)}, u32[]{:S(2)}) collective-permute-start(f32[128,256]{1,0:T(8,128)S(1)} %gate.16.refs_0_), channel_id=1, source_target_pairs={{0,24},{4,28},{8,16},{12,20},{16,8},{20,12},{24,0},{28,4},{1,25},{... | collective-permute-start | bytes 393224 | tf_op jit(solution)/shard_map/ppermute | solution.py:454
  10.0 2.6 %collective-permute-done.5.refs_3_ = f32[128,256]{1,0:T(8,128)S(1)} collective-permute-done((f32[128,256]{1,0:T(8,128)S(1)}, f32[128,256]{1,0:T(8,128)S(1)}, u32[]{:S(2)}, u32[]{:S(2)}) %collective-permute-start.5) | collective-permute-done | bytes 131104 | tf_op jit(solution)/shard_map/ppermute | solution.py:454
  13.9 2.6 %collective-permute-done.4.refs_2_ = f32[128,256]{1,0:T(8,128)S(1)} collective-permute-done((f32[128,256]{1,0:T(8,128)S(1)}, f32[128,256]{1,0:T(8,128)S(1)}, u32[]{:S(2)}, u32[]{:S(2)}) %collective-permute-start.4) | collective-permute-done | bytes 131104 | tf_op jit(solution)/shard_map/ppermute | solution.py:454
  17.9 2.0 %collective-permute-start.7 = (f32[192,256]{1,0:T(8,128)S(1)}, f32[192,256]{1,0:T(8,128)S(1)}, u32[]{:S(2)}, u32[]{:S(2)}) collective-permute-start(f32[192,256]{1,0:T(8,128)S(1)} %fill.16.refs_1_.source), channel_id=1, source_target_pairs={{0,1},{1,2},{2,3},{4,5},{5,6},{6,7},{8,9},{9,10},{10,11},{12,13},{... | collective-permute-start | bytes 589832 | tf_op jit(solution)/shard_map/ppermute | solution.py:495
  21.8 1.9 %collective-permute-start.15 = (f32[192,256]{1,0:T(8,128)S(1)}, f32[192,256]{1,0:T(8,128)S(1)}, u32[]{:S(2)}, u32[]{:S(2)}) collective-permute-start(f32[192,256]{1,0:T(8,128)S(1)} %fill.18.refs_1_.source), channel_id=1, source_target_pairs={{0,1},{1,2},{2,3},{4,5},{5,6},{6,7},{8,9},{9,10},{10,11},{12,13},{... | collective-permute-start | bytes 589832 | tf_op jit(solution)/shard_map/ppermute | solution.py:495
  23.8 1.9 %collective-permute-start.13 = (f32[192,256]{1,0:T(8,128)S(1)}, f32[192,256]{1,0:T(8,128)S(1)}, u32[]{:S(2)}, u32[]{:S(2)}) collective-permute-start(f32[192,256]{1,0:T(8,128)S(1)} %fill.19.refs_1_.source), channel_id=1, source_target_pairs={{0,1},{1,2},{2,3},{4,5},{5,6},{6,7},{8,9},{9,10},{10,11},{12,13},{... | collective-permute-start | bytes 589832 | tf_op jit(solution)/shard_map/ppermute | solution.py:495
  25.8 4.6 %collective-permute-done.7._ = f32[192,256]{1,0:T(8,128)S(1)} collective-permute-done((f32[192,256]{1,0:T(8,128)S(1)}, f32[192,256]{1,0:T(8,128)S(1)}, u32[]{:S(2)}, u32[]{:S(2)}) %collective-permute-start.7) | collective-permute-done | bytes 196640 | tf_op jit(solution)/shard_map/ppermute | solution.py:495
  30.4 1.9 %collective-permute-start.12 = (f32[192,256]{1,0:T(8,128)S(1)}, f32[192,256]{1,0:T(8,128)S(1)}, u32[]{:S(2)}, u32[]{:S(2)}) collective-permute-start(f32[192,256]{1,0:T(8,128)S(1)} %fill.20.refs_1_.source), channel_id=1, source_target_pairs={{0,1},{1,2},{2,3},{4,5},{5,6},{6,7},{8,9},{9,10},{10,11},{12,13},{... | collective-permute-start | bytes 589832 | tf_op jit(solution)/shard_map/ppermute | solution.py:495
  32.4 3.0 %collective-permute-done.15._ = f32[192,256]{1,0:T(8,128)S(1)} collective-permute-done((f32[192,256]{1,0:T(8,128)S(1)}, f32[192,256]{1,0:T(8,128)S(1)}, u32[]{:S(2)}, u32[]{:S(2)}) %collective-permute-start.15) | collective-permute-done | bytes 196640 | tf_op jit(solution)/shard_map/ppermute | solution.py:495
  35.4 1.9 %collective-permute-start.16 = (f32[192,256]{1,0:T(8,128)S(1)}, f32[192,256]{1,0:T(8,128)S(1)}, u32[]{:S(2)}, u32[]{:S(2)}) collective-permute-start(f32[192,256]{1,0:T(8,128)S(1)} %fill.23.source), channel_id=1, source_target_pairs={{0,1},{1,2},{2,3},{4,5},{5,6},{6,7},{8,9},{9,10},{10,11},{12,13},{... | collective-permute-start | bytes 589832 | tf_op jit(solution)/shard_map/ppermute | solution.py:495
  37.4 2.2 %collective-permute-done.13._ = f32[192,256]{1,0:T(8,128)S(1)} collective-permute-done((f32[192,256]{1,0:T(8,128)S(1)}, f32[192,256]{1,0:T(8,128)S(1)}, u32[]{:S(2)}, u32[]{:S(2)}) %collective-permute-start.13) | collective-permute-done | bytes 196640 | tf_op jit(solution)/shard_map/ppermute | solution.py:495
  40.4 1.9 %collective-permute-start.19 = (f32[192,256]{1,0:T(8,128)S(1)}, f32[192,256]{1,0:T(8,128)S(1)}, u32[]{:S(2)}, u32[]{:S(2)}) collective-permute-start(f32[192,256]{1,0:T(8,128)S(1)} %fill.21.refs_1_.source), channel_id=1, source_target_pairs={{0,1},{1,2},{2,3},{4,5},{5,6},{6,7},{8,9},{9,10},{10,11},{12,13},{... | collective-permute-start | bytes 589832 | tf_op jit(solution)/shard_map/ppermute | solution.py:495
  43.8 1.9 %collective-permute-start.14 = (f32[192,256]{1,0:T(8,128)S(1)}, f32[192,256]{1,0:T(8,128)S(1)}, u32[]{:S(2)}, u32[]{:S(2)}) collective-permute-start(f32[192,256]{1,0:T(8,128)S(1)} %fill.22.refs_1_.source), channel_id=1, source_target_pairs={{0,1},{1,2},{2,3},{4,5},{5,6},{6,7},{8,9},{9,10},{10,11},{12,13},{... | collective-permute-start | bytes 589832 | tf_op jit(solution)/shard_map/ppermute | solution.py:495
  48.0 1.9 %collective-permute-start.24 = (f32[192,256]{1,0:T(8,128)S(1)}, f32[192,256]{1,0:T(8,128)S(1)}, u32[]{:S(2)}, u32[]{:S(2)}) collective-permute-start(f32[192,256]{1,0:T(8,128)S(1)} %fill.24.refs_1_.source), channel_id=1, source_target_pairs={{0,1},{1,2},{2,3},{4,5},{5,6},{6,7},{8,9},{9,10},{10,11},{12,13},{... | collective-permute-start | bytes 589832 | tf_op jit(solution)/shard_map/ppermute | solution.py:495
  52.3 2.1 %collective-permute-start.21 = (f32[192,256]{1,0:T(8,128)S(1)}, f32[192,256]{1,0:T(8,128)S(1)}, u32[]{:S(2)}, u32[]{:S(2)}) collective-permute-start(f32[192,256]{1,0:T(8,128)S(1)} %fill.26.source), channel_id=1, source_target_pairs={{0,1},{1,2},{2,3},{4,5},{5,6},{6,7},{8,9},{9,10},{10,11},{12,13},{... | collective-permute-start | bytes 589832 | tf_op jit(solution)/shard_map/ppermute | solution.py:495
  54.4 2.1 %collective-permute-done.14._ = f32[192,256]{1,0:T(8,128)S(1)} collective-permute-done((f32[192,256]{1,0:T(8,128)S(1)}, f32[192,256]{1,0:T(8,128)S(1)}, u32[]{:S(2)}, u32[]{:S(2)}) %collective-permute-start.14) | collective-permute-done | bytes 196640 | tf_op jit(solution)/shard_map/ppermute | solution.py:495
  56.5 1.9 %collective-permute-start.17 = (f32[192,256]{1,0:T(8,128)S(1)}, f32[192,256]{1,0:T(8,128)S(1)}, u32[]{:S(2)}, u32[]{:S(2)}) collective-permute-start(f32[192,256]{1,0:T(8,128)S(1)} %fill.25.refs_1_.source), channel_id=1, source_target_pairs={{0,1},{1,2},{2,3},{4,5},{5,6},{6,7},{8,9},{9,10},{10,11},{12,13},{... | collective-permute-start | bytes 589832 | tf_op jit(solution)/shard_map/ppermute | solution.py:495
  60.7 1.9 %collective-permute-start.25 = (f32[192,256]{1,0:T(8,128)S(1)}, f32[192,256]{1,0:T(8,128)S(1)}, u32[]{:S(2)}, u32[]{:S(2)}) collective-permute-start(f32[192,256]{1,0:T(8,128)S(1)} %fill.27.source.refs_4_), channel_id=1, source_target_pairs={{0,1},{1,2},{2,3},{4,5},{5,6},{6,7},{8,9},{9,10},{10,11},{12,13},{... | collective-permute-start | bytes 589832 | tf_op jit(solution)/shard_map/ppermute | solution.py:495
  66.8 2.3 %collective-permute-done.17.refs_0_ = f32[192,256]{1,0:T(8,128)S(1)} collective-permute-done((f32[192,256]{1,0:T(8,128)S(1)}, f32[192,256]{1,0:T(8,128)S(1)}, u32[]{:S(2)}, u32[]{:S(2)}) %collective-permute-start.17) | collective-permute-done | bytes 196640 | tf_op jit(solution)/shard_map/ppermute | solution.py:495
  78.8 2.9 %collective-permute-done.18.refs_0_ = f32[192,256]{1,0:T(8,128)S(1)} collective-permute-done((f32[192,256]{1,0:T(8,128)S(1)}, f32[192,256]{1,0:T(8,128)S(1)}, u32[]{:S(2)}, u32[]{:S(2)}) %collective-permute-start.18) | collective-permute-done | bytes 196640 | tf_op jit(solution)/shard_map/ppermute | solution.py:495
  88.8 3.2 %collective-permute-start.27 = (f32[256,256]{1,0:T(8,128)S(1)}, f32[256,256]{1,0:T(8,128)S(1)}, u32[]{:S(2)}, u32[]{:S(2)}) collective-permute-start(f32[256,256]{1,0:T(8,128)S(1)} %get-tuple-element.104), channel_id=1, source_target_pairs={{0,4},{4,0},{8,12},{12,8},{16,20},{20,16},{24,28},{28,24},{1,5},{5... | collective-permute-start | bytes 786440 | tf_op jit(solution)/shard_map/ppermute | solution.py:454
  92.0 4.2 %collective-permute-start.31 = (f32[160,256]{1,0:T(8,128)S(1)}, f32[160,256]{1,0:T(8,128)S(1)}, u32[]{:S(2)}, u32[]{:S(2)}) collective-permute-start(f32[160,256]{1,0:T(8,128)S(1)} %cut.1), channel_id=1, source_target_pairs={{2,3},{6,7},{10,11},{14,15},{18,19},{22,23},{26,27},{30,31}} | collective-permute-start | bytes 491528 | tf_op jit(solution)/shard_map/ppermute | solution.py:495
  100.3 2.0 %collective-permute-done.29.refs_2_ = f32[64,256]{1,0:T(8,128)S(1)} collective-permute-done((f32[64,256]{1,0:T(8,128)S(1)}, f32[64,256]{1,0:T(8,128)S(1)}, u32[]{:S(2)}, u32[]{:S(2)}) %collective-permute-start.29) | collective-permute-done | bytes 65568 | tf_op jit(solution)/shard_map/ppermute | solution.py:454
  112.6 3.9 %subtract.1 = f32[3072,512]{1,0:T(8,128)} custom-call(s32[1]{0:T(128)} %bitcast.1.row_ref, f32[3072,512]{1,0:T(8,128)S(1)} %copy-done, bf16[3072,512]{1,0:T(8,128)(2,1)S(1)} %get-tuple-element.110.p, f32[256,256]{1,0:T(8,128)S(1)} %stack.1.mine_ref, f32[256,256]{1,0:T(8,128)S(1)} %collective-permute-done.35.other_ref), custom_call_target="tpu_custom_call" | custom-call | flops 1 | bytes 1 | tf_op jit(solution)/shard_map/subtract/pallas_call | solution.py:433
  (119 shorter events, 56.0 us)
Async XLA Ops:
  2.5 7.3 %collective-permute-start.9 = (f32[192,256]{1,0:T(8,128)S(1)}, f32[192,256]{1,0:T(8,128)S(1)}, u32[]{:S(2)}, u32[]{:S(2)}) collective-permute-start(f32[192,256]{1,0:T(8,128)S(1)} %get-tuple-element.112), channel_id=1, source_target_pairs={{0,1},{4,5},{8,9},{12,13},{16,17},{20,21},{24,25},{28,29}} | collective-permute-start | bytes 589832 | tf_op jit(solution)/shard_map/ppermute | solution.py:495
  4.0 12.5 %collective-permute-start.6 = (f32[192,256]{1,0:T(8,128)S(1)}, f32[192,256]{1,0:T(8,128)S(1)}, u32[]{:S(2)}, u32[]{:S(2)}) collective-permute-start(f32[192,256]{1,0:T(8,128)S(1)} %get-tuple-element.113), channel_id=1, source_target_pairs={{0,1},{4,5},{8,9},{12,13},{16,17},{20,21},{24,25},{28,29}} | collective-permute-start | bytes 589832 | tf_op jit(solution)/shard_map/ppermute | solution.py:495
  6.0 11.9 %collective-permute-start.1 = (f32[192,256]{1,0:T(8,128)S(1)}, f32[192,256]{1,0:T(8,128)S(1)}, u32[]{:S(2)}, u32[]{:S(2)}) collective-permute-start(f32[192,256]{1,0:T(8,128)S(1)} %fill.14.source), channel_id=1, source_target_pairs={{0,1},{1,2},{4,5},{5,6},{8,9},{9,10},{12,13},{13,14},{16,17},{17,1... | collective-permute-start | bytes 589832 | tf_op jit(solution)/shard_map/ppermute | solution.py:495
  9.5 7.0 %collective-permute-start.4 = (f32[128,256]{1,0:T(8,128)S(1)}, f32[128,256]{1,0:T(8,128)S(1)}, u32[]{:S(2)}, u32[]{:S(2)}) collective-permute-start(f32[128,256]{1,0:T(8,128)S(1)} %gate.16.refs_0_), channel_id=1, source_target_pairs={{0,16},{4,20},{8,24},{12,28},{16,0},{20,4},{24,8},{28,12},{1,17},{... | collective-permute-start | bytes 393224 | tf_op jit(solution)/shard_map/ppermute | solution.py:454
  9.7 6.7 %collective-permute-start.3 = (f32[128,256]{1,0:T(8,128)S(1)}, f32[128,256]{1,0:T(8,128)S(1)}, u32[]{:S(2)}, u32[]{:S(2)}) collective-permute-start(f32[128,256]{1,0:T(8,128)S(1)} %gate.16.refs_0_), channel_id=1, source_target_pairs={{0,8},{4,12},{8,0},{12,4},{16,24},{20,28},{24,16},{28,20},{1,9},{5... | collective-permute-start | bytes 393224 | tf_op jit(solution)/shard_map/ppermute | solution.py:454
  12.6 9.1 %collective-permute-start.10 = (f32[192,256]{1,0:T(8,128)S(1)}, f32[192,256]{1,0:T(8,128)S(1)}, u32[]{:S(2)}, u32[]{:S(2)}) collective-permute-start(f32[192,256]{1,0:T(8,128)S(1)} %fill.17.source), channel_id=1, source_target_pairs={{0,1},{1,2},{4,5},{5,6},{8,9},{9,10},{12,13},{13,14},{16,17},{17,1... | collective-permute-start | bytes 589832 | tf_op jit(solution)/shard_map/ppermute | solution.py:495
  16.5 7.2 %collective-permute-start.11 = (f32[192,256]{1,0:T(8,128)S(1)}, f32[192,256]{1,0:T(8,128)S(1)}, u32[]{:S(2)}, u32[]{:S(2)}) collective-permute-start(f32[192,256]{1,0:T(8,128)S(1)} %fill.15.refs_1_.source), channel_id=1, source_target_pairs={{0,1},{1,2},{4,5},{5,6},{8,9},{9,10},{12,13},{13,14},{16,17},{17,1... | collective-permute-start | bytes 589832 | tf_op jit(solution)/shard_map/ppermute | solution.py:495
  17.9 12.5 %collective-permute-start.7 = (f32[192,256]{1,0:T(8,128)S(1)}, f32[192,256]{1,0:T(8,128)S(1)}, u32[]{:S(2)}, u32[]{:S(2)}) collective-permute-start(f32[192,256]{1,0:T(8,128)S(1)} %fill.16.refs_1_.source), channel_id=1, source_target_pairs={{0,1},{1,2},{2,3},{4,5},{5,6},{6,7},{8,9},{9,10},{10,11},{12,13},{... | collective-permute-start | bytes 589832 | tf_op jit(solution)/shard_map/ppermute | solution.py:495
  21.8 13.6 %collective-permute-start.15 = (f32[192,256]{1,0:T(8,128)S(1)}, f32[192,256]{1,0:T(8,128)S(1)}, u32[]{:S(2)}, u32[]{:S(2)}) collective-permute-start(f32[192,256]{1,0:T(8,128)S(1)} %fill.18.refs_1_.source), channel_id=1, source_target_pairs={{0,1},{1,2},{2,3},{4,5},{5,6},{6,7},{8,9},{9,10},{10,11},{12,13},{... | collective-permute-start | bytes 589832 | tf_op jit(solution)/shard_map/ppermute | solution.py:495
  23.8 15.8 %collective-permute-start.13 = (f32[192,256]{1,0:T(8,128)S(1)}, f32[192,256]{1,0:T(8,128)S(1)}, u32[]{:S(2)}, u32[]{:S(2)}) collective-permute-start(f32[192,256]{1,0:T(8,128)S(1)} %fill.19.refs_1_.source), channel_id=1, source_target_pairs={{0,1},{1,2},{2,3},{4,5},{5,6},{6,7},{8,9},{9,10},{10,11},{12,13},{... | collective-permute-start | bytes 589832 | tf_op jit(solution)/shard_map/ppermute | solution.py:495
  30.4 13.5 %collective-permute-start.12 = (f32[192,256]{1,0:T(8,128)S(1)}, f32[192,256]{1,0:T(8,128)S(1)}, u32[]{:S(2)}, u32[]{:S(2)}) collective-permute-start(f32[192,256]{1,0:T(8,128)S(1)} %fill.20.refs_1_.source), channel_id=1, source_target_pairs={{0,1},{1,2},{2,3},{4,5},{5,6},{6,7},{8,9},{9,10},{10,11},{12,13},{... | collective-permute-start | bytes 589832 | tf_op jit(solution)/shard_map/ppermute | solution.py:495
  35.4 12.6 %collective-permute-start.16 = (f32[192,256]{1,0:T(8,128)S(1)}, f32[192,256]{1,0:T(8,128)S(1)}, u32[]{:S(2)}, u32[]{:S(2)}) collective-permute-start(f32[192,256]{1,0:T(8,128)S(1)} %fill.23.source), channel_id=1, source_target_pairs={{0,1},{1,2},{2,3},{4,5},{5,6},{6,7},{8,9},{9,10},{10,11},{12,13},{... | collective-permute-start | bytes 589832 | tf_op jit(solution)/shard_map/ppermute | solution.py:495
  40.4 11.8 %collective-permute-start.19 = (f32[192,256]{1,0:T(8,128)S(1)}, f32[192,256]{1,0:T(8,128)S(1)}, u32[]{:S(2)}, u32[]{:S(2)}) collective-permute-start(f32[192,256]{1,0:T(8,128)S(1)} %fill.21.refs_1_.source), channel_id=1, source_target_pairs={{0,1},{1,2},{2,3},{4,5},{5,6},{6,7},{8,9},{9,10},{10,11},{12,13},{... | collective-permute-start | bytes 589832 | tf_op jit(solution)/shard_map/ppermute | solution.py:495
  43.8 12.6 %collective-permute-start.14 = (f32[192,256]{1,0:T(8,128)S(1)}, f32[192,256]{1,0:T(8,128)S(1)}, u32[]{:S(2)}, u32[]{:S(2)}) collective-permute-start(f32[192,256]{1,0:T(8,128)S(1)} %fill.22.refs_1_.source), channel_id=1, source_target_pairs={{0,1},{1,2},{2,3},{4,5},{5,6},{6,7},{8,9},{9,10},{10,11},{12,13},{... | collective-permute-start | bytes 589832 | tf_op jit(solution)/shard_map/ppermute | solution.py:495
  48.0 12.6 %collective-permute-start.24 = (f32[192,256]{1,0:T(8,128)S(1)}, f32[192,256]{1,0:T(8,128)S(1)}, u32[]{:S(2)}, u32[]{:S(2)}) collective-permute-start(f32[192,256]{1,0:T(8,128)S(1)} %fill.24.refs_1_.source), channel_id=1, source_target_pairs={{0,1},{1,2},{2,3},{4,5},{5,6},{6,7},{8,9},{9,10},{10,11},{12,13},{... | collective-permute-start | bytes 589832 | tf_op jit(solution)/shard_map/ppermute | solution.py:495
  52.3 12.6 %collective-permute-start.21 = (f32[192,256]{1,0:T(8,128)S(1)}, f32[192,256]{1,0:T(8,128)S(1)}, u32[]{:S(2)}, u32[]{:S(2)}) collective-permute-start(f32[192,256]{1,0:T(8,128)S(1)} %fill.26.source), channel_id=1, source_target_pairs={{0,1},{1,2},{2,3},{4,5},{5,6},{6,7},{8,9},{9,10},{10,11},{12,13},{... | collective-permute-start | bytes 589832 | tf_op jit(solution)/shard_map/ppermute | solution.py:495
  56.5 12.6 %collective-permute-start.17 = (f32[192,256]{1,0:T(8,128)S(1)}, f32[192,256]{1,0:T(8,128)S(1)}, u32[]{:S(2)}, u32[]{:S(2)}) collective-permute-start(f32[192,256]{1,0:T(8,128)S(1)} %fill.25.refs_1_.source), channel_id=1, source_target_pairs={{0,1},{1,2},{2,3},{4,5},{5,6},{6,7},{8,9},{9,10},{10,11},{12,13},{... | collective-permute-start | bytes 589832 | tf_op jit(solution)/shard_map/ppermute | solution.py:495
  60.7 12.6 %collective-permute-start.25 = (f32[192,256]{1,0:T(8,128)S(1)}, f32[192,256]{1,0:T(8,128)S(1)}, u32[]{:S(2)}, u32[]{:S(2)}) collective-permute-start(f32[192,256]{1,0:T(8,128)S(1)} %fill.27.source.refs_4_), channel_id=1, source_target_pairs={{0,1},{1,2},{2,3},{4,5},{5,6},{6,7},{8,9},{9,10},{10,11},{12,13},{... | collective-permute-start | bytes 589832 | tf_op jit(solution)/shard_map/ppermute | solution.py:495
  64.9 12.6 %collective-permute-start.22 = (f32[192,256]{1,0:T(8,128)S(1)}, f32[192,256]{1,0:T(8,128)S(1)}, u32[]{:S(2)}, u32[]{:S(2)}) collective-permute-start(f32[192,256]{1,0:T(8,128)S(1)} %gate.28.source), channel_id=1, source_target_pairs={{1,2},{2,3},{5,6},{6,7},{9,10},{10,11},{13,14},{14,15},{17,18},{18... | collective-permute-start | bytes 589832 | tf_op jit(solution)/shard_map/ppermute | solution.py:495
  69.1 12.6 %collective-permute-start.18 = (f32[192,256]{1,0:T(8,128)S(1)}, f32[192,256]{1,0:T(8,128)S(1)}, u32[]{:S(2)}, u32[]{:S(2)}) collective-permute-start(f32[192,256]{1,0:T(8,128)S(1)} %gate.26.source), channel_id=1, source_target_pairs={{1,2},{2,3},{5,6},{6,7},{9,10},{10,11},{13,14},{14,15},{17,18},{18... | collective-permute-start | bytes 589832 | tf_op jit(solution)/shard_map/ppermute | solution.py:495
  73.3 14.6 %collective-permute-start.26 = (f32[192,256]{1,0:T(8,128)S(1)}, f32[192,256]{1,0:T(8,128)S(1)}, u32[]{:S(2)}, u32[]{:S(2)}) collective-permute-start(f32[192,256]{1,0:T(8,128)S(1)} %gate.30.source.refs_5_), channel_id=1, source_target_pairs={{1,2},{2,3},{5,6},{6,7},{9,10},{10,11},{13,14},{14,15},{17,18},{18... | collective-permute-start | bytes 589832 | tf_op jit(solution)/shard_map/ppermute | solution.py:495
  77.5 10.5 %collective-permute-start.23 = (f32[192,256]{1,0:T(8,128)S(1)}, f32[192,256]{1,0:T(8,128)S(1)}, u32[]{:S(2)}, u32[]{:S(2)}) collective-permute-start(f32[192,256]{1,0:T(8,128)S(1)} %gate.29.source), channel_id=1, source_target_pairs={{2,3},{6,7},{10,11},{14,15},{18,19},{22,23},{26,27},{30,31}} | collective-permute-start | bytes 589832 | tf_op jit(solution)/shard_map/ppermute | solution.py:495
  88.8 7.4 %collective-permute-start.27 = (f32[256,256]{1,0:T(8,128)S(1)}, f32[256,256]{1,0:T(8,128)S(1)}, u32[]{:S(2)}, u32[]{:S(2)}) collective-permute-start(f32[256,256]{1,0:T(8,128)S(1)} %get-tuple-element.104), channel_id=1, source_target_pairs={{0,4},{4,0},{8,12},{12,8},{16,20},{20,16},{24,28},{28,24},{1,5},{5... | collective-permute-start | bytes 786440 | tf_op jit(solution)/shard_map/ppermute | solution.py:454
  92.0 7.7 %collective-permute-start.31 = (f32[160,256]{1,0:T(8,128)S(1)}, f32[160,256]{1,0:T(8,128)S(1)}, u32[]{:S(2)}, u32[]{:S(2)}) collective-permute-start(f32[160,256]{1,0:T(8,128)S(1)} %cut.1), channel_id=1, source_target_pairs={{2,3},{6,7},{10,11},{14,15},{18,19},{22,23},{26,27},{30,31}} | collective-permute-start | bytes 491528 | tf_op jit(solution)/shard_map/ppermute | solution.py:495
  (13 other events, 47.7 us)

commit v8 on v7

--- a/solution.py
+++ b/solution.py
@@ -472,7 +472,7 @@
             if s < LAG:
                 sent.append(matrix[s * rows : (s + 1) * rows, :PANEL])
             elif s < shifts:
-                after = [sums[s - 2 * LAG][0]] if s - 2 * LAG in sums else []
+                after = [sums[s - LAG - 1][0]] if s - LAG - 1 in sums else []
                 if s == LAG:
                     keep, give = gram_part(col, row, matrix)
                     half = add([keep, swap(give, 1)])

time: 117 us -> 117 us (level)
  no operation moved by 1% of the time
where the time goes in v8:
time: 117 us
  starting transfers between devices  53.9 us (46%)
  waiting for transfers between devices  39.9 us (34%)
  Pallas kernels  19.3 us (16%)
  local copies, waits for them, and re-layouts  2.08 us (2%)
  between operations  1.52 us (1%)
    ppermute x23, starting transfers between devices, shards(): received.append(lax.ppermute(x, 'col', hops))  40.3 us
    ppermute x23, waiting for transfers between devices, shards(): received.append(lax.ppermute(x, 'col', hops))  26.2 us
    ppermute x13, waiting for transfers between devices, swap(): return lax.ppermute(x, 'row', [(r, r ^ bit) for r in range(n_row)])  13.8 us
    ppermute x13, starting transfers between devices, swap(): return lax.ppermute(x, 'row', [(r, r ^ bit) for r in range(n_row)])  13.6 us
    pallas_call x22, Pallas kernels, consume(): pl.pallas_call(body, in_specs=[SMEM, SMEM, VMEM, VMEM] + ([VMEM, ANY] if...  13.5 us
    pallas_call x1, Pallas kernels, subtract(): pl.pallas_call(body, in_specs=[SMEM] + [VMEM] * 4, out_specs=ANY, out_sha...  3.88 us
  transfers between devices with their start and end apart: 36, of which 25 were waited for; matrix products, arithmetic and copies ran while one was open for 0% of the time, Pallas kernels for 12%

profile of v8, /device:TPU:17, one launch (start us, length us, event | category | flops | bytes accessed | tf_op | source)
XLA Modules:
  0.0 116.7 jit_solution(12764612802280206370)
XLA Ops:
  7.3 2.2 %collective-permute-start.5 = (f32[128,256]{1,0:T(8,128)S(1)}, f32[128,256]{1,0:T(8,128)S(1)}, u32[]{:S(2)}, u32[]{:S(2)}) collective-permute-start(f32[128,256]{1,0:T(8,128)S(1)} %gate.16.refs_0_), channel_id=1, source_target_pairs={{0,24},{4,28},{8,16},{12,20},{16,8},{20,12},{24,0},{28,4},{1,25},{... | collective-permute-start | bytes 393224 | tf_op jit(solution)/shard_map/ppermute | solution.py:454
  10.0 2.6 %collective-permute-done.5.refs_3_ = f32[128,256]{1,0:T(8,128)S(1)} collective-permute-done((f32[128,256]{1,0:T(8,128)S(1)}, f32[128,256]{1,0:T(8,128)S(1)}, u32[]{:S(2)}, u32[]{:S(2)}) %collective-permute-start.5) | collective-permute-done | bytes 131104 | tf_op jit(solution)/shard_map/ppermute | solution.py:454
  13.9 2.6 %collective-permute-done.4.refs_2_ = f32[128,256]{1,0:T(8,128)S(1)} collective-permute-done((f32[128,256]{1,0:T(8,128)S(1)}, f32[128,256]{1,0:T(8,128)S(1)}, u32[]{:S(2)}, u32[]{:S(2)}) %collective-permute-start.4) | collective-permute-done | bytes 131104 | tf_op jit(solution)/shard_map/ppermute | solution.py:454
  17.9 2.0 %collective-permute-start.7 = (f32[192,256]{1,0:T(8,128)S(1)}, f32[192,256]{1,0:T(8,128)S(1)}, u32[]{:S(2)}, u32[]{:S(2)}) collective-permute-start(f32[192,256]{1,0:T(8,128)S(1)} %fill.16.refs_1_.source), channel_id=1, source_target_pairs={{0,1},{1,2},{2,3},{4,5},{5,6},{6,7},{8,9},{9,10},{10,11},{12,13},{... | collective-permute-start | bytes 589832 | tf_op jit(solution)/shard_map/ppermute | solution.py:495
  21.9 1.9 %collective-permute-start.15 = (f32[192,256]{1,0:T(8,128)S(1)}, f32[192,256]{1,0:T(8,128)S(1)}, u32[]{:S(2)}, u32[]{:S(2)}) collective-permute-start(f32[192,256]{1,0:T(8,128)S(1)} %fill.18.refs_1_.source), channel_id=1, source_target_pairs={{0,1},{1,2},{2,3},{4,5},{5,6},{6,7},{8,9},{9,10},{10,11},{12,13},{... | collective-permute-start | bytes 589832 | tf_op jit(solution)/shard_map/ppermute | solution.py:495
  23.9 1.9 %collective-permute-start.13 = (f32[192,256]{1,0:T(8,128)S(1)}, f32[192,256]{1,0:T(8,128)S(1)}, u32[]{:S(2)}, u32[]{:S(2)}) collective-permute-start(f32[192,256]{1,0:T(8,128)S(1)} %fill.19.refs_1_.source), channel_id=1, source_target_pairs={{0,1},{1,2},{2,3},{4,5},{5,6},{6,7},{8,9},{9,10},{10,11},{12,13},{... | collective-permute-start | bytes 589832 | tf_op jit(solution)/shard_map/ppermute | solution.py:495
  25.9 4.4 %collective-permute-done.7._ = f32[192,256]{1,0:T(8,128)S(1)} collective-permute-done((f32[192,256]{1,0:T(8,128)S(1)}, f32[192,256]{1,0:T(8,128)S(1)}, u32[]{:S(2)}, u32[]{:S(2)}) %collective-permute-start.7) | collective-permute-done | bytes 196640 | tf_op jit(solution)/shard_map/ppermute | solution.py:495
  30.4 1.9 %collective-permute-start.12 = (f32[192,256]{1,0:T(8,128)S(1)}, f32[192,256]{1,0:T(8,128)S(1)}, u32[]{:S(2)}, u32[]{:S(2)}) collective-permute-start(f32[192,256]{1,0:T(8,128)S(1)} %fill.20.refs_1_.source), channel_id=1, source_target_pairs={{0,1},{1,2},{2,3},{4,5},{5,6},{6,7},{8,9},{9,10},{10,11},{12,13},{... | collective-permute-start | bytes 589832 | tf_op jit(solution)/shard_map/ppermute | solution.py:495
  33.1 2.5 %collective-permute-done.15._ = f32[192,256]{1,0:T(8,128)S(1)} collective-permute-done((f32[192,256]{1,0:T(8,128)S(1)}, f32[192,256]{1,0:T(8,128)S(1)}, u32[]{:S(2)}, u32[]{:S(2)}) %collective-permute-start.15) | collective-permute-done | bytes 196640 | tf_op jit(solution)/shard_map/ppermute | solution.py:495
  35.7 1.9 %collective-permute-start.16 = (f32[192,256]{1,0:T(8,128)S(1)}, f32[192,256]{1,0:T(8,128)S(1)}, u32[]{:S(2)}, u32[]{:S(2)}) collective-permute-start(f32[192,256]{1,0:T(8,128)S(1)} %fill.23.source), channel_id=1, source_target_pairs={{0,1},{1,2},{2,3},{4,5},{5,6},{6,7},{8,9},{9,10},{10,11},{12,13},{... | collective-permute-start | bytes 589832 | tf_op jit(solution)/shard_map/ppermute | solution.py:495
  40.7 1.9 %collective-permute-start.18 = (f32[192,256]{1,0:T(8,128)S(1)}, f32[192,256]{1,0:T(8,128)S(1)}, u32[]{:S(2)}, u32[]{:S(2)}) collective-permute-start(f32[192,256]{1,0:T(8,128)S(1)} %fill.21.refs_1_.source), channel_id=1, source_target_pairs={{0,1},{1,2},{2,3},{4,5},{5,6},{6,7},{8,9},{9,10},{10,11},{12,13},{... | collective-permute-start | bytes 589832 | tf_op jit(solution)/shard_map/ppermute | solution.py:495
  44.1 1.9 %collective-permute-start.14 = (f32[192,256]{1,0:T(8,128)S(1)}, f32[192,256]{1,0:T(8,128)S(1)}, u32[]{:S(2)}, u32[]{:S(2)}) collective-permute-start(f32[192,256]{1,0:T(8,128)S(1)} %fill.22.refs_1_.source), channel_id=1, source_target_pairs={{0,1},{1,2},{2,3},{4,5},{5,6},{6,7},{8,9},{9,10},{10,11},{12,13},{... | collective-permute-start | bytes 589832 | tf_op jit(solution)/shard_map/ppermute | solution.py:495
  48.3 1.9 %collective-permute-start.21 = (f32[192,256]{1,0:T(8,128)S(1)}, f32[192,256]{1,0:T(8,128)S(1)}, u32[]{:S(2)}, u32[]{:S(2)}) collective-permute-start(f32[192,256]{1,0:T(8,128)S(1)} %fill.24.refs_1_.source), channel_id=1, source_target_pairs={{0,1},{1,2},{2,3},{4,5},{5,6},{6,7},{8,9},{9,10},{10,11},{12,13},{... | collective-permute-start | bytes 589832 | tf_op jit(solution)/shard_map/ppermute | solution.py:495
  54.5 2.3 %collective-permute-done.14._ = f32[192,256]{1,0:T(8,128)S(1)} collective-permute-done((f32[192,256]{1,0:T(8,128)S(1)}, f32[192,256]{1,0:T(8,128)S(1)}, u32[]{:S(2)}, u32[]{:S(2)}) %collective-permute-start.14) | collective-permute-done | bytes 196640 | tf_op jit(solution)/shard_map/ppermute | solution.py:495
  56.7 1.9 %collective-permute-start.17 = (f32[192,256]{1,0:T(8,128)S(1)}, f32[192,256]{1,0:T(8,128)S(1)}, u32[]{:S(2)}, u32[]{:S(2)}) collective-permute-start(f32[192,256]{1,0:T(8,128)S(1)} %fill.25.refs_1_.source), channel_id=1, source_target_pairs={{0,1},{1,2},{2,3},{4,5},{5,6},{6,7},{8,9},{9,10},{10,11},{12,13},{... | collective-permute-start | bytes 589832 | tf_op jit(solution)/shard_map/ppermute | solution.py:495
  61.0 1.9 %collective-permute-start.25 = (f32[192,256]{1,0:T(8,128)S(1)}, f32[192,256]{1,0:T(8,128)S(1)}, u32[]{:S(2)}, u32[]{:S(2)}) collective-permute-start(f32[192,256]{1,0:T(8,128)S(1)} %fill.27.source.refs_4_), channel_id=1, source_target_pairs={{0,1},{1,2},{2,3},{4,5},{5,6},{6,7},{8,9},{9,10},{10,11},{12,13},{... | collective-permute-start | bytes 589832 | tf_op jit(solution)/shard_map/ppermute | solution.py:495
  67.1 2.3 %collective-permute-done.17.refs_0_ = f32[192,256]{1,0:T(8,128)S(1)} collective-permute-done((f32[192,256]{1,0:T(8,128)S(1)}, f32[192,256]{1,0:T(8,128)S(1)}, u32[]{:S(2)}, u32[]{:S(2)}) %collective-permute-start.17) | collective-permute-done | bytes 196640 | tf_op jit(solution)/shard_map/ppermute | solution.py:495
  79.1 2.9 %collective-permute-done.19.refs_0_ = f32[192,256]{1,0:T(8,128)S(1)} collective-permute-done((f32[192,256]{1,0:T(8,128)S(1)}, f32[192,256]{1,0:T(8,128)S(1)}, u32[]{:S(2)}, u32[]{:S(2)}) %collective-permute-start.19) | collective-permute-done | bytes 196640 | tf_op jit(solution)/shard_map/ppermute | solution.py:495
  86.7 2.0 %collective-permute-done.22.source = f32[192,256]{1,0:T(8,128)S(1)} collective-permute-done((f32[192,256]{1,0:T(8,128)S(1)}, f32[192,256]{1,0:T(8,128)S(1)}, u32[]{:S(2)}, u32[]{:S(2)}) %collective-permute-start.22) | collective-permute-done | bytes 196640 | tf_op jit(solution)/shard_map/ppermute | solution.py:495
  89.0 2.2 %collective-permute-start.27 = (f32[256,256]{1,0:T(8,128)S(1)}, f32[256,256]{1,0:T(8,128)S(1)}, u32[]{:S(2)}, u32[]{:S(2)}) collective-permute-start(f32[256,256]{1,0:T(8,128)S(1)} %get-tuple-element.104), channel_id=1, source_target_pairs={{0,4},{4,0},{8,12},{12,8},{16,20},{20,16},{24,28},{28,24},{1,5},{5... | collective-permute-start | bytes 786440 | tf_op jit(solution)/shard_map/ppermute | solution.py:454
  91.3 4.8 %collective-permute-start.31 = (f32[160,256]{1,0:T(8,128)S(1)}, f32[160,256]{1,0:T(8,128)S(1)}, u32[]{:S(2)}, u32[]{:S(2)}) collective-permute-start(f32[160,256]{1,0:T(8,128)S(1)} %cut.1), channel_id=1, source_target_pairs={{2,3},{6,7},{10,11},{14,15},{18,19},{22,23},{26,27},{30,31}} | collective-permute-start | bytes 491528 | tf_op jit(solution)/shard_map/ppermute | solution.py:495
  96.2 2.1 %collective-permute-start.28 = (f32[64,256]{1,0:T(8,128)S(1)}, f32[64,256]{1,0:T(8,128)S(1)}, u32[]{:S(2)}, u32[]{:S(2)}) collective-permute-start(f32[64,256]{1,0:T(8,128)S(1)} %get-tuple-element.106), channel_id=1, source_target_pairs={{0,24},{4,28},{8,16},{12,20},{16,8},{20,12},{24,0},{28,4},{1,25},{... | collective-permute-start | bytes 196616 | tf_op jit(solution)/shard_map/ppermute | solution.py:454
  108.0 2.0 %collective-permute-done.32.refs_1_ = f32[64,256]{1,0:T(8,128)S(1)} collective-permute-done((f32[64,256]{1,0:T(8,128)S(1)}, f32[64,256]{1,0:T(8,128)S(1)}, u32[]{:S(2)}, u32[]{:S(2)}) %collective-permute-start.32) | collective-permute-done | bytes 65568 | tf_op jit(solution)/shard_map/ppermute | solution.py:454
  112.7 3.9 %subtract.1 = f32[3072,512]{1,0:T(8,128)} custom-call(s32[1]{0:T(128)} %bitcast.1.row_ref, f32[3072,512]{1,0:T(8,128)S(1)} %copy-done, bf16[3072,512]{1,0:T(8,128)(2,1)S(1)} %get-tuple-element.110.p, f32[256,256]{1,0:T(8,128)S(1)} %stack.1.mine_ref, f32[256,256]{1,0:T(8,128)S(1)} %collective-permute-done.35.other_ref), custom_call_target="tpu_custom_call" | custom-call | flops 1 | bytes 1 | tf_op jit(solution)/shard_map/subtract/pallas_call | solution.py:433
  (119 shorter events, 57.1 us)
Async XLA Ops:
  2.5 7.3 %collective-permute-start.8 = (f32[192,256]{1,0:T(8,128)S(1)}, f32[192,256]{1,0:T(8,128)S(1)}, u32[]{:S(2)}, u32[]{:S(2)}) collective-permute-start(f32[192,256]{1,0:T(8,128)S(1)} %get-tuple-element.112), channel_id=1, source_target_pairs={{0,1},{4,5},{8,9},{12,13},{16,17},{20,21},{24,25},{28,29}} | collective-permute-start | bytes 589832 | tf_op jit(solution)/shard_map/ppermute | solution.py:495
  4.0 12.5 %collective-permute-start.6 = (f32[192,256]{1,0:T(8,128)S(1)}, f32[192,256]{1,0:T(8,128)S(1)}, u32[]{:S(2)}, u32[]{:S(2)}) collective-permute-start(f32[192,256]{1,0:T(8,128)S(1)} %get-tuple-element.113), channel_id=1, source_target_pairs={{0,1},{4,5},{8,9},{12,13},{16,17},{20,21},{24,25},{28,29}} | collective-permute-start | bytes 589832 | tf_op jit(solution)/shard_map/ppermute | solution.py:495
  6.0 11.9 %collective-permute-start.1 = (f32[192,256]{1,0:T(8,128)S(1)}, f32[192,256]{1,0:T(8,128)S(1)}, u32[]{:S(2)}, u32[]{:S(2)}) collective-permute-start(f32[192,256]{1,0:T(8,128)S(1)} %fill.14.source), channel_id=1, source_target_pairs={{0,1},{1,2},{4,5},{5,6},{8,9},{9,10},{12,13},{13,14},{16,17},{17,1... | collective-permute-start | bytes 589832 | tf_op jit(solution)/shard_map/ppermute | solution.py:495
  9.5 7.0 %collective-permute-start.4 = (f32[128,256]{1,0:T(8,128)S(1)}, f32[128,256]{1,0:T(8,128)S(1)}, u32[]{:S(2)}, u32[]{:S(2)}) collective-permute-start(f32[128,256]{1,0:T(8,128)S(1)} %gate.16.refs_0_), channel_id=1, source_target_pairs={{0,16},{4,20},{8,24},{12,28},{16,0},{20,4},{24,8},{28,12},{1,17},{... | collective-permute-start | bytes 393224 | tf_op jit(solution)/shard_map/ppermute | solution.py:454
  9.7 6.7 %collective-permute-start.3 = (f32[128,256]{1,0:T(8,128)S(1)}, f32[128,256]{1,0:T(8,128)S(1)}, u32[]{:S(2)}, u32[]{:S(2)}) collective-permute-start(f32[128,256]{1,0:T(8,128)S(1)} %gate.16.refs_0_), channel_id=1, source_target_pairs={{0,8},{4,12},{8,0},{12,4},{16,24},{20,28},{24,16},{28,20},{1,9},{5... | collective-permute-start | bytes 393224 | tf_op jit(solution)/shard_map/ppermute | solution.py:454
  12.6 9.2 %collective-permute-start.10 = (f32[192,256]{1,0:T(8,128)S(1)}, f32[192,256]{1,0:T(8,128)S(1)}, u32[]{:S(2)}, u32[]{:S(2)}) collective-permute-start(f32[192,256]{1,0:T(8,128)S(1)} %fill.17.source), channel_id=1, source_target_pairs={{0,1},{1,2},{4,5},{5,6},{8,9},{9,10},{12,13},{13,14},{16,17},{17,1... | collective-permute-start | bytes 589832 | tf_op jit(solution)/shard_map/ppermute | solution.py:495
  16.5 7.3 %collective-permute-start.11 = (f32[192,256]{1,0:T(8,128)S(1)}, f32[192,256]{1,0:T(8,128)S(1)}, u32[]{:S(2)}, u32[]{:S(2)}) collective-permute-start(f32[192,256]{1,0:T(8,128)S(1)} %fill.15.refs_1_.source), channel_id=1, source_target_pairs={{0,1},{1,2},{4,5},{5,6},{8,9},{9,10},{12,13},{13,14},{16,17},{17,1... | collective-permute-start | bytes 589832 | tf_op jit(solution)/shard_map/ppermute | solution.py:495
  17.9 12.5 %collective-permute-start.7 = (f32[192,256]{1,0:T(8,128)S(1)}, f32[192,256]{1,0:T(8,128)S(1)}, u32[]{:S(2)}, u32[]{:S(2)}) collective-permute-start(f32[192,256]{1,0:T(8,128)S(1)} %fill.16.refs_1_.source), channel_id=1, source_target_pairs={{0,1},{1,2},{2,3},{4,5},{5,6},{6,7},{8,9},{9,10},{10,11},{12,13},{... | collective-permute-start | bytes 589832 | tf_op jit(solution)/shard_map/ppermute | solution.py:495
  21.9 13.8 %collective-permute-start.15 = (f32[192,256]{1,0:T(8,128)S(1)}, f32[192,256]{1,0:T(8,128)S(1)}, u32[]{:S(2)}, u32[]{:S(2)}) collective-permute-start(f32[192,256]{1,0:T(8,128)S(1)} %fill.18.refs_1_.source), channel_id=1, source_target_pairs={{0,1},{1,2},{2,3},{4,5},{5,6},{6,7},{8,9},{9,10},{10,11},{12,13},{... | collective-permute-start | bytes 589832 | tf_op jit(solution)/shard_map/ppermute | solution.py:495
  23.9 16.0 %collective-permute-start.13 = (f32[192,256]{1,0:T(8,128)S(1)}, f32[192,256]{1,0:T(8,128)S(1)}, u32[]{:S(2)}, u32[]{:S(2)}) collective-permute-start(f32[192,256]{1,0:T(8,128)S(1)} %fill.19.refs_1_.source), channel_id=1, source_target_pairs={{0,1},{1,2},{2,3},{4,5},{5,6},{6,7},{8,9},{9,10},{10,11},{12,13},{... | collective-permute-start | bytes 589832 | tf_op jit(solution)/shard_map/ppermute | solution.py:495
  30.4 13.7 %collective-permute-start.12 = (f32[192,256]{1,0:T(8,128)S(1)}, f32[192,256]{1,0:T(8,128)S(1)}, u32[]{:S(2)}, u32[]{:S(2)}) collective-permute-start(f32[192,256]{1,0:T(8,128)S(1)} %fill.20.refs_1_.source), channel_id=1, source_target_pairs={{0,1},{1,2},{2,3},{4,5},{5,6},{6,7},{8,9},{9,10},{10,11},{12,13},{... | collective-permute-start | bytes 589832 | tf_op jit(solution)/shard_map/ppermute | solution.py:495
  35.7 12.6 %collective-permute-start.16 = (f32[192,256]{1,0:T(8,128)S(1)}, f32[192,256]{1,0:T(8,128)S(1)}, u32[]{:S(2)}, u32[]{:S(2)}) collective-permute-start(f32[192,256]{1,0:T(8,128)S(1)} %fill.23.source), channel_id=1, source_target_pairs={{0,1},{1,2},{2,3},{4,5},{5,6},{6,7},{8,9},{9,10},{10,11},{12,13},{... | collective-permute-start | bytes 589832 | tf_op jit(solution)/shard_map/ppermute | solution.py:495
  40.7 11.8 %collective-permute-start.18 = (f32[192,256]{1,0:T(8,128)S(1)}, f32[192,256]{1,0:T(8,128)S(1)}, u32[]{:S(2)}, u32[]{:S(2)}) collective-permute-start(f32[192,256]{1,0:T(8,128)S(1)} %fill.21.refs_1_.source), channel_id=1, source_target_pairs={{0,1},{1,2},{2,3},{4,5},{5,6},{6,7},{8,9},{9,10},{10,11},{12,13},{... | collective-permute-start | bytes 589832 | tf_op jit(solution)/shard_map/ppermute | solution.py:495
  44.1 12.6 %collective-permute-start.14 = (f32[192,256]{1,0:T(8,128)S(1)}, f32[192,256]{1,0:T(8,128)S(1)}, u32[]{:S(2)}, u32[]{:S(2)}) collective-permute-start(f32[192,256]{1,0:T(8,128)S(1)} %fill.22.refs_1_.source), channel_id=1, source_target_pairs={{0,1},{1,2},{2,3},{4,5},{5,6},{6,7},{8,9},{9,10},{10,11},{12,13},{... | collective-permute-start | bytes 589832 | tf_op jit(solution)/shard_map/ppermute | solution.py:495
  48.3 12.6 %collective-permute-start.21 = (f32[192,256]{1,0:T(8,128)S(1)}, f32[192,256]{1,0:T(8,128)S(1)}, u32[]{:S(2)}, u32[]{:S(2)}) collective-permute-start(f32[192,256]{1,0:T(8,128)S(1)} %fill.24.refs_1_.source), channel_id=1, source_target_pairs={{0,1},{1,2},{2,3},{4,5},{5,6},{6,7},{8,9},{9,10},{10,11},{12,13},{... | collective-permute-start | bytes 589832 | tf_op jit(solution)/shard_map/ppermute | solution.py:495
  52.5 12.6 %collective-permute-start.20 = (f32[192,256]{1,0:T(8,128)S(1)}, f32[192,256]{1,0:T(8,128)S(1)}, u32[]{:S(2)}, u32[]{:S(2)}) collective-permute-start(f32[192,256]{1,0:T(8,128)S(1)} %fill.26.source), channel_id=1, source_target_pairs={{0,1},{1,2},{2,3},{4,5},{5,6},{6,7},{8,9},{9,10},{10,11},{12,13},{... | collective-permute-start | bytes 589832 | tf_op jit(solution)/shard_map/ppermute | solution.py:495
  56.7 12.6 %collective-permute-start.17 = (f32[192,256]{1,0:T(8,128)S(1)}, f32[192,256]{1,0:T(8,128)S(1)}, u32[]{:S(2)}, u32[]{:S(2)}) collective-permute-start(f32[192,256]{1,0:T(8,128)S(1)} %fill.25.refs_1_.source), channel_id=1, source_target_pairs={{0,1},{1,2},{2,3},{4,5},{5,6},{6,7},{8,9},{9,10},{10,11},{12,13},{... | collective-permute-start | bytes 589832 | tf_op jit(solution)/shard_map/ppermute | solution.py:495
  61.0 12.6 %collective-permute-start.25 = (f32[192,256]{1,0:T(8,128)S(1)}, f32[192,256]{1,0:T(8,128)S(1)}, u32[]{:S(2)}, u32[]{:S(2)}) collective-permute-start(f32[192,256]{1,0:T(8,128)S(1)} %fill.27.source.refs_4_), channel_id=1, source_target_pairs={{0,1},{1,2},{2,3},{4,5},{5,6},{6,7},{8,9},{9,10},{10,11},{12,13},{... | collective-permute-start | bytes 589832 | tf_op jit(solution)/shard_map/ppermute | solution.py:495
  65.2 12.6 %collective-permute-start.23 = (f32[192,256]{1,0:T(8,128)S(1)}, f32[192,256]{1,0:T(8,128)S(1)}, u32[]{:S(2)}, u32[]{:S(2)}) collective-permute-start(f32[192,256]{1,0:T(8,128)S(1)} %gate.27.source), channel_id=1, source_target_pairs={{1,2},{2,3},{5,6},{6,7},{9,10},{10,11},{13,14},{14,15},{17,18},{18... | collective-permute-start | bytes 589832 | tf_op jit(solution)/shard_map/ppermute | solution.py:495
  69.4 12.6 %collective-permute-start.19 = (f32[192,256]{1,0:T(8,128)S(1)}, f32[192,256]{1,0:T(8,128)S(1)}, u32[]{:S(2)}, u32[]{:S(2)}) collective-permute-start(f32[192,256]{1,0:T(8,128)S(1)} %gate.26.source), channel_id=1, source_target_pairs={{1,2},{2,3},{5,6},{6,7},{9,10},{10,11},{13,14},{14,15},{17,18},{18... | collective-permute-start | bytes 589832 | tf_op jit(solution)/shard_map/ppermute | solution.py:495
  73.6 13.0 %collective-permute-start.26 = (f32[192,256]{1,0:T(8,128)S(1)}, f32[192,256]{1,0:T(8,128)S(1)}, u32[]{:S(2)}, u32[]{:S(2)}) collective-permute-start(f32[192,256]{1,0:T(8,128)S(1)} %gate.30.source.refs_5_), channel_id=1, source_target_pairs={{1,2},{2,3},{5,6},{6,7},{9,10},{10,11},{13,14},{14,15},{17,18},{18... | collective-permute-start | bytes 589832 | tf_op jit(solution)/shard_map/ppermute | solution.py:495
  77.8 8.9 %collective-permute-start.24 = (f32[192,256]{1,0:T(8,128)S(1)}, f32[192,256]{1,0:T(8,128)S(1)}, u32[]{:S(2)}, u32[]{:S(2)}) collective-permute-start(f32[192,256]{1,0:T(8,128)S(1)} %gate.29.source), channel_id=1, source_target_pairs={{2,3},{6,7},{10,11},{14,15},{18,19},{22,23},{26,27},{30,31}} | collective-permute-start | bytes 589832 | tf_op jit(solution)/shard_map/ppermute | solution.py:495
  89.0 7.1 %collective-permute-start.27 = (f32[256,256]{1,0:T(8,128)S(1)}, f32[256,256]{1,0:T(8,128)S(1)}, u32[]{:S(2)}, u32[]{:S(2)}) collective-permute-start(f32[256,256]{1,0:T(8,128)S(1)} %get-tuple-element.104), channel_id=1, source_target_pairs={{0,4},{4,0},{8,12},{12,8},{16,20},{20,16},{24,28},{28,24},{1,5},{5... | collective-permute-start | bytes 786440 | tf_op jit(solution)/shard_map/ppermute | solution.py:454
  91.3 8.4 %collective-permute-start.31 = (f32[160,256]{1,0:T(8,128)S(1)}, f32[160,256]{1,0:T(8,128)S(1)}, u32[]{:S(2)}, u32[]{:S(2)}) collective-permute-start(f32[160,256]{1,0:T(8,128)S(1)} %cut.1), channel_id=1, source_target_pairs={{2,3},{6,7},{10,11},{14,15},{18,19},{22,23},{26,27},{30,31}} | collective-permute-start | bytes 491528 | tf_op jit(solution)/shard_map/ppermute | solution.py:495
  (13 other events, 47.3 us)
